TPU v7x, 32 devices: a whole 2x2x4 slice. The times are simulated.
32 devices in a mesh: groups: 2 (over y), replica: 4 (over x, core), tensor: 4 (over z).
Axes of the slice: x: 2, y: 2, z: 4, core: 2. Of those that a mesh axis runs over, the one named last changes fastest.
Arguments:
- layer_input: bfloat16 [6144, 8192], P(('groups', 'replica', 'tensor')), parts along dimension 0, may hold values from -6 to 6
- input_norm_weight: bfloat16 [8192], replicated, may hold values from 0.099609375 to 1.8984375
- query_base_matrix: bfloat16 [8192, 8192], P(None, 'tensor'), may hold values from -0.0625 to 0.0625
- adapter_down_weight: bfloat16 [4, 8192, 64], P('replica'), may hold values from -0.0625 to 0.0625
- adapter_up_weight: bfloat16 [4, 64, 8192], P('replica', None, 'tensor'), may hold values from -0.75 to 0.75
- token_adapter_index: int32 [6144], P(('groups', 'replica')), parts along dimension 0, may hold values from 0 to 3
Outputs:
- queries: bfloat16 [6144, 8192], P(('groups', 'replica'), 'tensor'), parts along dimension 0
There are 2 independent parts, one for each index of `groups`. A program takes and returns all parts, laid end to end along the dimension named above; an argument that names none is the same for every part. Nothing has to cross between parts.
All inputs are finite; a program needn't handle non-finite values.
Results may differ from a plain program's by a relative error of at most 0.0055.
Values may be sent and summed in bfloat16 or wider, within the bound.
No kernel may reach another device: no remote copies, remote signals or barrier semaphores. Data moves between devices by JAX's collectives and lax.ppermute only.
A program may use at most 128 MiB of HBM per device.

v0:
```python
import jax
import jax.numpy as jnp
from jax import lax
from jax.sharding import PartitionSpec as P

adapter_scale = 2.0


def selector(token_ids, adapter_count):
    return (token_ids[:, None] == jnp.arange(adapter_count, dtype=jnp.int32)[None, :]).astype(
        jnp.float32
    )


def body(
    layer_input,
    input_norm_weight,
    query_base_matrix,
    adapter_down_weight,
    adapter_up_weight,
    token_adapter_index,
):
    xf = layer_input.astype(jnp.float32)
    ms = jnp.mean(xf * xf, axis=-1, keepdims=True)
    normed = (xf * lax.rsqrt(ms + 1e-05) * input_norm_weight.astype(jnp.float32)).astype(
        jnp.bfloat16
    )
    rows = layer_input.shape[0]
    down_all, up_all = (
        lax.all_gather(adapter_down_weight, "replica", axis=0, tiled=True),
        lax.all_gather(adapter_up_weight, "replica", axis=0, tiled=True),
    )
    adapter_count = down_all.shape[0]
    rank = down_all.shape[2]
    flattened_down = jnp.transpose(down_all, (1, 0, 2)).reshape(
        down_all.shape[1], adapter_count * rank
    )
    up_flat = up_all.reshape(adapter_count * rank, up_all.shape[2])
    begin_own = lax.axis_index("tensor") * rows
    own_ids = lax.dynamic_slice_in_dim(token_adapter_index, begin_own, rows, 0)
    onehot = selector(own_ids, adapter_count)
    low_all = jnp.dot(normed, flattened_down, preferred_element_type=jnp.float32).reshape(
        -1, adapter_count, rank
    )
    low_own = jnp.sum(onehot[:, :, None] * low_all, axis=1).astype(jnp.bfloat16)
    low_every = lax.all_gather(low_own, "tensor", axis=0, tiled=True)
    onehot = selector(token_adapter_index, adapter_count)
    masked_update = (
        (onehot[:, :, None] * low_every[:, None, :].astype(jnp.float32))
        .reshape(-1, adapter_count * rank)
        .astype(jnp.bfloat16)
    )
    adapter_update = jnp.dot(masked_update, up_flat, preferred_element_type=jnp.float32)
    base_output = jnp.dot(
        lax.all_gather(normed, "tensor", axis=0, tiled=True),
        query_base_matrix,
        preferred_element_type=jnp.float32,
    )
    return (base_output + adapter_scale * adapter_update).astype(jnp.bfloat16)


def solution(mesh):
    placed = (
        P(("groups", "replica", "tensor"), None),
        P(),
        P(None, "tensor"),
        P("replica", None, None),
        P("replica", None, "tensor"),
        P(("groups", "replica")),
    )
    return jax.shard_map(
        body,
        mesh=mesh,
        in_specs=placed,
        out_specs=P(("groups", "replica"), "tensor"),
        check_vma=False,
    )
```

profile of v0, /device:TPU:0, one launch (start us, length us, event | category | flops | bytes accessed | tf_op | source)
XLA Modules:
  0.0 312.2 jit_solution(16625836939533837196)
XLA Ops:
  6.5 0.0 copy-start
  6.5 0.0 all-gather.7.cloned.1.call-start
  6.5 0.7 all-gather.7.cloned.1.call-update
  7.3 0.0 all-gather.5.cloned.1.call-start
  7.3 0.9 convert_element_type.38
  8.2 0.0 copy-start.1
  8.2 2.6 fusion
  10.8 0.0 copy-done
  10.8 2.5 fusion.2
  13.4 0.0 all-gather.5.cloned.1.call-update
  13.4 0.0 all-gather.9.cloned.1.call-start
  13.4 0.7 all-gather.9.cloned.1.call-update
  14.1 0.0 copy-done.1
  14.2 0.1 dynamic_slice.3
  14.2 31.9 %all-gather.7.cloned.1.call-done = bf16[4,8192,64]{1,2,0:T(8,128)(2,1)} async-done(((bf16[1,8192,64]{1,2,0:T(8,128)(2,1)}), bf16[4,8192,64]{1,2,0:T(8,128)(2,1)}) %all-gather.7.cloned.1.call-update) | async-done | bytes 4194320 | tf_op jit(solution)/shard_map/all_gather | solution.py:30
  46.1 4.4 %fusion.13 = bf16[192,64]{0,1:T(8,128)(2,1)S(1)} fusion(bf16[4,8192,64]{1,2,0:T(8,128)(2,1)} %all-gather.7.cloned.1.call-done, bf16[192,8192]{1,0:T(8,128)(2,1)} %fusion.2, f32[192,4]{0,1:T(4,128)S(1)} %fusion.21), kind=kOutput, calls=%fused_computation.12 | convolution fusion | flops 805392384 | bytes 7367680 | tf_op jit(solution)/shard_map/dot_general | solution.py:42
  50.5 13.7 %all-gather = bf16[4,192,64]{1,2,0:T(8,128)(2,1)S(1)} all-gather(bf16[1,192,64]{1,2,0:T(8,128)(2,1)S(1)} %bitcast.34), channel_id=1, replica_groups=mesh['groups'=2,'replica'=4,'tensor'=4] {'tensor'}, dimensions={0}, use_global_device_ids=true | all-gather | bytes 122880 | tf_op jit(solution)/shard_map/all_gather | solution.py:46
  64.2 0.1 copy.8
  64.3 0.2 reshape.68
  64.5 201.8 %all-gather.5.cloned.1.call-done = bf16[768,8192]{1,0:T(8,128)(2,1)} async-done(((bf16[192,8192]{1,0:T(8,128)(2,1)}), bf16[768,8192]{1,0:T(8,128)(2,1)}) %all-gather.5.cloned.1.call-update) | async-done | bytes 12582928 | tf_op jit(solution)/shard_map/all_gather | solution.py:55
  266.3 33.6 %fusion.22 = f32[768,2048]{1,0:T(8,128)} fusion(bf16[768,8192]{1,0:T(8,128)(2,1)} %all-gather.5.cloned.1.call-done, bf16[8192,2048]{1,0:T(8,128)(2,1)} %param.8), kind=kOutput, calls=%fused_computation.22 | convolution fusion | flops 25769803776 | bytes 52428800 | tf_op jit(solution)/shard_map/dot_general | solution.py:54
  299.9 0.0 all-gather.9.cloned.1.call-done
  299.9 5.8 %fusion.4 = bf16[768,2048]{1,0:T(8,128)(2,1)} fusion(f32[768,2048]{1,0:T(8,128)} %fusion.22, bf16[4,64,2048]{2,1,0:T(8,128)(2,1)} %all-gather.9.cloned.1.call-done, f32[768,64]{0,1:T(8,128)S(1)} %reshape.68, f32[768,4]{0,1:T(4,128)S(1)} %fusion.20), kind=kOutput, calls=%fused_computation.7 | convolution fusion | flops 810418176 | bytes 10694656 | tf_op jit(solution)/shard_map/dot_general | solution.py:53
  (3 shorter events, 0.0 us)
Async XLA Ops:
  6.5 4.3 %copy-start = (bf16[192,8192]{1,0:T(8,128)(2,1)S(1)}, bf16[192,8192]{1,0:T(8,128)(2,1)}, u32[]{:S(2)}) copy-start(bf16[192,8192]{1,0:T(8,128)(2,1)} %param.6) | copy-start | bytes 9437188
  6.5 39.6 %all-gather.7.cloned.1.call-start = ((), (), s32[]{:S(2)}) async-start(), calls=%async_computation.1 | async-start | bytes 5242880 | tf_op jit(solution)/shard_map/all_gather | solution.py:30
  7.3 259.0 %all-gather.5.cloned.1.call-start = ((), (), s32[]{:S(2)}) async-start(), calls=%async_computation | async-start | bytes 15728640 | tf_op jit(solution)/shard_map/all_gather | solution.py:55
  8.2 5.9 %copy-start.1 = (s32[768]{0:T(1024)S(1)}, s32[768]{0:T(1024)}, u32[]{:S(2)}) copy-start(s32[768]{0:T(1024)} %param.11) | copy-start | bytes 9220
  13.4 286.5 %all-gather.9.cloned.1.call-start = ((), (), s32[]{:S(2)}) async-start(), calls=%async_computation.2 | async-start | bytes 1310720 | tf_op jit(solution)/shard_map/all_gather | solution.py:31
Sparse Core Ops, SparseCore 0:
  8.9 37.1 all-gather.6
  47.7 218.5 all-gather.4
  267.9 14.9 all-gather.8
where the time goes:
time: 312 us
  waiting for transfers between devices  235 us (75%)
  matrix products  43.8 us (14%)
  blocking collectives  13.7 us (4%)
  between operations  13.2 us (4%)
  other arithmetic  6.06 us (2%)
    all_gather x1, waiting for transfers between devices, body(): lax.all_gather(normed, 'tensor', axis=0, tiled=True)  202 us
    dot_general x1, matrix products, body(): jnp.dot(lax.all_gather(normed, 'tensor', axis=0, tiled=True), query_base_...  33.6 us
    all_gather x1, waiting for transfers between devices, body(): lax.all_gather(adapter_down_weight, 'replica', axis=0, tiled=True)  31.9 us
    all_gather x1, blocking collectives, body(): low_every = lax.all_gather(low_own, 'tensor', axis=0, tiled=True)  13.7 us
  transfers between devices with their start and end apart: 3, of which 2 were waited for; matrix products, arithmetic and copies ran while one was open for 14% of the time, Pallas kernels for 0%

commit v1 on v0

v1 whole, which is shorter than its diff:
```python
import jax
import jax.numpy as jnp
from jax import lax
from jax.sharding import PartitionSpec as P

adapter_scale = 2.0


def body(
    layer_input,
    input_norm_weight,
    query_base_matrix,
    adapter_down_weight,
    adapter_up_weight,
    token_adapter_index,
):
    xf = layer_input.astype(jnp.float32)
    ms = jnp.mean(xf * xf, axis=-1, keepdims=True)
    normed = (xf * lax.rsqrt(ms + 1e-05) * input_norm_weight.astype(jnp.float32)).astype(
        jnp.bfloat16
    )
    width = layer_input.shape[1]
    parts = 4
    step = width // parts
    gathered = [
        lax.all_gather(normed[:, i * step : (i + 1) * step], "tensor", axis=0, tiled=True)
        for i in range(parts)
    ]
    count = lax.axis_size("replica")
    me = lax.axis_index("replica")
    down, up = [adapter_down_weight[0]], [adapter_up_weight[0]]
    for hop in range(1, count):
        pairs = [(i, i ^ hop if count == 4 else (i + hop) % count) for i in range(count)]
        down.append(lax.ppermute(adapter_down_weight[0], "replica", pairs))
        up.append(lax.ppermute(adapter_up_weight[0], "replica", pairs))
    if count == 4:
        owners = [me ^ hop for hop in range(count)]
    else:
        owners = [(me - hop) % count for hop in range(count)]
    down_cat = jnp.concatenate(down, axis=1)
    up_cat = jnp.concatenate(up, axis=0)
    rank = adapter_down_weight.shape[2]
    total = low_all = None
    for i in range(parts):
        rows = slice(i * step, (i + 1) * step)
        p = jnp.dot(gathered[i], query_base_matrix[rows], preferred_element_type=jnp.float32)
        q = jnp.dot(gathered[i], down_cat[rows], preferred_element_type=jnp.float32)
        total = p if total is None else total + p
        low_all = q if low_all is None else low_all + q
    column_owner = jnp.repeat(jnp.stack(owners), rank).astype(jnp.int32)
    chosen = token_adapter_index[:, None] == column_owner[None, :]
    masked = jnp.where(chosen, low_all, 0.0).astype(jnp.bfloat16)
    update = jnp.dot(masked, up_cat, preferred_element_type=jnp.float32)
    return (total + adapter_scale * update).astype(jnp.bfloat16)


def solution(mesh):
    placed = (
        P(("groups", "replica", "tensor"), None),
        P(),
        P(None, "tensor"),
        P("replica", None, None),
        P("replica", None, "tensor"),
        P(("groups", "replica")),
    )
    return jax.shard_map(
        body,
        mesh=mesh,
        in_specs=placed,
        out_specs=P(("groups", "replica"), "tensor"),
        check_vma=False,
    )
```

time: 312 us -> 307 us (0.984)
  waiting for transfers between devices: 235 us -> 205 us
  matrix products: 43.8 us -> 72.6 us
  blocking collectives: 13.7 us -> 0 us
  starting transfers between devices: 0.08 us -> 6.56 us
    all_gather x3 -> x4, waiting for transfers between devices: 234 us -> 161 us  [body(): lax.all_gather(normed[:, i * step:(i + 1) * step], 'tensor', axis=0, tile...]
    ppermute x0 -> x6, waiting for transfers between devices: none -> 42.8 us  [the longest x3 42.8 us: body(): down.append(lax.ppermute(adapter_down_weight[0], 'replica', pairs))]
    dot_general x3 -> x8, matrix products: 43.8 us -> 72.6 us  [the longest x4 47.1 us: body(): jnp.dot(gathered[i], query_base_matrix[rows], preferred_element_type=jnp....]
    all_gather x1 -> x0, blocking collectives: 13.7 us -> none  [body(): low_every = lax.all_gather(low_own, 'tensor', axis=0, tiled=True)]
    ppermute x0 -> x6, starting transfers between devices: none -> 6.44 us  [the longest x3 3.32 us: body(): up.append(lax.ppermute(adapter_up_weight[0], 'replica', pairs))]
    concatenate x0 -> x1, other arithmetic: none -> 3.21 us  [body(): down_cat = jnp.concatenate(down, axis=1)]
  transfers between devices with their start and end apart: 3 -> 10, of which waited for: 2 -> 6; matrix products, arithmetic and copies ran while one was open for 14% -> 20% of each run, Pallas kernels for 0% -> 0%
where the time goes in v1:
time: 307 us
  waiting for transfers between devices  205 us (67%)
  matrix products  72.6 us (24%)
  between operations  13.2 us (4%)
  other arithmetic  7.63 us (2%)
  starting transfers between devices  6.56 us (2%)
    all_gather x4, waiting for transfers between devices, body(): lax.all_gather(normed[:, i * step:(i + 1) * step], 'tensor', axis=0, tile...  161 us
    dot_general x4, matrix products, body(): jnp.dot(gathered[i], query_base_matrix[rows], preferred_element_type=jnp....  47.1 us
    ppermute x3, waiting for transfers between devices, body(): down.append(lax.ppermute(adapter_down_weight[0], 'replica', pairs))  42.8 us
    dot_general x1, matrix products, body(): update = jnp.dot(masked, up_cat, preferred_element_type=jnp.float32)  14.7 us
    dot_general x3, matrix products, body(): q = jnp.dot(gathered[i], down_cat[rows], preferred_element_type=jnp.float32)  10.7 us
  transfers between devices with their start and end apart: 10, of which 6 were waited for; matrix products, arithmetic and copies ran while one was open for 20% of the time, Pallas kernels for 0%

profile of v1, /device:TPU:0, one launch (start us, length us, event | category | flops | bytes accessed | tf_op | source)
XLA Modules:
  0.0 306.7 jit_solution(10531121617245242687)
XLA Ops:
  6.5 2.8 fusion.8
  9.3 0.7 convert_element_type.16
  10.0 0.9 fusion.10
  10.9 1.7 fusion.36
  12.7 0.0 all-gather.9.cloned.1.call-start
  12.7 0.7 all-gather.9.cloned.1.call-update
  13.5 0.7 all-gather.7.cloned.1.call-update
  14.1 0.0 all-gather.5.cloned.1.call-start
  14.2 2.4 collective-permute-start.2
  16.6 0.6 collective-permute-start.1
  17.3 0.0 collective-permute-start
  17.3 1.5 collective-permute-start.5
  18.8 0.6 collective-permute-start.4
  19.5 0.1 pad_add_fusion
  19.5 0.1 broadcast_in_dim.10
  19.6 0.1 eq.16
  19.7 20.5 %collective-permute-done.2 = bf16[8192,64]{0,1:T(8,128)(2,1)S(1)} collective-permute-done((bf16[8192,64]{0,1:T(8,128)(2,1)S(1)}, bf16[8192,64]{0,1:T(8,128)(2,1)S(1)}, u32[]{:S(2)}, u32[]{:S(2)}) %collective-permute-start.2) | collective-permute-done | bytes 1048608 | tf_op jit(solution)/shard_map/ppermute | solution.py:34
  40.2 1.2 collective-permute-start.3
  41.4 22.2 %collective-permute-done.1 = bf16[8192,64]{0,1:T(8,128)(2,1)S(1)} collective-permute-done((bf16[8192,64]{0,1:T(8,128)(2,1)S(1)}, bf16[8192,64]{0,1:T(8,128)(2,1)S(1)}, u32[]{:S(2)}, u32[]{:S(2)}) %collective-permute-start.1) | collective-permute-done | bytes 1048608 | tf_op jit(solution)/shard_map/ppermute | solution.py:34
  63.7 3.2 %pad_maximum_fusion = bf16[8192,256]{0,1:T(8,128)(2,1)} fusion(bf16[8192,64]{0,1:T(8,128)(2,1)S(1)} %collective-permute-done.2, bf16[8192,64]{0,1:T(8,128)(2,1)S(1)} %collective-permute-done.1, bf16[8192,64]{0,1:T(8,128)(2,1)} %collective-permute-done, bf16[8192,64]{0,1:T(8,128)(2,1)S(1)} %bitcast.17), kind=kLoop, calls=%fused_computation.14 | loop fusion | flops 16777216 | bytes 8388608 | tf_op jit(solution)/shard_map/concatenate | solution.py:40
  66.9 12.1 %all-gather.11.cloned.1.call-done = bf16[768,2048]{1,0:T(8,128)(2,1)} async-done(((bf16[192,2048]{1,0:T(8,128)(2,1)}), bf16[768,2048]{1,0:T(8,128)(2,1)}) %all-gather.11.cloned.1.call-update) | async-done | bytes 3145744 | tf_op jit(solution)/shard_map/all_gather | solution.py:26
  79.0 12.7 %fusion = f32[768,2048]{1,0:T(8,128)} fusion(bf16[768,2048]{1,0:T(8,128)(2,1)} %all-gather.11.cloned.1.call-done, bf16[8192,2048]{1,0:T(8,128)(2,1)} %param.8), kind=kOutput, calls=%fused_computation | convolution fusion | flops 6442450944 | bytes 17825792 | tf_op jit(solution)/shard_map/dot_general | solution.py:46
  91.7 3.1 %fusion.15 = f32[768,256]{1,0:T(8,128)} fusion(bf16[768,2048]{1,0:T(8,128)(2,1)S(1)} %copy-done.5, bf16[8192,256]{0,1:T(8,128)(2,1)} %pad_maximum_fusion), kind=kOutput, calls=%fused_computation.20 | convolution fusion | flops 805306368 | bytes 4980736 | tf_op jit(solution)/shard_map/dot_general | solution.py:47
  94.8 47.9 %all-gather.9.cloned.1.call-done = bf16[768,2048]{1,0:T(8,128)(2,1)} async-done(((bf16[192,2048]{1,0:T(8,128)(2,1)}), bf16[768,2048]{1,0:T(8,128)(2,1)}) %all-gather.9.cloned.1.call-update) | async-done | bytes 3145744 | tf_op jit(solution)/shard_map/all_gather | solution.py:26
  142.8 4.3 %fusion.17 = f32[768,256]{1,0:T(8,128)} fusion(bf16[768,2048]{1,0:T(8,128)(2,1)} %all-gather.9.cloned.1.call-done, bf16[8192,256]{0,1:T(8,128)(2,1)} %pad_maximum_fusion), kind=kOutput, calls=%fused_computation.22 | convolution fusion | flops 805306368 | bytes 4980736 | tf_op jit(solution)/shard_map/dot_general | solution.py:47
  147.0 10.8 %fusion.2 = f32[768,2048]{1,0:T(8,128)} fusion(bf16[768,2048]{1,0:T(8,128)(2,1)S(1)} %copy-done.7, bf16[8192,2048]{1,0:T(8,128)(2,1)} %param.8), kind=kOutput, calls=%fused_computation.2 | convolution fusion | flops 6442450944 | bytes 17825792 | tf_op jit(solution)/shard_map/dot_general | solution.py:46
  157.9 48.7 %all-gather.7.cloned.1.call-done = bf16[768,2048]{1,0:T(8,128)(2,1)} async-done(((bf16[192,2048]{1,0:T(8,128)(2,1)}), bf16[768,2048]{1,0:T(8,128)(2,1)}) %all-gather.7.cloned.1.call-update) | async-done | bytes 3145744 | tf_op jit(solution)/shard_map/all_gather | solution.py:26
  206.5 11.7 %fusion.4 = f32[768,2048]{1,0:T(8,128)} fusion(bf16[768,2048]{1,0:T(8,128)(2,1)} %all-gather.7.cloned.1.call-done, bf16[8192,2048]{1,0:T(8,128)(2,1)} %param.8), kind=kOutput, calls=%fused_computation.4 | convolution fusion | flops 6442450944 | bytes 17825792 | tf_op jit(solution)/shard_map/dot_general | solution.py:46
  218.2 51.9 %all-gather.5.cloned.1.call-done = bf16[768,2048]{1,0:T(8,128)(2,1)} async-done(((bf16[192,2048]{1,0:T(8,128)(2,1)}), bf16[768,2048]{1,0:T(8,128)(2,1)}) %all-gather.5.cloned.1.call-update) | async-done | bytes 3145744 | tf_op jit(solution)/shard_map/all_gather | solution.py:26
  270.1 11.9 %fusion.6 = f32[768,2048]{1,0:T(8,128)} fusion(bf16[768,2048]{1,0:T(8,128)(2,1)} %all-gather.5.cloned.1.call-done, bf16[8192,2048]{1,0:T(8,128)(2,1)} %param.8), kind=kOutput, calls=%fused_computation.6 | convolution fusion | flops 6442450944 | bytes 17825792 | tf_op jit(solution)/shard_map/dot_general | solution.py:46
  282.1 3.3 %fusion.19 = f32[768,256]{1,0:T(8,128)} fusion(bf16[768,2048]{1,0:T(8,128)(2,1)S(1)} %copy-done.6, bf16[8192,256]{0,1:T(8,128)(2,1)} %pad_maximum_fusion), kind=kOutput, calls=%fused_computation.24 | convolution fusion | flops 805306368 | bytes 4980736 | tf_op jit(solution)/shard_map/dot_general | solution.py:47
  285.4 14.7 %add_convert_fusion = bf16[768,2048]{1,0:T(8,128)(2,1)} fusion(f32[768,2048]{1,0:T(8,128)} %fusion, f32[768,2048]{1,0:T(8,128)} %fusion.2, f32[768,2048]{1,0:T(8,128)} %fusion.6, f32[768,2048]{1,0:T(8,128)} %fusion.4, bf16[64,2048]{1,0:T(8,128)(2,1)} %collective-permute-done.5, bf16[64,2048]{1,0:T(8,128)(2,1)} %collective-permute-done.4, ...), kind=kOutput, calls=%fused_computation.13 | convolution fusion | flops 1625423872 | bytes 35917824 | tf_op jit(solution)/shard_map/dot_general | solution.py:53
  (25 shorter events, 0.1 us)
Async XLA Ops:
  6.5 3.5 %copy-start = (bf16[192,8192]{1,0:T(8,128)(2,1)S(1)}, bf16[192,8192]{1,0:T(8,128)(2,1)}, u32[]{:S(2)}) copy-start(bf16[192,8192]{1,0:T(8,128)(2,1)} %param.6) | copy-start | bytes 9437188
  6.5 72.5 %all-gather.11.cloned.1.call-start = ((), (), s32[]{:S(2)}) async-start(), calls=%async_computation.3 | async-start | bytes 3932160 | tf_op jit(solution)/shard_map/all_gather | solution.py:26
  10.9 3.3 %copy-start.2 = (bf16[1,8192,64]{1,2,0:T(8,128)(2,1)S(1)}, bf16[1,8192,64]{1,2,0:T(8,128)(2,1)}, u32[]{:S(2)}) copy-start(bf16[1,8192,64]{1,2,0:T(8,128)(2,1)} %param.9) | copy-start | bytes 3145732
  10.9 6.4 %copy-start.3 = (bf16[1,64,2048]{2,1,0:T(8,128)(2,1)S(1)}, bf16[1,64,2048]{2,1,0:T(8,128)(2,1)}, u32[]{:S(2)}) copy-start(bf16[1,64,2048]{2,1,0:T(8,128)(2,1)} %param.10) | copy-start | bytes 786436
  12.7 130.1 %all-gather.9.cloned.1.call-start = ((), (), s32[]{:S(2)}) async-start(), calls=%async_computation.2 | async-start | bytes 3932160 | tf_op jit(solution)/shard_map/all_gather | solution.py:26
  13.4 193.1 %all-gather.7.cloned.1.call-start = ((), (), s32[]{:S(2)}) async-start(), calls=%async_computation.1 | async-start | bytes 3932160 | tf_op jit(solution)/shard_map/all_gather | solution.py:26
  14.1 256.0 %all-gather.5.cloned.1.call-start = ((), (), s32[]{:S(2)}) async-start(), calls=%async_computation | async-start | bytes 3932160 | tf_op jit(solution)/shard_map/all_gather | solution.py:26
  14.2 26.0 %collective-permute-start.2 = (bf16[8192,64]{0,1:T(8,128)(2,1)S(1)}, bf16[8192,64]{0,1:T(8,128)(2,1)S(1)}, u32[]{:S(2)}, u32[]{:S(2)}) collective-permute-start(bf16[8192,64]{0,1:T(8,128)(2,1)S(1)} %bitcast.14), channel_id=1, source_target_pairs={{0,12},{4,8},{8,4},{12,0},{1,13},{5,9},{9,5},{13,1},{2,14},{6,10},... | collective-permute-start | bytes 3145736 | tf_op jit(solution)/shard_map/ppermute | solution.py:34
  16.6 47.0 %collective-permute-start.1 = (bf16[8192,64]{0,1:T(8,128)(2,1)S(1)}, bf16[8192,64]{0,1:T(8,128)(2,1)S(1)}, u32[]{:S(2)}, u32[]{:S(2)}) collective-permute-start(bf16[8192,64]{0,1:T(8,128)(2,1)S(1)} %bitcast.15), channel_id=1, source_target_pairs={{0,8},{4,12},{8,0},{12,4},{1,9},{5,13},{9,1},{13,5},{2,10},{6,14},... | collective-permute-start | bytes 3145736 | tf_op jit(solution)/shard_map/ppermute | solution.py:34
  17.3 46.4 %collective-permute-start = (bf16[8192,64]{0,1:T(8,128)(2,1)S(1)}, bf16[8192,64]{0,1:T(8,128)(2,1)}, u32[]{:S(2)}, u32[]{:S(2)}) collective-permute-start(bf16[8192,64]{0,1:T(8,128)(2,1)S(1)} %bitcast.16), channel_id=1, source_target_pairs={{0,4},{4,0},{8,12},{12,8},{1,5},{5,1},{9,13},{13,9},{2,6},{6,2},{1... | collective-permute-start | bytes 3145736 | tf_op jit(solution)/shard_map/ppermute | solution.py:34
  17.3 268.1 %collective-permute-start.5 = (bf16[64,2048]{1,0:T(8,128)(2,1)S(1)}, bf16[64,2048]{1,0:T(8,128)(2,1)}, u32[]{:S(2)}, u32[]{:S(2)}) collective-permute-start(bf16[64,2048]{1,0:T(8,128)(2,1)S(1)} %bitcast.18), channel_id=1, source_target_pairs={{0,12},{4,8},{8,4},{12,0},{1,13},{5,9},{9,5},{13,1},{2,14},{6,10},... | collective-permute-start | bytes 786440 | tf_op jit(solution)/shard_map/ppermute | solution.py:35
  18.8 266.6 %collective-permute-start.4 = (bf16[64,2048]{1,0:T(8,128)(2,1)S(1)}, bf16[64,2048]{1,0:T(8,128)(2,1)}, u32[]{:S(2)}, u32[]{:S(2)}) collective-permute-start(bf16[64,2048]{1,0:T(8,128)(2,1)S(1)} %bitcast.19), channel_id=1, source_target_pairs={{0,8},{4,12},{8,0},{12,4},{1,9},{5,13},{9,1},{13,5},{2,10},{6,14},... | collective-permute-start | bytes 786440 | tf_op jit(solution)/shard_map/ppermute | solution.py:35
  40.2 245.2 %collective-permute-start.3 = (bf16[64,2048]{1,0:T(8,128)(2,1)S(1)}, bf16[64,2048]{1,0:T(8,128)(2,1)}, u32[]{:S(2)}, u32[]{:S(2)}) collective-permute-start(bf16[64,2048]{1,0:T(8,128)(2,1)S(1)} %bitcast.20), channel_id=1, source_target_pairs={{0,4},{4,0},{8,12},{12,8},{1,5},{5,1},{9,13},{13,9},{2,6},{6,2},{1... | collective-permute-start | bytes 786440 | tf_op jit(solution)/shard_map/ppermute | solution.py:35
  79.0 12.7 %copy-start.5 = (bf16[768,2048]{1,0:T(8,128)(2,1)S(1)}, bf16[768,2048]{1,0:T(8,128)(2,1)}, u32[]{:S(2)}) copy-start(bf16[768,2048]{1,0:T(8,128)(2,1)} %all-gather.11.cloned.1.call-done) | copy-start | bytes 9437188
  142.8 4.3 %copy-start.7 = (bf16[768,2048]{1,0:T(8,128)(2,1)S(1)}, bf16[768,2048]{1,0:T(8,128)(2,1)}, u32[]{:S(2)}) copy-start(bf16[768,2048]{1,0:T(8,128)(2,1)} %all-gather.9.cloned.1.call-done) | copy-start | bytes 9437188
  270.1 11.9 %copy-start.6 = (bf16[768,2048]{1,0:T(8,128)(2,1)S(1)}, bf16[768,2048]{1,0:T(8,128)(2,1)}, u32[]{:S(2)}) copy-start(bf16[768,2048]{1,0:T(8,128)(2,1)} %all-gather.7.cloned.1.call-done) | copy-start | bytes 9437188
  282.0 3.4 %copy-start.1 = (bf16[768,2048]{1,0:T(8,128)(2,1)S(1)}, bf16[768,2048]{1,0:T(8,128)(2,1)}, u32[]{:S(2)}) copy-start(bf16[768,2048]{1,0:T(8,128)(2,1)} %all-gather.5.cloned.1.call-done) | copy-start | bytes 9437188
  282.0 3.4 %copy-start.4 = (s32[768]{0:T(1024)S(1)}, s32[768]{0:T(1024)}, u32[]{:S(2)}) copy-start(s32[768]{0:T(1024)} %param.11) | copy-start | bytes 9220
Sparse Core Ops, SparseCore 0:
  12.8 66.1 all-gather.10
  80.6 62.1 all-gather.8
  144.3 62.1 all-gather.6
  207.9 62.1 all-gather.4

commit v2 on v1

v2 whole, which is shorter than its diff:
```python
import jax
import jax.numpy as jnp
from jax import lax
from jax.experimental import pallas as pl
from jax.experimental.pallas import tpu as pltpu
from jax.sharding import PartitionSpec as P

adapter_scale = 2.0
lanes = 128
vmem = 56 * 1024 * 1024
f32 = jnp.float32
bf16 = jnp.bfloat16


def plain(
    layer_input,
    input_norm_weight,
    query_base_matrix,
    adapter_down_weight,
    adapter_up_weight,
    token_adapter_index,
):
    xf = layer_input.astype(f32)
    ms = jnp.mean(xf * xf, axis=-1, keepdims=True)
    normed = (xf * lax.rsqrt(ms + 1e-05) * input_norm_weight.astype(f32)).astype(bf16)
    gathered = lax.all_gather(normed, "tensor", axis=0, tiled=True)
    down_all = lax.all_gather(adapter_down_weight, "replica", axis=0, tiled=True)
    up_all = lax.all_gather(adapter_up_weight, "replica", axis=0, tiled=True)
    count, width, rank = down_all.shape
    down_cat = jnp.transpose(down_all, (1, 0, 2)).reshape(width, count * rank)
    low_all = jnp.dot(gathered, down_cat, preferred_element_type=f32)
    owner = jnp.repeat(jnp.arange(count, dtype=jnp.int32), rank)
    chosen = token_adapter_index[:, None] == owner[None, :]
    masked = jnp.where(chosen, low_all, 0.0).astype(bf16)
    update = jnp.dot(
        masked, up_all.reshape(count * rank, up_all.shape[2]), preferred_element_type=f32
    )
    base = jnp.dot(gathered, query_base_matrix, preferred_element_type=f32)
    return (base + adapter_scale * update).astype(bf16)


def norm_chunks(x, gain, parts):
    rows, width = x.shape
    step = width // parts
    block = 48

    def kernel(x_ref, g_ref, *out_refs):
        xf = x_ref[...].astype(f32)
        ms = jnp.mean(xf * xf, axis=-1, keepdims=True)
        y = (xf * lax.rsqrt(ms + 1e-05) * g_ref[...].astype(f32)).astype(bf16)
        for i, out_ref in enumerate(out_refs):
            out_ref[...] = y[:, i * step : (i + 1) * step]

    return pl.pallas_call(
        kernel,
        grid=(rows // block,),
        in_specs=[
            pl.BlockSpec((block, width), lambda i: (i, 0)),
            pl.BlockSpec((1, width), lambda i: (0, 0)),
        ],
        out_specs=[pl.BlockSpec((block, step), lambda i: (i, 0))] * parts,
        out_shape=[jax.ShapeDtypeStruct((rows, step), bf16)] * parts,
        compiler_params=pltpu.CompilerParams(vmem_limit_bytes=vmem),
        cost_estimate=pl.CostEstimate(
            flops=5 * rows * width, bytes_accessed=4 * rows * width, transcendentals=rows
        ),
        name="norm_chunks",
    )(x, gain)


def dot_t(a, b):
    return lax.dot_general(a, b, (((1,), (1,)), ((), ())), preferred_element_type=f32)


def product(first, xs, weight, pool, carry=None, finish=None):
    rows, step = xs[0][0].shape
    width, features = weight.shape
    pool_rows = pool.shape[0]
    tile = 512
    tiles = features // tile
    steps = len(xs)
    flat = [a for t in xs for a in t]
    has_partial = finish is not None and finish["partial"] is not None
    has_prev = finish is not None and finish["prev"] is not None

    def kernel(row_ref, *refs):
        refs = list(refs)
        x_refs = [refs.pop(0) for _ in flat]
        w_ref, down_ref = refs.pop(0), refs.pop(0)
        acc_in = low_in = None
        if carry is not None:
            acc_in, low_in = refs.pop(0), refs.pop(0)
        if finish is not None:
            up_ref, owner_ref, ids_ref = refs.pop(0), refs.pop(0), refs.pop(0)
            part_ref = refs.pop(0) if has_partial else None
            if has_prev:
                refs.pop(0)
            out_ref, acc, low, mask = refs
        else:
            acc, low = refs
        n, k = pl.program_id(0), pl.program_id(1)
        at = 0
        for i, t in enumerate(xs):
            mine = x_refs[at : at + len(t)]
            at += len(t)

            @pl.when(k == i)
            def _():
                x = mine[0][...]
                for other in mine[1:]:
                    x = x + other[...]
                p = jnp.dot(x, w_ref[...], preferred_element_type=f32)
                if i == 0 and carry is not None:
                    p = p + acc_in[...]
                acc[...] = p if i == 0 else acc[...] + p

                @pl.when(n == 0)
                def _():
                    q = dot_t(x, down_ref[...])
                    if i == 0 and carry is not None:
                        q = q + low_in[...]
                    low[...] = q if i == 0 else low[...] + q

        if finish is not None:

            @pl.when(jnp.logical_and(n == 0, k == steps - 1))
            def _():
                total = low[...]
                if has_partial:
                    sent = part_ref[:, features : features + lanes].astype(f32)
                    total = total + jnp.concatenate([sent] * (pool_rows // lanes), axis=1)
                chosen = ids_ref[...] == owner_ref[...]
                mask[...] = jnp.where(chosen, total, 0.0).astype(bf16)

            @pl.when(k == steps - 1)
            def _():
                y = adapter_scale * jnp.dot(mask[...], up_ref[...], preferred_element_type=f32)
                y = y + acc[...]
                if has_partial:
                    y = y + part_ref[:, pl.ds(pl.multiple_of(n * tile, tile), tile)].astype(f32)
                out_ref[...] = y.astype(bf16)

    whole = lambda shape: pl.BlockSpec(shape, lambda n, k, row: (0, 0))
    in_specs = [whole((rows, step)) for _ in flat]
    operands = list(flat)
    in_specs += [
        pl.BlockSpec((step, tile), lambda n, k, row: (first + k, n)),
        pl.BlockSpec(
            (pool_rows, step),
            lambda n, k, row: (0, jnp.where(n == 0, first + k, first + steps - 1)),
        ),
    ]
    operands += [weight, pool]
    if carry is not None:
        in_specs += [
            pl.BlockSpec((rows, tile), lambda n, k, row: (0, n)),
            whole((rows, pool_rows)),
        ]
        operands += list(carry)
    aliases = {}
    if finish is None:
        row = jnp.zeros((1,), jnp.int32)
        out_shape = [
            jax.ShapeDtypeStruct((rows, features), f32),
            jax.ShapeDtypeStruct((rows, pool_rows), f32),
        ]
        out_specs = [
            pl.BlockSpec((rows, tile), lambda n, k, row: (0, n)),
            whole((rows, pool_rows)),
        ]
        scratch = []
    else:
        row = finish["row"].reshape(1)
        in_specs += [
            pl.BlockSpec((pool_rows, tile), lambda n, k, row: (0, width // tile + n)),
            whole((1, pool_rows)),
            pl.BlockSpec((rows, 1), lambda n, k, row: (row[0], 0)),
        ]
        operands += [pool, finish["owner"], finish["ids"]]
        if has_partial:
            in_specs.append(whole((rows, features + lanes)))
            operands.append(finish["partial"])
        if has_prev:
            in_specs.append(pl.BlockSpec(memory_space=pl.ANY))
            operands.append(finish["prev"])
            aliases = {len(operands): 0}
        out_shape = jax.ShapeDtypeStruct((finish["ids"].shape[0], features), bf16)
        out_specs = pl.BlockSpec((rows, tile), lambda n, k, row: (row[0], n))
        scratch = [
            pltpu.VMEM((rows, tile), f32),
            pltpu.VMEM((rows, pool_rows), f32),
            pltpu.VMEM((rows, pool_rows), bf16),
        ]
    flops = 2 * rows * steps * step * (features + pool_rows)
    return pl.pallas_call(
        kernel,
        grid_spec=pltpu.PrefetchScalarGridSpec(
            num_scalar_prefetch=1,
            grid=(tiles, steps),
            in_specs=in_specs,
            out_specs=out_specs,
            scratch_shapes=scratch,
        ),
        out_shape=out_shape,
        input_output_aliases=aliases,
        compiler_params=pltpu.CompilerParams(vmem_limit_bytes=vmem),
        cost_estimate=pl.CostEstimate(
            flops=flops, bytes_accessed=2 * steps * step * features, transcendentals=0
        ),
        name="product",
    )(row, *operands)


def partial_product(chunks, slabs, places, row, ids, owner, pool):
    rows, step = chunks[0].shape
    features = slabs[0][0].shape[1]
    pool_rows = pool.shape[0]
    tile = 512
    tiles = features // tile
    count = len(chunks)
    flat = [a for s in slabs for a in s]
    per = len(slabs[0])
    span = slabs[0][0].shape[0]

    def kernel(row_ref, place_ref, *refs):
        x_refs = refs[:count]
        w_refs = refs[count : count + len(flat)]
        down_ref, owner_ref, ids_ref, out_ref, moved = refs[count + len(flat) :]
        n = pl.program_id(0)

        @pl.when(n == 0)
        def _():
            low = None
            for s in range(count):
                for j in range(step // lanes):
                    off = pl.multiple_of(place_ref[j] * lanes, lanes)
                    moved[s, :, j * lanes : (j + 1) * lanes] = x_refs[s][:, pl.ds(off, lanes)]
                q = dot_t(x_refs[s][...], down_ref[:, s * step : (s + 1) * step])
                low = q if low is None else low + q
            low = jnp.where(ids_ref[...] == owner_ref[...], low, 0.0)
            sent = low[:, :lanes]
            for j in range(1, pool_rows // lanes):
                sent = sent + low[:, j * lanes : (j + 1) * lanes]
            out_ref[:, features:] = sent.astype(bf16)

        total = None
        for s in range(count):
            for i in range(per):
                x = moved[s, :, i * span : (i + 1) * span]
                p = jnp.dot(x, w_refs[s * per + i][...], preferred_element_type=f32)
                total = p if total is None else total + p
        out_ref[:, pl.ds(pl.multiple_of(n * tile, tile), tile)] = total.astype(bf16)

    whole = lambda shape: pl.BlockSpec(shape, lambda n, row, place: (0, 0))
    return pl.pallas_call(
        kernel,
        grid_spec=pltpu.PrefetchScalarGridSpec(
            num_scalar_prefetch=2,
            grid=(tiles,),
            in_specs=[whole((rows, step))] * count
            + [pl.BlockSpec((span, tile), lambda n, row, place: (0, n))] * len(flat)
            + [
                whole((pool_rows, count * step)),
                whole((1, pool_rows)),
                pl.BlockSpec((rows, 1), lambda n, row, place: (row[0], 0)),
            ],
            out_specs=whole((rows, features + lanes)),
            scratch_shapes=[pltpu.VMEM((count, rows, step), bf16)],
        ),
        out_shape=jax.ShapeDtypeStruct((rows, features + lanes), bf16),
        compiler_params=pltpu.CompilerParams(vmem_limit_bytes=vmem),
        cost_estimate=pl.CostEstimate(
            flops=2 * rows * count * step * features,
            bytes_accessed=2 * count * step * features,
            transcendentals=0,
        ),
        name="partial_product",
    )(row.reshape(1), places, *chunks, *flat, pool, owner, ids)


def body(
    layer_input,
    input_norm_weight,
    query_base_matrix,
    adapter_down_weight,
    adapter_up_weight,
    token_adapter_index,
):
    rank = adapter_down_weight.shape[2]
    parts = 4
    step = layer_input.shape[1] // parts
    t = lax.axis_index("tensor")
    r = lax.axis_index("replica")
    q = lax.axis_index("groups") * 4 + r
    inward = lambda a: lax.ppermute(a, "tensor", [(0, 1), (3, 2)])
    outward = lambda a: lax.ppermute(a, "tensor", [(1, 0), (2, 3)])
    cross = lambda a: lax.ppermute(a, "tensor", [(1, 2), (2, 1)])
    swap_y = lambda a: lax.ppermute(a, "groups", [(0, 1), (1, 0)])
    swap_x = lambda a: lax.ppermute(a, "replica", [(i, i ^ 2) for i in range(4)])
    swap_core = lambda a: lax.ppermute(a, "replica", [(i, i ^ 1) for i in range(4)])

    piece = step // 8
    half = piece // 2
    sent = [
        inward(lax.dynamic_slice_in_dim(query_base_matrix, s * step + q * piece, piece, 0))
        for s in range(2)
    ]

    pool = jnp.concatenate([adapter_down_weight[0].T, adapter_up_weight[0]], axis=1)
    pool = jnp.concatenate([pool, swap_x(pool)], axis=0)
    pool = jnp.concatenate([pool, swap_core(pool)], axis=0)
    owner = jnp.repeat(jnp.stack([r, r ^ 2, r ^ 1, r ^ 3]), rank).astype(jnp.int32)[None, :]
    ids = token_adapter_index[:, None]

    own = norm_chunks(layer_input, input_norm_weight[None, :], parts)
    order = (2, 3, 0, 1)
    out_own = {k: outward(own[k]) for k in (2, 3)}
    mid = {k: cross(own[k]) for k in order}
    end = {k: inward(own[k]) for k in order}
    out_mid = {k: outward(mid[k]) for k in (2, 3)}
    far = {k: cross(end[k]) for k in order}
    out_far = {k: outward(far[k]) for k in (2, 3)}

    slabs = []
    for s in range(2):
        a, b = sent[s][:half], sent[s][half:]
        a = jnp.concatenate([a, swap_y(a)], axis=0)
        b = jnp.concatenate([b, swap_x(b)], axis=0)
        mine = jnp.concatenate([a, swap_x(a), b, swap_y(b)], axis=0)
        slabs.append([mine, swap_core(mine)])
    places = []
    for o in (q, q ^ 1):
        places += [2 * o, 2 * (o ^ 4), 2 * (o ^ 2), 2 * (o ^ 6)]
        places += [2 * o + 1, 2 * (o ^ 2) + 1, 2 * (o ^ 4) + 1, 2 * (o ^ 6) + 1]
    places = jnp.stack(places).astype(jnp.int32)

    mid_row = jnp.where(t < 2, 2, 1).astype(jnp.int32)
    far_row = jnp.where(t < 2, 3, 0).astype(jnp.int32)
    t = t.astype(jnp.int32)

    def help_with(x, row):
        return outward(partial_product([x[0], x[1]], slabs, places, row, ids, owner, pool))

    def finish(row, partial, prev):
        return dict(row=row, partial=partial, prev=prev, owner=owner, ids=ids)

    part_own = help_with(own, t)
    part_mid = help_with(mid, mid_row)
    part_far = help_with(far, far_row)

    w = query_base_matrix
    out = product(0, [(own[k],) for k in range(4)], w, pool, None, finish(t, None, None))
    xs = [(end[0],), (end[1],), (end[2], out_own[2]), (end[3], out_own[3])]
    out = product(0, xs, w, pool, None, finish(t ^ 1, part_own, out))
    xs = [(mid[0],), (mid[1],), (mid[2], out_mid[2]), (mid[3], out_mid[3])]
    out = product(0, xs, w, pool, None, finish(mid_row, part_mid, out))
    carry = product(0, [(far[0],), (far[1],)], w, pool)
    xs = [(far[2], out_far[2]), (far[3], out_far[3])]
    return product(2, xs, w, pool, carry, finish(far_row, part_far, out))


def solution(mesh):
    placed = (
        P(("groups", "replica", "tensor"), None),
        P(),
        P(None, "tensor"),
        P("replica", None, None),
        P("replica", None, "tensor"),
        P(("groups", "replica")),
    )
    line = mesh.shape["tensor"] == 4 and mesh.shape["replica"] == 4 and mesh.shape["groups"] == 2
    return jax.shard_map(
        body if line else plain,
        mesh=mesh,
        in_specs=placed,
        out_specs=P(("groups", "replica"), "tensor"),
        check_vma=False,
    )
```

time: 307 us -> 395 us (1.29)
  Pallas kernels: 0 us -> 142 us
  matrix products: 72.6 us -> 0 us
  starting transfers between devices: 6.56 us -> 50.4 us
  waiting for transfers between devices: 205 us -> 170 us
  local copies, waits for them, and re-layouts: 1.9 us -> 20.1 us
  between operations: 13.2 us -> 0.49 us
    all_gather x4 -> x0, waiting for transfers between devices: 161 us -> none  [body(): lax.all_gather(normed[:, i * step:(i + 1) * step], 'tensor', axis=0, tile...]
    pallas_call x0 -> x9, Pallas kernels: none -> 142 us  [the longest x5 102 us: product(): pl.pallas_call(kernel, grid_spec=pltpu.PrefetchScalarGridSpec(num_scalar_...]
    ppermute x6 -> x35, waiting for transfers between devices: 42.8 us -> 170 us  [the longest x6 70.3 us: body(): inward = lambda a: lax.ppermute(a, 'tensor', [(0, 1), (3, 2)])]
    dot_general x8 -> x0, matrix products: 72.6 us -> none  [the longest x4 47.1 us: body(): jnp.dot(gathered[i], query_base_matrix[rows], preferred_element_type=jnp....]
    ppermute x6 -> x35, starting transfers between devices: 6.44 us -> 50.4 us  [the longest x6 19.5 us: body(): inward = lambda a: lax.ppermute(a, 'tensor', [(0, 1), (3, 2)])]
    unnamed x16 -> x58, local copies, waits for them, and re-layouts: 0.03 us -> 10 us
    concatenate x1 -> x7, other arithmetic: 3.21 us -> 10 us  [the longest x1 6.86 us: body(): pool = jnp.concatenate([pool, swap_core(pool)], axis=0)]
  transfers between devices with their start and end apart: 10 -> 35, of which waited for: 6 -> 16; matrix products, arithmetic and copies ran while one was open for 20% -> 6% of each run, Pallas kernels for 0% -> 32%
where the time goes in v2:
time: 395 us; the launch traced here: 394 us
  waiting for transfers between devices  170 us (43%)
  Pallas kernels  142 us (36%)
  starting transfers between devices  50.4 us (13%)
  local copies, waits for them, and re-layouts  20.1 us (5%)
  other arithmetic  10.1 us (3%)
    pallas_call x5, Pallas kernels, product(): pl.pallas_call(kernel, grid_spec=pltpu.PrefetchScalarGridSpec(num_scalar_...  102 us
    ppermute x6, waiting for transfers between devices, body(): inward = lambda a: lax.ppermute(a, 'tensor', [(0, 1), (3, 2)])  70.3 us
    ppermute x9, waiting for transfers between devices, body(): outward = lambda a: lax.ppermute(a, 'tensor', [(1, 0), (2, 3)])  56.7 us
    ppermute x5, waiting for transfers between devices, body(): lax.ppermute(a, 'replica', [(i, i ^ 2) for i in range(4)])  37.3 us
    pallas_call x3, Pallas kernels, partial_product(): pl.pallas_call(kernel, grid_spec=pltpu.PrefetchScalarGridSpec(num_scalar_...  36.1 us
    ppermute x6, starting transfers between devices, body(): inward = lambda a: lax.ppermute(a, 'tensor', [(0, 1), (3, 2)])  19.5 us
    ppermute x9, starting transfers between devices, body(): outward = lambda a: lax.ppermute(a, 'tensor', [(1, 0), (2, 3)])  11.8 us
    unnamed x58, local copies, waits for them, and re-layouts  10 us
  transfers between devices with their start and end apart: 35, of which 16 were waited for; matrix products, arithmetic and copies ran while one was open for 6% of the time, Pallas kernels for 32%

profile of v2, /device:TPU:0, one launch (start us, length us, event | category | flops | bytes accessed | tf_op | source)
XLA Modules:
  0.0 393.6 jit_solution(11725697828409753311)
XLA Ops:
  0.0 2.9 constant_dynamic-slice_fusion
  2.9 5.0 %collective-permute-start.18 = (bf16[256,2048]{1,0:T(8,128)(2,1)S(1)}, bf16[256,2048]{1,0:T(8,128)(2,1)S(1)}, u32[]{:S(2)}, u32[]{:S(2)}) collective-permute-start(bf16[256,2048]{1,0:T(8,128)(2,1)S(1)} %get-tuple-element.17), channel_id=1, source_target_pairs={{0,1},{3,2},{4,5},{7,6},{8,9},{11,10},{12,13},{15,14},{16,17},{19,... | collective-permute-start | bytes 3145736 | tf_op jit(solution)/shard_map/ppermute | solution.py:295
  12.6 4.8 %norm_chunks.1 = (bf16[192,2048]{1,0:T(8,128)(2,1)}, bf16[192,2048]{1,0:T(8,128)(2,1)}, bf16[192,2048]{1,0:T(8,128)(2,1)}, bf16[192,2048]{1,0:T(8,128)(2,1)}) custom-call(bf16[192,8192]{1,0:T(8,128)(2,1)} %x_ref.1, bf16[1,8192]{1,0:T(2,128)(2,1)} %broadcast_in_dim.9.g_ref), custom_call_target="tpu_custom_call" | custom-call | flops 7864320 | bytes 6291456 | tf_op jit(solution)/shard_map/norm_chunks/pallas_call | solution.py:54
  18.8 12.7 %collective-permute-done.18 = bf16[256,2048]{1,0:T(8,128)(2,1)S(1)} collective-permute-done((bf16[256,2048]{1,0:T(8,128)(2,1)S(1)}, bf16[256,2048]{1,0:T(8,128)(2,1)S(1)}, u32[]{:S(2)}, u32[]{:S(2)}) %collective-permute-start.18) | collective-permute-done | bytes 1048608 | tf_op jit(solution)/shard_map/ppermute | solution.py:295
  35.4 18.6 %collective-permute-done.12 = bf16[256,2048]{1,0:T(8,128)(2,1)S(1)} collective-permute-done((bf16[256,2048]{1,0:T(8,128)(2,1)}, bf16[256,2048]{1,0:T(8,128)(2,1)S(1)}, u32[]{:S(2)}, u32[]{:S(2)}) %collective-permute-start.12) | collective-permute-done | bytes 1048608 | tf_op jit(solution)/shard_map/ppermute | solution.py:295
  58.0 1.7 pad_maximum_fusion.1
  61.3 5.7 %collective-permute-done.13 = bf16[128,2048]{1,0:T(8,128)(2,1)S(1)} collective-permute-done((bf16[128,2048]{1,0:T(8,128)(2,1)S(1)}, bf16[128,2048]{1,0:T(8,128)(2,1)S(1)}, u32[]{:S(2)}, u32[]{:S(2)}) %collective-permute-start.13) | collective-permute-done | bytes 524320 | tf_op jit(solution)/shard_map/ppermute | solution.py:298
  68.6 2.7 collective-permute-done.15
  73.8 20.0 %collective-permute-done.20 = bf16[256,2048]{1,0:T(8,128)(2,1)S(1)} collective-permute-done((bf16[256,2048]{1,0:T(8,128)(2,1)S(1)}, bf16[256,2048]{1,0:T(8,128)(2,1)S(1)}, u32[]{:S(2)}, u32[]{:S(2)}) %collective-permute-start.20) | collective-permute-done | bytes 1048608 | tf_op jit(solution)/shard_map/ppermute | solution.py:299
  98.3 14.5 %collective-permute-done.14 = bf16[256,2048]{1,0:T(8,128)(2,1)S(1)} collective-permute-done((bf16[256,2048]{1,0:T(8,128)(2,1)S(1)}, bf16[256,2048]{1,0:T(8,128)(2,1)S(1)}, u32[]{:S(2)}, u32[]{:S(2)}) %collective-permute-start.14) | collective-permute-done | bytes 1048608 | tf_op jit(solution)/shard_map/ppermute | solution.py:299
  116.7 4.3 %collective-permute-start.10 = (bf16[192,2048]{1,0:T(8,128)(2,1)S(1)}, bf16[192,2048]{1,0:T(8,128)(2,1)S(1)}, u32[]{:S(2)}, u32[]{:S(2)}) collective-permute-start(bf16[192,2048]{1,0:T(8,128)(2,1)S(1)} %copy-done.3), channel_id=1, source_target_pairs={{0,1},{3,2},{4,5},{7,6},{8,9},{11,10},{12,13},{15,14},{16,17},{19,... | collective-permute-start | bytes 2359304 | tf_op jit(solution)/shard_map/ppermute | solution.py:295
  121.1 2.2 collective-permute-start.3
  123.3 15.6 %collective-permute-done.10.refs_1_ = bf16[192,2048]{1,0:T(8,128)(2,1)S(1)} collective-permute-done((bf16[192,2048]{1,0:T(8,128)(2,1)S(1)}, bf16[192,2048]{1,0:T(8,128)(2,1)S(1)}, u32[]{:S(2)}, u32[]{:S(2)}) %collective-permute-start.10) | collective-permute-done | bytes 786464 | tf_op jit(solution)/shard_map/ppermute | solution.py:295
  139.8 5.3 %collective-permute-start.8 = (bf16[192,2048]{1,0:T(8,128)(2,1)}, bf16[192,2048]{1,0:T(8,128)(2,1)}, u32[]{:S(2)}, u32[]{:S(2)}) collective-permute-start(bf16[192,2048]{1,0:T(8,128)(2,1)} %get-tuple-element.13.refs_0_), channel_id=1, source_target_pairs={{0,1},{3,2},{4,5},{7,6},{8,9},{11,10},{12,13},{15,14},{16,17},{19,... | collective-permute-start | bytes 2359304 | tf_op jit(solution)/shard_map/ppermute | solution.py:295
  145.0 10.7 %collective-permute-done.3.refs_4_ = bf16[192,2048]{1,0:T(8,128)(2,1)} collective-permute-done((bf16[192,2048]{1,0:T(8,128)(2,1)S(1)}, bf16[192,2048]{1,0:T(8,128)(2,1)}, u32[]{:S(2)}, u32[]{:S(2)}) %collective-permute-start.3) | collective-permute-done | bytes 786464 | tf_op jit(solution)/shard_map/ppermute | solution.py:295
  159.5 12.8 %collective-permute-done.8.refs_0_ = bf16[192,2048]{1,0:T(8,128)(2,1)} collective-permute-done((bf16[192,2048]{1,0:T(8,128)(2,1)}, bf16[192,2048]{1,0:T(8,128)(2,1)}, u32[]{:S(2)}, u32[]{:S(2)}) %collective-permute-start.8) | collective-permute-done | bytes 786464 | tf_op jit(solution)/shard_map/ppermute | solution.py:295
  173.6 3.4 collective-permute-done.32.refs_3_
  179.2 6.9 %pad_maximum_fusion.refs_3_.refs_6_.refs_5_.refs_7_.refs_8_ = bf16[256,10240]{1,0:T(8,128)(2,1)} fusion(bf16[128,10240]{1,0:T(8,128)(2,1)} %collective-permute-done.7, bf16[64,10240]{1,0:T(8,128)(2,1)S(1)} %collective-permute-done.6, bf16[64,2048]{1,0:T(8,128)(2,1)S(1)} %bitcast.33, bf16[64,8192]{1,0:T(8,128)(2,1)S(1)} %bitcast.30), kind=kLoop, calls=%fused_computation | loop fusion | flops 20971520 | bytes 10485760 | tf_op jit(solution)/shard_map/concatenate | solution.py:311
  186.1 7.6 %collective-permute-done.33.refs_5_ = bf16[192,2048]{1,0:T(8,128)(2,1)S(1)} collective-permute-done((bf16[192,2048]{1,0:T(8,128)(2,1)}, bf16[192,2048]{1,0:T(8,128)(2,1)S(1)}, u32[]{:S(2)}, u32[]{:S(2)}) %collective-permute-start.33) | collective-permute-done | bytes 786464 | tf_op jit(solution)/shard_map/ppermute | solution.py:296
  195.9 24.2 %product.6.refs_12_ = bf16[768,2048]{1,0:T(8,128)(2,1)} custom-call(s32[1]{0:T(128)} %bitcast.26.row_ref, bf16[192,2048]{1,0:T(8,128)(2,1)} %get-tuple-element.13.refs_0_, bf16[192,2048]{1,0:T(8,128)(2,1)} %get-tuple-element.14.refs_1_, bf16[192,2048]{1,0:T(8,128)(2,1)} %get-tuple-element.11.refs_2_, bf16[192,2048]{1,0:T(8,128)(2,1)} %get-tuple-element.12.refs_3_, ...), custom_call_target="tpu_custom_call" | custom-call | flops 7247757312 | bytes 33554432 | tf_op jit(solution)/shard_map/product/pallas_call | solution.py:195
  222.3 12.0 %partial_product.5 = bf16[192,2176]{1,0:T(8,128)(2,1)} custom-call(s32[1]{0:T(128)} %bitcast.26.row_ref, s32[16]{0:T(128)} %stack.87.place_ref, bf16[192,2048]{1,0:T(8,128)(2,1)} %get-tuple-element.13.refs_0_, bf16[192,2048]{1,0:T(8,128)(2,1)} %get-tuple-element.14.refs_1_, bf16[1024,2048]{1,0:T(8,128)(2,1)} %constant_dynamic-update-slice_fusion.refs_2_, ...), custom_call_target="tpu_custom_call" | custom-call | flops 3221225472 | bytes 16777216 | tf_op jit(solution)/shard_map/partial_product/pallas_call | solution.py:255
  238.1 12.8 %product.5 = (f32[192,2048]{1,0:T(8,128)}, f32[192,256]{1,0:T(8,128)}) custom-call(s32[1]{0:T(128)} %constant.10.clone.1.row_ref, bf16[192,2048]{1,0:T(8,128)(2,1)} %copy-done.5, bf16[192,2048]{1,0:T(8,128)(2,1)} %copy-done.4, bf16[8192,2048]{1,0:T(8,128)(2,1)} %refs_4_.3, bf16[256,10240]{1,0:T(8,128)(2,1)} %pad_maximum_fusion.refs_3_.refs_6_.refs_5_.refs_7_.refs_8_), custom_call_target="tpu_custom_call" | custom-call | flops 3623878656 | bytes 16777216 | tf_op jit(solution)/shard_map/product/pallas_call | solution.py:195
  250.9 12.1 %partial_product.4 = bf16[192,2176]{1,0:T(8,128)(2,1)} custom-call(s32[1]{0:T(128)} %bitcast.24.row_ref, s32[16]{0:T(128)} %stack.87.place_ref, bf16[192,2048]{1,0:T(8,128)(2,1)} %copy-done.1, bf16[192,2048]{1,0:T(8,128)(2,1)} %copy-done.2, bf16[1024,2048]{1,0:T(8,128)(2,1)} %constant_dynamic-update-slice_fusion.refs_2_, ...), custom_call_target="tpu_custom_call" | custom-call | flops 3221225472 | bytes 16777216 | tf_op jit(solution)/shard_map/partial_product/pallas_call | solution.py:255
  265.6 12.1 %partial_product.3 = bf16[192,2176]{1,0:T(8,128)(2,1)} custom-call(s32[1]{0:T(128)} %bitcast.row_ref, s32[16]{0:T(128)} %stack.87.place_ref, bf16[192,2048]{1,0:T(8,128)(2,1)} %copy-done.5, bf16[192,2048]{1,0:T(8,128)(2,1)} %copy-done.4, bf16[1024,2048]{1,0:T(8,128)(2,1)} %constant_dynamic-update-slice_fusion.refs_2_, ...), custom_call_target="tpu_custom_call" | custom-call | flops 3221225472 | bytes 16777216 | tf_op jit(solution)/shard_map/partial_product/pallas_call | solution.py:255
  280.3 3.2 collective-permute-done.34.refs_11_
  284.8 25.0 %product.7.refs_12_ = bf16[768,2048]{1,0:T(8,128)(2,1)} custom-call(s32[1]{0:T(128)} %bitcast.25.row_ref, bf16[192,2048]{1,0:T(8,128)(2,1)} %collective-permute-done.8.refs_0_, bf16[192,2048]{1,0:T(8,128)(2,1)} %copy-done.12, bf16[192,2048]{1,0:T(8,128)(2,1)} %copy-done.10, ...), custom_call_target="tpu_custom_call", output_to_operand_aliasing={{}: (13, {})} | custom-call | flops 7247757312 | bytes 33554432 | tf_op jit(solution)/shard_map/product/pallas_call | solution.py:195
  309.8 2.8 collective-permute-done.30.refs_5_
  312.6 17.9 %collective-permute-done.31.refs_11_ = bf16[192,2176]{1,0:T(8,128)(2,1)S(1)} collective-permute-done((bf16[192,2176]{1,0:T(8,128)(2,1)}, bf16[192,2176]{1,0:T(8,128)(2,1)S(1)}, u32[]{:S(2)}, u32[]{:S(2)}) %collective-permute-start.31) | collective-permute-done | bytes 835616 | tf_op jit(solution)/shard_map/ppermute | solution.py:296
  331.4 24.9 %product.8.refs_12_ = bf16[768,2048]{1,0:T(8,128)(2,1)} custom-call(s32[1]{0:T(128)} %bitcast.24.row_ref, bf16[192,2048]{1,0:T(8,128)(2,1)} %copy-done.1, bf16[192,2048]{1,0:T(8,128)(2,1)} %copy-done.2, bf16[192,2048]{1,0:T(8,128)(2,1)} %collective-permute-done.27.refs_2_, bf16[192,2048]{1,0:T(8,128)(2,1)} %copy-done.16, ...), custom_call_target="tpu_custom_call", output_to_operand_aliasing={{}: (13, {})} | custom-call | flops 7247757312 | bytes 33554432 | tf_op jit(solution)/shard_map/product/pallas_call | solution.py:195
  356.3 7.9 %collective-permute-done.5.refs_3_ = bf16[192,2048]{1,0:T(8,128)(2,1)S(1)} collective-permute-done((bf16[192,2048]{1,0:T(8,128)(2,1)}, bf16[192,2048]{1,0:T(8,128)(2,1)S(1)}, u32[]{:S(2)}, u32[]{:S(2)}) %collective-permute-start.5) | collective-permute-done | bytes 786464 | tf_op jit(solution)/shard_map/ppermute | solution.py:296
  364.2 13.9 %collective-permute-done.24.refs_11_ = bf16[192,2176]{1,0:T(8,128)(2,1)S(1)} collective-permute-done((bf16[192,2176]{1,0:T(8,128)(2,1)}, bf16[192,2176]{1,0:T(8,128)(2,1)S(1)}, u32[]{:S(2)}, u32[]{:S(2)}) %collective-permute-start.24) | collective-permute-done | bytes 835616 | tf_op jit(solution)/shard_map/ppermute | solution.py:296
  379.0 14.6 %product.9 = bf16[768,2048]{1,0:T(8,128)(2,1)} custom-call(s32[1]{0:T(128)} %bitcast.row_ref, bf16[192,2048]{1,0:T(8,128)(2,1)} %copy-done.20, bf16[192,2048]{1,0:T(8,128)(2,1)} %copy-done.21, bf16[192,2048]{1,0:T(8,128)(2,1)} %collective-permute-done.4.refs_2_, bf16[192,2048]{1,0:T(8,128)(2,1)} %copy-done.22, ...), custom_call_target="tpu_custom_call", output_to_operand_aliasing={{}: (13, {})} | custom-call | flops 3623878656 | bytes 16777216 | tf_op jit(solution)/shard_map/product/pallas_call | solution.py:195
  (123 shorter events, 52.4 us)
Async XLA Ops:
  2.9 28.5 %collective-permute-start.18 = (bf16[256,2048]{1,0:T(8,128)(2,1)S(1)}, bf16[256,2048]{1,0:T(8,128)(2,1)S(1)}, u32[]{:S(2)}, u32[]{:S(2)}) collective-permute-start(bf16[256,2048]{1,0:T(8,128)(2,1)S(1)} %get-tuple-element.17), channel_id=1, source_target_pairs={{0,1},{3,2},{4,5},{7,6},{8,9},{11,10},{12,13},{15,14},{16,17},{19,... | collective-permute-start | bytes 3145736 | tf_op jit(solution)/shard_map/ppermute | solution.py:295
  7.9 46.1 %collective-permute-start.12 = (bf16[256,2048]{1,0:T(8,128)(2,1)}, bf16[256,2048]{1,0:T(8,128)(2,1)S(1)}, u32[]{:S(2)}, u32[]{:S(2)}) collective-permute-start(bf16[256,2048]{1,0:T(8,128)(2,1)} %get-tuple-element.18), channel_id=1, source_target_pairs={{0,1},{3,2},{4,5},{7,6},{8,9},{11,10},{12,13},{15,14},{16,17},{19,... | collective-permute-start | bytes 3145736 | tf_op jit(solution)/shard_map/ppermute | solution.py:295
  10.5 46.0 %collective-permute-start.6 = (bf16[64,10240]{1,0:T(8,128)(2,1)}, bf16[64,10240]{1,0:T(8,128)(2,1)S(1)}, u32[]{:S(2)}, u32[]{:S(2)}) collective-permute-start(bf16[64,10240]{1,0:T(8,128)(2,1)} %pad_maximum_fusion.2), channel_id=1, source_target_pairs={{0,8},{4,12},{8,0},{12,4},{1,9},{5,13},{9,1},{13,5},{2,10},{6,14},... | collective-permute-start | bytes 3932168 | tf_op jit(solution)/shard_map/ppermute | solution.py:299
  17.4 103.6 %collective-permute-start = (bf16[192,2048]{1,0:T(8,128)(2,1)}, bf16[192,2048]{1,0:T(8,128)(2,1)S(1)}, u32[]{:S(2)}, u32[]{:S(2)}) collective-permute-start(bf16[192,2048]{1,0:T(8,128)(2,1)} %get-tuple-element.11.refs_2_), channel_id=1, source_target_pairs={{0,1},{3,2},{4,5},{7,6},{8,9},{11,10},{12,13},{15,14},{16,17},{19,... | collective-permute-start | bytes 2359304 | tf_op jit(solution)/shard_map/ppermute | solution.py:295
  32.4 27.4 %collective-permute-start.19 = (bf16[128,2048]{1,0:T(8,128)(2,1)S(1)}, bf16[128,2048]{1,0:T(8,128)(2,1)S(1)}, u32[]{:S(2)}, u32[]{:S(2)}) collective-permute-start(bf16[128,2048]{1,0:T(8,128)(2,1)S(1)} %get-tuple-element.21), channel_id=1, source_target_pairs={{0,16},{16,0},{1,17},{17,1},{2,18},{18,2},{3,19},{19,3},{4,20},{20... | collective-permute-start | bytes 1572872 | tf_op jit(solution)/shard_map/ppermute | solution.py:298
  33.9 27.4 %collective-permute-start.21 = (bf16[128,2048]{1,0:T(8,128)(2,1)S(1)}, bf16[128,2048]{1,0:T(8,128)(2,1)S(1)}, u32[]{:S(2)}, u32[]{:S(2)}) collective-permute-start(bf16[128,2048]{1,0:T(8,128)(2,1)S(1)} %get-tuple-element.19), channel_id=1, source_target_pairs={{0,8},{4,12},{8,0},{12,4},{1,9},{5,13},{9,1},{13,5},{2,10},{6,14},... | collective-permute-start | bytes 1572872 | tf_op jit(solution)/shard_map/ppermute | solution.py:299
  59.8 34.0 %collective-permute-start.20 = (bf16[256,2048]{1,0:T(8,128)(2,1)S(1)}, bf16[256,2048]{1,0:T(8,128)(2,1)S(1)}, u32[]{:S(2)}, u32[]{:S(2)}) collective-permute-start(bf16[256,2048]{1,0:T(8,128)(2,1)S(1)} %pad_maximum_fusion.5), channel_id=1, source_target_pairs={{0,8},{4,12},{8,0},{12,4},{1,9},{5,13},{9,1},{13,5},{2,10},{6,14},... | collective-permute-start | bytes 3145736 | tf_op jit(solution)/shard_map/ppermute | solution.py:299
  61.2 116.4 %collective-permute-start.7 = (bf16[128,10240]{1,0:T(8,128)(2,1)}, bf16[128,10240]{1,0:T(8,128)(2,1)}, u32[]{:S(2)}, u32[]{:S(2)}) collective-permute-start(bf16[128,10240]{1,0:T(8,128)(2,1)} %pad_maximum_fusion.1), channel_id=1, source_target_pairs={{0,4},{4,0},{8,12},{12,8},{1,5},{5,1},{9,13},{13,9},{2,6},{6,2},{1... | collective-permute-start | bytes 7864328 | tf_op jit(solution)/shard_map/ppermute | solution.py:300
  67.1 30.1 %collective-permute-start.22 = (bf16[256,2048]{1,0:T(8,128)(2,1)S(1)}, bf16[256,2048]{1,0:T(8,128)(2,1)S(1)}, u32[]{:S(2)}, u32[]{:S(2)}) collective-permute-start(bf16[256,2048]{1,0:T(8,128)(2,1)S(1)} %pad_maximum_fusion.6), channel_id=1, source_target_pairs={{0,16},{16,0},{1,17},{17,1},{2,18},{18,2},{3,19},{19,3},{4,20},{20... | collective-permute-start | bytes 3145736 | tf_op jit(solution)/shard_map/ppermute | solution.py:298
  71.4 41.4 %collective-permute-start.14 = (bf16[256,2048]{1,0:T(8,128)(2,1)S(1)}, bf16[256,2048]{1,0:T(8,128)(2,1)S(1)}, u32[]{:S(2)}, u32[]{:S(2)}) collective-permute-start(bf16[256,2048]{1,0:T(8,128)(2,1)S(1)} %pad_maximum_fusion.3), channel_id=1, source_target_pairs={{0,8},{4,12},{8,0},{12,4},{1,9},{5,13},{9,1},{13,5},{2,10},{6,14},... | collective-permute-start | bytes 3145736 | tf_op jit(solution)/shard_map/ppermute | solution.py:299
  93.8 21.8 %collective-permute-start.16 = (bf16[256,2048]{1,0:T(8,128)(2,1)S(1)}, bf16[256,2048]{1,0:T(8,128)(2,1)S(1)}, u32[]{:S(2)}, u32[]{:S(2)}) collective-permute-start(bf16[256,2048]{1,0:T(8,128)(2,1)S(1)} %pad_maximum_fusion.4), channel_id=1, source_target_pairs={{0,16},{16,0},{1,17},{17,1},{2,18},{18,2},{3,19},{19,3},{4,20},{20... | collective-permute-start | bytes 3145736 | tf_op jit(solution)/shard_map/ppermute | solution.py:298
  98.3 121.9 %collective-permute-start.23 = (bf16[1024,2048]{1,0:T(8,128)(2,1)}, bf16[1024,2048]{1,0:T(8,128)(2,1)}, u32[]{:S(2)}, u32[]{:S(2)}) collective-permute-start(bf16[1024,2048]{1,0:T(8,128)(2,1)} %constant_dynamic-update-slice_fusion.6.refs_4_), channel_id=1, source_target_pairs={{0,4},{4,0},{8,12},{12,8},{1,5},{5,1},{9,13},{13,9},{2,6},{6,2},{1... | collective-permute-start | bytes 12582920 | tf_op jit(solution)/shard_map/ppermute | solution.py:300
  116.7 104.3 %collective-permute-start.17 = (bf16[1024,2048]{1,0:T(8,128)(2,1)}, bf16[1024,2048]{1,0:T(8,128)(2,1)}, u32[]{:S(2)}, u32[]{:S(2)}) collective-permute-start(bf16[1024,2048]{1,0:T(8,128)(2,1)} %constant_dynamic-update-slice_fusion.refs_2_), channel_id=1, source_target_pairs={{0,4},{4,0},{8,12},{12,8},{1,5},{5,1},{9,13},{13,9},{2,6},{6,2},{1... | collective-permute-start | bytes 12582920 | tf_op jit(solution)/shard_map/ppermute | solution.py:300
  116.7 22.1 %collective-permute-start.10 = (bf16[192,2048]{1,0:T(8,128)(2,1)S(1)}, bf16[192,2048]{1,0:T(8,128)(2,1)S(1)}, u32[]{:S(2)}, u32[]{:S(2)}) collective-permute-start(bf16[192,2048]{1,0:T(8,128)(2,1)S(1)} %copy-done.3), channel_id=1, source_target_pairs={{0,1},{3,2},{4,5},{7,6},{8,9},{11,10},{12,13},{15,14},{16,17},{19,... | collective-permute-start | bytes 2359304 | tf_op jit(solution)/shard_map/ppermute | solution.py:295
  121.1 34.6 %collective-permute-start.3 = (bf16[192,2048]{1,0:T(8,128)(2,1)S(1)}, bf16[192,2048]{1,0:T(8,128)(2,1)}, u32[]{:S(2)}, u32[]{:S(2)}) collective-permute-start(bf16[192,2048]{1,0:T(8,128)(2,1)S(1)} %copy-done.18), channel_id=1, source_target_pairs={{0,1},{3,2},{4,5},{7,6},{8,9},{11,10},{12,13},{15,14},{16,17},{19,... | collective-permute-start | bytes 2359304 | tf_op jit(solution)/shard_map/ppermute | solution.py:295
  139.8 32.5 %collective-permute-start.8 = (bf16[192,2048]{1,0:T(8,128)(2,1)}, bf16[192,2048]{1,0:T(8,128)(2,1)}, u32[]{:S(2)}, u32[]{:S(2)}) collective-permute-start(bf16[192,2048]{1,0:T(8,128)(2,1)} %get-tuple-element.13.refs_0_), channel_id=1, source_target_pairs={{0,1},{3,2},{4,5},{7,6},{8,9},{11,10},{12,13},{15,14},{16,17},{19,... | collective-permute-start | bytes 2359304 | tf_op jit(solution)/shard_map/ppermute | solution.py:295
  155.7 21.2 %collective-permute-start.32 = (bf16[192,2048]{1,0:T(8,128)(2,1)}, bf16[192,2048]{1,0:T(8,128)(2,1)}, u32[]{:S(2)}, u32[]{:S(2)}) collective-permute-start(bf16[192,2048]{1,0:T(8,128)(2,1)} %get-tuple-element.11.refs_2_), channel_id=1, source_target_pairs={{1,0},{2,3},{5,4},{6,7},{9,8},{10,11},{13,12},{14,15},{17,16},{18,... | collective-permute-start | bytes 2359304 | tf_op jit(solution)/shard_map/ppermute | solution.py:296
  172.3 21.4 %collective-permute-start.33 = (bf16[192,2048]{1,0:T(8,128)(2,1)}, bf16[192,2048]{1,0:T(8,128)(2,1)S(1)}, u32[]{:S(2)}, u32[]{:S(2)}) collective-permute-start(bf16[192,2048]{1,0:T(8,128)(2,1)} %get-tuple-element.12.refs_3_), channel_id=1, source_target_pairs={{1,0},{2,3},{5,4},{6,7},{9,8},{10,11},{13,12},{14,15},{17,16},{18,... | collective-permute-start | bytes 2359304 | tf_op jit(solution)/shard_map/ppermute | solution.py:296
  177.6 17.5 %collective-permute-start.27 = (bf16[192,2048]{1,0:T(8,128)(2,1)}, bf16[192,2048]{1,0:T(8,128)(2,1)}, u32[]{:S(2)}, u32[]{:S(2)}) collective-permute-start(bf16[192,2048]{1,0:T(8,128)(2,1)} %get-tuple-element.11.refs_2_), channel_id=1, source_target_pairs={{1,2},{2,1},{5,6},{6,5},{9,10},{10,9},{13,14},{14,13},{17,18},{18,... | collective-permute-start | bytes 2359304 | tf_op jit(solution)/shard_map/ppermute | solution.py:297
  193.7 40.6 %collective-permute-start.26 = (bf16[192,2048]{1,0:T(8,128)(2,1)S(1)}, bf16[192,2048]{1,0:T(8,128)(2,1)S(1)}, u32[]{:S(2)}, u32[]{:S(2)}) collective-permute-start(bf16[192,2048]{1,0:T(8,128)(2,1)S(1)} %copy-done.3), channel_id=1, source_target_pairs={{1,2},{2,1},{5,6},{6,5},{9,10},{10,9},{13,14},{14,13},{17,18},{18,... | collective-permute-start | bytes 2359304 | tf_op jit(solution)/shard_map/ppermute | solution.py:297
  194.4 40.6 %collective-permute-start.11 = (bf16[192,2048]{1,0:T(8,128)(2,1)S(1)}, bf16[192,2048]{1,0:T(8,128)(2,1)S(1)}, u32[]{:S(2)}, u32[]{:S(2)}) collective-permute-start(bf16[192,2048]{1,0:T(8,128)(2,1)S(1)} %copy-done.13), channel_id=1, source_target_pairs={{1,2},{2,1},{5,6},{6,5},{9,10},{10,9},{13,14},{14,13},{17,18},{18,... | collective-permute-start | bytes 2359304 | tf_op jit(solution)/shard_map/ppermute | solution.py:297
  195.1 41.5 %collective-permute-start.9 = (bf16[192,2048]{1,0:T(8,128)(2,1)}, bf16[192,2048]{1,0:T(8,128)(2,1)S(1)}, u32[]{:S(2)}, u32[]{:S(2)}) collective-permute-start(bf16[192,2048]{1,0:T(8,128)(2,1)} %collective-permute-done.8.refs_0_), channel_id=1, source_target_pairs={{1,2},{2,1},{5,6},{6,5},{9,10},{10,9},{13,14},{14,13},{17,18},{18,... | collective-permute-start | bytes 2359304 | tf_op jit(solution)/shard_map/ppermute | solution.py:297
  220.1 42.8 %collective-permute-start.29 = (bf16[192,2048]{1,0:T(8,128)(2,1)S(1)}, bf16[192,2048]{1,0:T(8,128)(2,1)S(1)}, u32[]{:S(2)}, u32[]{:S(2)}) collective-permute-start(bf16[192,2048]{1,0:T(8,128)(2,1)S(1)} %copy-done.19), channel_id=1, source_target_pairs={{1,2},{2,1},{5,6},{6,5},{9,10},{10,9},{13,14},{14,13},{17,18},{18,... | collective-permute-start | bytes 2359304 | tf_op jit(solution)/shard_map/ppermute | solution.py:297
  221.0 43.3 %collective-permute-start.28 = (bf16[192,2048]{1,0:T(8,128)(2,1)}, bf16[192,2048]{1,0:T(8,128)(2,1)S(1)}, u32[]{:S(2)}, u32[]{:S(2)}) collective-permute-start(bf16[192,2048]{1,0:T(8,128)(2,1)} %collective-permute-done.27.refs_2_), channel_id=1, source_target_pairs={{1,0},{2,3},{5,4},{6,7},{9,8},{10,11},{13,12},{14,15},{17,16},{18,... | collective-permute-start | bytes 2359304 | tf_op jit(solution)/shard_map/ppermute | solution.py:296
  234.3 43.4 %collective-permute-start.1 = (bf16[192,2048]{1,0:T(8,128)(2,1)S(1)}, bf16[192,2048]{1,0:T(8,128)(2,1)S(1)}, u32[]{:S(2)}, u32[]{:S(2)}) collective-permute-start(bf16[192,2048]{1,0:T(8,128)(2,1)S(1)} %copy-done.11), channel_id=1, source_target_pairs={{1,2},{2,1},{5,6},{6,5},{9,10},{10,9},{13,14},{14,13},{17,18},{18,... | collective-permute-start | bytes 2359304 | tf_op jit(solution)/shard_map/ppermute | solution.py:297
  235.0 43.9 %collective-permute-start.4 = (bf16[192,2048]{1,0:T(8,128)(2,1)}, bf16[192,2048]{1,0:T(8,128)(2,1)}, u32[]{:S(2)}, u32[]{:S(2)}) collective-permute-start(bf16[192,2048]{1,0:T(8,128)(2,1)} %collective-permute-done.3.refs_4_), channel_id=1, source_target_pairs={{1,2},{2,1},{5,6},{6,5},{9,10},{10,9},{13,14},{14,13},{17,18},{18,... | collective-permute-start | bytes 2359304 | tf_op jit(solution)/shard_map/ppermute | solution.py:297
  236.6 46.9 %collective-permute-start.34 = (bf16[192,2176]{1,0:T(8,128)(2,1)}, bf16[192,2176]{1,0:T(8,128)(2,1)S(1)}, u32[]{:S(2)}, u32[]{:S(2)}) collective-permute-start(bf16[192,2176]{1,0:T(8,128)(2,1)} %partial_product.5), channel_id=1, source_target_pairs={{1,0},{2,3},{5,4},{6,7},{9,8},{10,11},{13,12},{14,15},{17,16},{18,... | collective-permute-start | bytes 2506760 | tf_op jit(solution)/shard_map/ppermute | solution.py:296
  263.0 49.6 %collective-permute-start.30 = (bf16[192,2048]{1,0:T(8,128)(2,1)S(1)}, bf16[192,2048]{1,0:T(8,128)(2,1)S(1)}, u32[]{:S(2)}, u32[]{:S(2)}) collective-permute-start(bf16[192,2048]{1,0:T(8,128)(2,1)S(1)} %collective-permute-done.29.refs_4_), channel_id=1, source_target_pairs={{1,0},{2,3},{5,4},{6,7},{9,8},{10,11},{13,12},{14,15},{17,16},{18,... | collective-permute-start | bytes 2359304 | tf_op jit(solution)/shard_map/ppermute | solution.py:296
  264.3 66.2 %collective-permute-start.31 = (bf16[192,2176]{1,0:T(8,128)(2,1)}, bf16[192,2176]{1,0:T(8,128)(2,1)S(1)}, u32[]{:S(2)}, u32[]{:S(2)}) collective-permute-start(bf16[192,2176]{1,0:T(8,128)(2,1)} %partial_product.4), channel_id=1, source_target_pairs={{1,0},{2,3},{5,4},{6,7},{9,8},{10,11},{13,12},{14,15},{17,16},{18,... | collective-permute-start | bytes 2506760 | tf_op jit(solution)/shard_map/ppermute | solution.py:296
  277.7 78.6 %collective-permute-start.2 = (bf16[192,2048]{1,0:T(8,128)(2,1)S(1)}, bf16[192,2048]{1,0:T(8,128)(2,1)S(1)}, u32[]{:S(2)}, u32[]{:S(2)}) collective-permute-start(bf16[192,2048]{1,0:T(8,128)(2,1)S(1)} %collective-permute-done.1.refs_0_), channel_id=1, source_target_pairs={{1,0},{2,3},{5,4},{6,7},{9,8},{10,11},{13,12},{14,15},{17,16},{18,... | collective-permute-start | bytes 2359304 | tf_op jit(solution)/shard_map/ppermute | solution.py:296
  279.0 85.2 %collective-permute-start.5 = (bf16[192,2048]{1,0:T(8,128)(2,1)}, bf16[192,2048]{1,0:T(8,128)(2,1)S(1)}, u32[]{:S(2)}, u32[]{:S(2)}) collective-permute-start(bf16[192,2048]{1,0:T(8,128)(2,1)} %collective-permute-done.4.refs_2_), channel_id=1, source_target_pairs={{1,0},{2,3},{5,4},{6,7},{9,8},{10,11},{13,12},{14,15},{17,16},{18,... | collective-permute-start | bytes 2359304 | tf_op jit(solution)/shard_map/ppermute | solution.py:296
  283.5 94.6 %collective-permute-start.24 = (bf16[192,2176]{1,0:T(8,128)(2,1)}, bf16[192,2176]{1,0:T(8,128)(2,1)S(1)}, u32[]{:S(2)}, u32[]{:S(2)}) collective-permute-start(bf16[192,2176]{1,0:T(8,128)(2,1)} %partial_product.3), channel_id=1, source_target_pairs={{1,0},{2,3},{5,4},{6,7},{9,8},{10,11},{13,12},{14,15},{17,16},{18,... | collective-permute-start | bytes 2506760 | tf_op jit(solution)/shard_map/ppermute | solution.py:296
  (28 other events, 437.3 us)

commit v3 on v0

v3 whole, which is shorter than its diff:
```python
import jax
import jax.numpy as jnp
from jax import lax
from jax.experimental import pallas as pl
from jax.experimental.pallas import tpu as pltpu
from jax.sharding import PartitionSpec as P

adapter_scale = 2.0
lanes = 128
vmem = 48 * 1024 * 1024
f32 = jnp.float32
bf16 = jnp.bfloat16


def plain(
    layer_input,
    input_norm_weight,
    query_base_matrix,
    adapter_down_weight,
    adapter_up_weight,
    token_adapter_index,
):
    xf = layer_input.astype(f32)
    ms = jnp.mean(xf * xf, axis=-1, keepdims=True)
    normed = (xf * lax.rsqrt(ms + 1e-05) * input_norm_weight.astype(f32)).astype(bf16)
    gathered = lax.all_gather(normed, "tensor", axis=0, tiled=True)
    down_all = lax.all_gather(adapter_down_weight, "replica", axis=0, tiled=True)
    up_all = lax.all_gather(adapter_up_weight, "replica", axis=0, tiled=True)
    count, width, rank = down_all.shape
    down_cat = jnp.transpose(down_all, (1, 0, 2)).reshape(width, count * rank)
    low_all = jnp.dot(gathered, down_cat, preferred_element_type=f32)
    owner = jnp.repeat(jnp.arange(count, dtype=jnp.int32), rank)
    chosen = token_adapter_index[:, None] == owner[None, :]
    masked = jnp.where(chosen, low_all, 0.0).astype(bf16)
    update = jnp.dot(
        masked, up_all.reshape(count * rank, up_all.shape[2]), preferred_element_type=f32
    )
    base = jnp.dot(gathered, query_base_matrix, preferred_element_type=f32)
    return (base + adapter_scale * update).astype(bf16)


def norm_chunks(x, gain, spans):
    rows, width = x.shape
    block = 48

    def kernel(x_ref, g_ref, *out_refs):
        xf = x_ref[...].astype(f32)
        ms = jnp.mean(xf * xf, axis=-1, keepdims=True)
        y = (xf * lax.rsqrt(ms + 1e-05) * g_ref[...].astype(f32)).astype(bf16)
        for (lo, hi), out_ref in zip(spans, out_refs):
            out_ref[...] = y[:, lo:hi]

    return pl.pallas_call(
        kernel,
        grid=(rows // block,),
        in_specs=[
            pl.BlockSpec((block, width), lambda i: (i, 0)),
            pl.BlockSpec((1, width), lambda i: (0, 0)),
        ],
        out_specs=[pl.BlockSpec((block, hi - lo), lambda i: (i, 0)) for lo, hi in spans],
        out_shape=[jax.ShapeDtypeStruct((rows, hi - lo), bf16) for lo, hi in spans],
        compiler_params=pltpu.CompilerParams(vmem_limit_bytes=vmem),
        cost_estimate=pl.CostEstimate(flops=1000, bytes_accessed=1000, transcendentals=0),
        name="norm_chunks",
    )(x, gain)


def dot_t(a, b):
    return lax.dot_general(a, b, (((1,), (1,)), ((), ())), preferred_element_type=f32)


def after(x, *others):
    return lax.optimization_barrier((x, *others))[0]


def constant(shape):
    return pl.BlockSpec(shape, lambda *_: (0, 0), pipeline_mode=pl.Buffered(1))


def product(pieces, rows, depth, weight, pool=None, choose=None):
    features = weight.shape[1]
    pool_rows = 0 if pool is None else pool.shape[0]
    tile = 256
    tiles = features // tile
    whole = lambda a: a if isinstance(a, tuple) else (a, 0, a.shape[1])
    pieces = [(r, f, [whole(a) for a in arrays]) for r, f, arrays in pieces]
    flat = []
    for _, _, arrays in pieces:
        flat += [a for a, _, _ in arrays if not any(a is b for b in flat)]

    def kernel(*refs):
        refs = list(refs)
        x_refs = [refs.pop(0) for _ in flat]
        w_ref = refs.pop(0)
        if pool is not None:
            down_ref = refs.pop(0)
        if choose is not None:
            owner_ref, ids_ref = refs.pop(0), refs.pop(0)
        if pool is not None:
            sem, held = refs.pop(), refs.pop()
            fetch = pltpu.make_async_copy(down_ref.at[:, pl.ds(0, depth)], held, sem)
        xs = refs.pop()
        out_ref = refs.pop(0)
        n = pl.program_id(0)

        @pl.when(n == 0)
        def _():
            for row, feature, arrays in pieces:
                x = None
                for a, lo, hi in arrays:
                    (at,) = [i for i, b in enumerate(flat) if a is b]
                    y = x_refs[at][:, lo:hi]
                    x = y if x is None else x + y
                xs[row : row + x.shape[0], feature : feature + x.shape[1]] = x
            if pool is not None:
                fetch.start()

        p = jnp.dot(xs[...], w_ref[...], preferred_element_type=f32)
        if choose is None:
            out_ref[...] = p
        else:
            out_ref[:, pl.ds(pl.multiple_of(n * tile, tile), tile)] = p.astype(bf16)

        if pool is not None:

            @pl.when(n == tiles - 1)
            def _():
                fetch.wait()
                low = dot_t(xs[...], held[...])
                if choose is None:
                    refs[0][...] = low
                else:
                    low = jnp.where(ids_ref[...] == owner_ref[...], low, 0.0)
                    chosen = low[:, :lanes]
                    for j in range(1, pool_rows // lanes):
                        chosen = chosen + low[:, j * lanes : (j + 1) * lanes]
                    out_ref[:, features:] = chosen.astype(bf16)

    in_specs = [constant(a.shape) for a in flat]
    in_specs += [pl.BlockSpec((depth, tile), lambda n: (0, n))]
    operands = flat + [weight]
    if pool is not None:
        in_specs.append(pl.BlockSpec(memory_space=pl.ANY))
        operands.append(pool)
    if pool is None:
        out_shape = jax.ShapeDtypeStruct((rows, features), f32)
        out_specs = pl.BlockSpec((rows, tile), lambda n: (0, n))
    elif choose is None:
        out_shape = [
            jax.ShapeDtypeStruct((rows, features), f32),
            jax.ShapeDtypeStruct((rows, pool_rows), f32),
        ]
        out_specs = [
            pl.BlockSpec((rows, tile), lambda n: (0, n)),
            pl.BlockSpec((rows, pool_rows), lambda n: (0, 0)),
        ]
    else:
        owner, ids = choose
        in_specs += [constant((1, pool_rows)), constant((rows, 1))]
        operands += [owner, ids]
        out_shape = jax.ShapeDtypeStruct((rows, features + lanes), bf16)
        out_specs = pl.BlockSpec((rows, features + lanes), lambda n: (0, 0))
    scratch = [pltpu.VMEM((rows, depth), bf16)]
    if pool is not None:
        scratch += [pltpu.VMEM((pool_rows, depth), bf16), pltpu.SemaphoreType.DMA(())]
    return pl.pallas_call(
        kernel,
        grid=(tiles,),
        in_specs=in_specs,
        out_specs=out_specs,
        out_shape=out_shape,
        scratch_shapes=scratch,
        compiler_params=pltpu.CompilerParams(vmem_limit_bytes=vmem),
        cost_estimate=pl.CostEstimate(flops=1000, bytes_accessed=1000, transcendentals=0),
        name="product" if choose is None else "product_sent",
    )(*operands)


def finish(acc, low, at, partial, part_at, pool, width, owner, ids, row, rows, prev):
    features = acc.shape[1]
    pool_rows = pool.shape[0]
    tile = 512
    tiles = features // tile

    def kernel(row_ref, *refs):
        refs = list(refs)
        acc_ref, low_ref, up_ref, owner_ref, ids_ref = [refs.pop(0) for _ in range(5)]
        if partial is not None:
            part_ref, sent_ref = refs.pop(0), refs.pop(0)
        if prev is not None:
            refs.pop(0)
        (out_ref,) = refs
        total = low_ref[...]
        y = acc_ref[...]
        if partial is not None:
            sent = sent_ref[...].astype(f32)
            total = total + jnp.concatenate([sent] * (pool_rows // lanes), axis=1)
            y = y + part_ref[...].astype(f32)
        mask = jnp.where(ids_ref[...] == owner_ref[...], total, 0.0).astype(bf16)
        y = y + adapter_scale * jnp.dot(mask, up_ref[...], preferred_element_type=f32)
        out_ref[...] = y.astype(bf16)

    in_specs = [
        pl.BlockSpec((rows, tile), lambda n, r: (at, n)),
        pl.BlockSpec((rows, pool_rows), lambda n, r: (at, 0)),
        pl.BlockSpec((pool_rows, tile), lambda n, r: (0, width // tile + n)),
        pl.BlockSpec((1, pool_rows), lambda n, r: (0, 0)),
        pl.BlockSpec((rows, 1), lambda n, r: (r[0], 0)),
    ]
    operands = [acc, low, pool, owner, ids]
    if partial is not None:
        in_specs += [
            pl.BlockSpec((rows, tile), lambda n, r: (part_at, n)),
            pl.BlockSpec((rows, lanes), lambda n, r: (part_at, features // lanes)),
        ]
        operands += [partial, partial]
    aliases = {}
    if prev is not None:
        in_specs.append(pl.BlockSpec(memory_space=pl.ANY))
        operands.append(prev)
        aliases = {len(operands): 0}
    return pl.pallas_call(
        kernel,
        grid_spec=pltpu.PrefetchScalarGridSpec(
            num_scalar_prefetch=1,
            grid=(tiles,),
            in_specs=in_specs,
            out_specs=pl.BlockSpec((rows, tile), lambda n, r: (r[0], n)),
        ),
        out_shape=jax.ShapeDtypeStruct((ids.shape[0], features), bf16),
        input_output_aliases=aliases,
        compiler_params=pltpu.CompilerParams(vmem_limit_bytes=vmem),
        cost_estimate=pl.CostEstimate(flops=1000, bytes_accessed=1000, transcendentals=0),
        name="finish",
    )(row.reshape(1), *operands)


def body(
    layer_input,
    input_norm_weight,
    query_base_matrix,
    adapter_down_weight,
    adapter_up_weight,
    token_adapter_index,
):
    rows, width = layer_input.shape
    count = lax.axis_size("replica")
    rank = adapter_down_weight.shape[2]
    t = lax.axis_index("tensor").astype(jnp.int32)
    q = lax.axis_index("groups") * count + lax.axis_index("replica")
    inward = lambda a: lax.ppermute(a, "tensor", [(0, 1), (3, 2)])
    outward = lambda a: lax.ppermute(a, "tensor", [(1, 0), (2, 3)])
    cross = lambda a: lax.ppermute(a, "tensor", [(1, 2), (2, 1)])

    h = width * 7 // 16
    m = (width + h) // 2
    piece = h // (count * lax.axis_size("groups"))
    share = lax.dynamic_slice_in_dim(query_base_matrix, q * piece, piece, 0)
    sent = inward(share)
    layer_input = after(layer_input, share)
    adapter_down_weight = after(adapter_down_weight, share)

    pool = jnp.concatenate([adapter_down_weight[0].T, adapter_up_weight[0]], axis=1)
    pool = lax.all_gather(pool, "replica", axis=0, tiled=True)
    owner = jnp.repeat(jnp.arange(count, dtype=jnp.int32), rank)[None, :]
    ids = token_adapter_index[:, None]

    own_h, own_d, own_d0, own_d1 = norm_chunks(
        layer_input, input_norm_weight[None, :], [(0, h), (h, width), (h, m), (m, width)]
    )
    w = query_base_matrix
    own = product([(0, 0, [own_h]), (0, h, [own_d])], rows, width, w)
    out_own = outward(own_d)
    mid_d = cross(own_d)
    end_d0 = inward(after(own_d0, sent))
    out_mid = outward(after(mid_d, out_own))
    mid_h = cross(after(own_h, mid_d, own))
    mid_row = jnp.where(t < 2, 2, 1).astype(jnp.int32)
    far_row = jnp.where(t < 2, 3, 0).astype(jnp.int32)
    last = (pool, width, owner, ids)
    own_low = dot_t(own_h, pool[:, :h]) + dot_t(own_d, pool[:, h:width])
    out = finish(own, own_low, 0, None, 0, *last, t, rows, None)
    end_d1 = inward(after(own_d1, end_d0, out))
    far_d0 = cross(after(end_d0, mid_h))
    end_h = inward(after(own_h, end_d1))
    out_far0 = outward(after(far_d0, out_mid))
    far_d1 = cross(after(end_d1, far_d0))
    mid = product(
        [(0, 0, [mid_h]), (0, h, [after(mid_d, far_d0), out_mid])], rows, width, w, pool
    )
    out_far1 = outward(after(far_d1, out_far0, mid[0]))
    far_h = cross(after(end_h, far_d1))
    sent = after(sent, mid_d, out_own, own)
    help_weight = lax.all_gather(sent, ("groups", "replica"), axis=0, tiled=True)

    pick = lambda row: lax.dynamic_slice_in_dim(ids, row * rows, rows, 0)
    ids_near = jnp.concatenate([pick(t), pick(mid_row)], axis=0)
    part_near = product(
        [(0, 0, [own_h]), (rows, 0, [mid_h])], 2 * rows, h, help_weight, pool,
        (owner, ids_near),
    )
    far_h = after(far_h, part_near)
    part_near = outward(after(part_near, out_far1))
    part_far = product([(0, 0, [far_h])], rows, h, help_weight, pool, (owner, pick(far_row)))
    far_h = after(far_h, part_far)
    part_far = outward(part_far)
    cut = m - h
    distant = product(
        [
            (0, 0, [end_h]),
            (0, h, [end_d0, (out_own, 0, cut)]),
            (0, m, [end_d1, (out_own, cut, width - h)]),
            (rows, 0, [far_h]),
            (rows, h, [far_d0, out_far0]),
            (rows, m, [far_d1, out_far1]),
        ],
        2 * rows, width, w, pool,
    )
    out = finish(*mid, 0, part_near, 1, *last, mid_row, rows, out)
    out = finish(*distant, 0, part_near, 0, *last, t ^ 1, rows, out)
    return finish(*distant, 1, part_far, 0, *last, far_row, rows, out)


def solution(mesh):
    placed = (
        P(("groups", "replica", "tensor"), None),
        P(),
        P(None, "tensor"),
        P("replica", None, None),
        P("replica", None, "tensor"),
        P(("groups", "replica")),
    )
    line = mesh.shape["tensor"] == 4 and mesh.shape["replica"] == 4 and mesh.shape["groups"] == 2
    return jax.shard_map(
        body if line else plain,
        mesh=mesh,
        in_specs=placed,
        out_specs=P(("groups", "replica"), "tensor"),
        check_vma=False,
    )
```

time: 312 us -> 238 us (0.76)
  the two profiles are of different devices: /device:TPU:0 before, /device:TPU:12 now
where the time goes in v3:
time: 238 us; the launch traced here: 236 us
  Pallas kernels  101 us (42%)
  waiting for transfers between devices  58.1 us (24%)
  starting transfers between devices  38.1 us (16%)
  local copies, waits for them, and re-layouts  18.1 us (8%)
  between operations  13.8 us (6%)
  matrix products  5.91 us (2%)
    pallas_call x5, Pallas kernels, product(): pl.pallas_call(kernel, grid=(tiles,), in_specs=in_specs, out_specs=out_sp...  81.4 us
    ppermute x5, waiting for transfers between devices, body(): cross = lambda a: lax.ppermute(a, 'tensor', [(1, 2), (2, 1)])  42 us
    ppermute x6, starting transfers between devices, body(): outward = lambda a: lax.ppermute(a, 'tensor', [(1, 0), (2, 3)])  16.6 us
    ppermute x5, starting transfers between devices, body(): cross = lambda a: lax.ppermute(a, 'tensor', [(1, 2), (2, 1)])  16.3 us
    pallas_call x4, Pallas kernels, finish(): pl.pallas_call(kernel, grid_spec=pltpu.PrefetchScalarGridSpec(num_scalar_...  15.8 us
    ppermute x4, waiting for transfers between devices, body(): inward = lambda a: lax.ppermute(a, 'tensor', [(0, 1), (3, 2)])  14.2 us
    unnamed x54, local copies, waits for them, and re-layouts  13.7 us
    dot_general x2, matrix products, dot_t(): lax.dot_general(a, b, (((1,), (1,)), ((), ())), preferred_element_type=f32)  5.91 us
  transfers between devices with their start and end apart: 17, of which 7 were waited for; matrix products, arithmetic and copies ran while one was open for 3% of the time, Pallas kernels for 41%

profile of v3, /device:TPU:12, one launch (start us, length us, event | category | flops | bytes accessed | tf_op | source)
XLA Modules:
  0.0 236.4 jit_solution(12451760965121013877)
XLA Ops:
  6.5 3.0 %constant_dynamic-slice_fusion = bf16[448,2048]{1,0:T(8,128)(2,1)} fusion(bf16[8192,2048]{1,0:T(8,128)(2,1)} %refs_9_.1, s32[]{:T(128)S(6)} %select_n.20), kind=kLoop, calls=%fused_computation.7 | loop fusion | bytes 3670020 | tf_op jit(solution)/shard_map/dynamic_slice | solution.py:258
  10.8 1.3 collective-permute-start
  12.1 3.9 %norm_chunks.1 = (bf16[192,3584]{1,0:T(8,128)(2,1)S(1)}, bf16[192,4608]{1,0:T(8,128)(2,1)S(1)}, bf16[192,2304]{1,0:T(8,128)(2,1)S(1)}, bf16[192,2304]{1,0:T(8,128)(2,1)S(1)}) custom-call(bf16[192,8192]{1,0:T(8,128)(2,1)} %x_ref, bf16[1,8192]{1,0:T(2,128)(2,1)S(1)} %broadcast_in_dim.19.g_ref), custom_call_target="tpu_custom_call" | custom-call | flops 1000 | bytes 1000 | tf_op jit(solution)/shard_map/norm_chunks/pallas_call | solution.py:53
  18.0 3.5 %collective-permute-start.5 = (bf16[192,4608]{1,0:T(8,128)(2,1)S(1)}, bf16[192,4608]{1,0:T(8,128)(2,1)S(1)}, u32[]{:S(2)}, u32[]{:S(2)}) collective-permute-start(bf16[192,4608]{1,0:T(8,128)(2,1)S(1)} %get-tuple-element.35.refs_1_), channel_id=1, source_target_pairs={{1,2},{2,1},{5,6},{6,5},{9,10},{10,9},{13,14},{14,13},{17,18},{18,... | collective-permute-start | bytes 5308424 | tf_op jit(solution)/shard_map/ppermute | solution.py:253
  21.5 3.3 %collective-permute-start.4 = (bf16[192,4608]{1,0:T(8,128)(2,1)S(1)}, bf16[192,4608]{1,0:T(8,128)(2,1)S(1)}, u32[]{:S(2)}, u32[]{:S(2)}) collective-permute-start(bf16[192,4608]{1,0:T(8,128)(2,1)S(1)} %get-tuple-element.35.refs_1_), channel_id=1, source_target_pairs={{1,0},{2,3},{5,4},{6,7},{9,8},{10,11},{13,12},{14,15},{17,16},{18,... | collective-permute-start | bytes 5308424 | tf_op jit(solution)/shard_map/ppermute | solution.py:252
  24.8 15.0 %product.3.refs_0_ = f32[192,2048]{1,0:T(8,128)S(1)} custom-call(bf16[192,3584]{1,0:T(8,128)(2,1)S(1)} %get-tuple-element.39.refs_0_, bf16[192,4608]{1,0:T(8,128)(2,1)S(1)} %get-tuple-element.35.refs_1_, bf16[8192,2048]{1,0:T(8,128)(2,1)} %refs_9_.1), custom_call_target="tpu_custom_call" | custom-call | flops 1000 | bytes 1000 | tf_op jit(solution)/shard_map/product/pallas_call | solution.py:166
  39.8 20.5 %collective-permute-done.5.refs_1_ = bf16[192,4608]{1,0:T(8,128)(2,1)S(1)} collective-permute-done((bf16[192,4608]{1,0:T(8,128)(2,1)S(1)}, bf16[192,4608]{1,0:T(8,128)(2,1)S(1)}, u32[]{:S(2)}, u32[]{:S(2)}) %collective-permute-start.5) | collective-permute-done | bytes 1769504 | tf_op jit(solution)/shard_map/ppermute | solution.py:253
  60.2 2.0 collective-permute-done.4.refs_2_
  63.4 3.4 %collective-permute-start.6 = (bf16[192,3584]{1,0:T(8,128)(2,1)S(1)}, bf16[192,3584]{1,0:T(8,128)(2,1)}, u32[]{:S(2)}, u32[]{:S(2)}) collective-permute-start(bf16[192,3584]{1,0:T(8,128)(2,1)S(1)} %get-tuple-element.39.refs_0_), channel_id=1, source_target_pairs={{1,2},{2,1},{5,6},{6,5},{9,10},{10,9},{13,14},{14,13},{17,18},{18,... | collective-permute-start | bytes 4128776 | tf_op jit(solution)/shard_map/ppermute | solution.py:253
  68.2 6.7 %collective-permute-start.10 = (bf16[192,4608]{1,0:T(8,128)(2,1)}, bf16[192,4608]{1,0:T(8,128)(2,1)}, u32[]{:S(2)}, u32[]{:S(2)}) collective-permute-start(bf16[192,4608]{1,0:T(8,128)(2,1)} %copy-done.2), channel_id=1, source_target_pairs={{1,0},{2,3},{5,4},{6,7},{9,8},{10,11},{13,12},{14,15},{17,16},{18,... | collective-permute-start | bytes 5308424 | tf_op jit(solution)/shard_map/ppermute | solution.py:252
  75.2 3.7 %fusion = f32[192,256]{1,0:T(8,128)S(1)} fusion(bf16[192,4608]{1,0:T(8,128)(2,1)} %copy-done.1, bf16[256,10240]{1,0:T(8,128)(2,1)} %all-gather.3.cloned.1.call-done.refs_2_.refs_3_.refs_4_.refs_10_), kind=kOutput, calls=%fused_computation | convolution fusion | flops 452984832 | bytes 4325376 | tf_op jit(solution)/shard_map/dot_general | solution.py:69
  78.9 2.2 fusion.4.refs_1_
  81.1 4.0 %finish.4.refs_7_ = bf16[768,2048]{1,0:T(8,128)(2,1)} custom-call(s32[1]{0:T(128)} %bitcast.1.row_ref, f32[192,2048]{1,0:T(8,128)S(1)} %product.3.refs_0_, f32[192,256]{1,0:T(8,128)S(1)} %fusion.4.refs_1_, bf16[256,10240]{1,0:T(8,128)(2,1)} %all-gather.3.cloned.1.call-done.refs_2_.refs_3_.refs_4_.refs_10_, ...), custom_call_target="tpu_custom_call" | custom-call | flops 1000 | bytes 1000 | tf_op jit(solution)/shard_map/finish/pallas_call | solution.py:222
  85.1 3.9 %collective-permute-done.1.refs_1_ = bf16[192,2304]{1,0:T(8,128)(2,1)} collective-permute-done((bf16[192,2304]{1,0:T(8,128)(2,1)}, bf16[192,2304]{1,0:T(8,128)(2,1)}, u32[]{:S(2)}, u32[]{:S(2)}) %collective-permute-start.1) | collective-permute-done | bytes 884768 | tf_op jit(solution)/shard_map/ppermute | solution.py:251
  90.3 5.8 %collective-permute-done.6.refs_1_.refs_0_ = bf16[192,3584]{1,0:T(8,128)(2,1)} collective-permute-done((bf16[192,3584]{1,0:T(8,128)(2,1)S(1)}, bf16[192,3584]{1,0:T(8,128)(2,1)}, u32[]{:S(2)}, u32[]{:S(2)}) %collective-permute-start.6) | collective-permute-done | bytes 1376288 | tf_op jit(solution)/shard_map/ppermute | solution.py:253
  96.1 3.5 %collective-permute-start.7 = (bf16[192,2304]{1,0:T(8,128)(2,1)}, bf16[192,2304]{1,0:T(8,128)(2,1)S(1)}, u32[]{:S(2)}, u32[]{:S(2)}) collective-permute-start(bf16[192,2304]{1,0:T(8,128)(2,1)} %collective-permute-done.1.refs_1_), channel_id=1, source_target_pairs={{1,2},{2,1},{5,6},{6,5},{9,10},{10,9},{13,14},{14,13},{17,18},{18,... | collective-permute-start | bytes 2654216 | tf_op jit(solution)/shard_map/ppermute | solution.py:253
  99.6 10.3 %collective-permute-done.2.refs_3_ = bf16[192,2304]{1,0:T(8,128)(2,1)S(1)} collective-permute-done((bf16[192,2304]{1,0:T(8,128)(2,1)S(1)}, bf16[192,2304]{1,0:T(8,128)(2,1)S(1)}, u32[]{:S(2)}, u32[]{:S(2)}) %collective-permute-start.2) | collective-permute-done | bytes 884768 | tf_op jit(solution)/shard_map/ppermute | solution.py:251
  111.2 6.2 %collective-permute-done.7.refs_5_ = bf16[192,2304]{1,0:T(8,128)(2,1)S(1)} collective-permute-done((bf16[192,2304]{1,0:T(8,128)(2,1)}, bf16[192,2304]{1,0:T(8,128)(2,1)S(1)}, u32[]{:S(2)}, u32[]{:S(2)}) %collective-permute-start.7) | collective-permute-done | bytes 884768 | tf_op jit(solution)/shard_map/ppermute | solution.py:253
  117.4 1.3 collective-permute-start.11
  118.8 3.5 %collective-permute-start.8 = (bf16[192,2304]{1,0:T(8,128)(2,1)S(1)}, bf16[192,2304]{1,0:T(8,128)(2,1)S(1)}, u32[]{:S(2)}, u32[]{:S(2)}) collective-permute-start(bf16[192,2304]{1,0:T(8,128)(2,1)S(1)} %collective-permute-done.2.refs_3_), channel_id=1, source_target_pairs={{1,2},{2,1},{5,6},{6,5},{9,10},{10,9},{13,14},{14,13},{17,18},{18,... | collective-permute-start | bytes 2654216 | tf_op jit(solution)/shard_map/ppermute | solution.py:253
  122.3 18.0 %product.4 = (f32[192,2048]{1,0:T(8,128)S(1)}, f32[192,256]{1,0:T(8,128)S(1)}) custom-call(bf16[192,3584]{1,0:T(8,128)(2,1)} %collective-permute-done.6.refs_1_.refs_0_, bf16[192,4608]{1,0:T(8,128)(2,1)S(1)} %copy-done.3, bf16[192,4608]{1,0:T(8,128)(2,1)} %collective-permute-done.10.refs_2_, bf16[8192,2048]{1,0:T(8,128)(2,1)} %refs_9_.1, ...), custom_call_target="tpu_custom_call" | custom-call | flops 1000 | bytes 1000 | tf_op jit(solution)/shard_map/product/pallas_call | solution.py:166
  143.3 1.3 collective-permute-start.12
  144.6 2.3 collective-permute-start.9
  148.9 13.6 %product_sent.2 = bf16[384,2176]{1,0:T(8,128)(2,1)} custom-call(bf16[192,3584]{1,0:T(8,128)(2,1)S(1)} %get-tuple-element.39.refs_0_, bf16[192,3584]{1,0:T(8,128)(2,1)} %collective-permute-done.6.refs_1_.refs_0_, bf16[3584,2048]{1,0:T(8,128)(2,1)} %all-gather.5.cloned.1.call-done.refs_2_.refs_1_, ...), custom_call_target="tpu_custom_call" | custom-call | flops 1000 | bytes 1000 | tf_op jit(solution)/shard_map/product_sent/pallas_call | solution.py:166
  163.5 2.4 %collective-permute-start.14 = (bf16[384,2176]{1,0:T(8,128)(2,1)}, bf16[384,2176]{1,0:T(8,128)(2,1)S(1)}, u32[]{:S(2)}, u32[]{:S(2)}) collective-permute-start(bf16[384,2176]{1,0:T(8,128)(2,1)} %product_sent.2), channel_id=1, source_target_pairs={{1,0},{2,3},{5,4},{6,7},{9,8},{10,11},{13,12},{14,15},{17,16},{18,... | collective-permute-start | bytes 5013512 | tf_op jit(solution)/shard_map/ppermute | solution.py:252
  166.1 9.5 %collective-permute-done.9.refs_0_.refs_4_ = bf16[192,3584]{1,0:T(8,128)(2,1)} collective-permute-done((bf16[192,3584]{1,0:T(8,128)(2,1)}, bf16[192,3584]{1,0:T(8,128)(2,1)}, u32[]{:S(2)}, u32[]{:S(2)}) %collective-permute-start.9) | collective-permute-done | bytes 1376288 | tf_op jit(solution)/shard_map/ppermute | solution.py:253
  175.5 11.4 %product_sent.3 = bf16[192,2176]{1,0:T(8,128)(2,1)} custom-call(bf16[192,3584]{1,0:T(8,128)(2,1)} %collective-permute-done.9.refs_0_.refs_4_, bf16[3584,2048]{1,0:T(8,128)(2,1)} %all-gather.5.cloned.1.call-done.refs_2_.refs_1_, bf16[256,10240]{1,0:T(8,128)(2,1)} %all-gather.3.cloned.1.call-done.refs_2_.refs_3_.refs_4_.refs_10_, ...), custom_call_target="tpu_custom_call" | custom-call | flops 1000 | bytes 1000 | tf_op jit(solution)/shard_map/product_sent/pallas_call | solution.py:166
  186.9 1.5 collective-permute-start.13
  194.3 23.5 %product.5 = (f32[384,2048]{1,0:T(8,128)}, f32[384,256]{1,0:T(8,128)S(1)}) custom-call(bf16[192,3584]{1,0:T(8,128)(2,1)} %collective-permute-done.3.refs_0_, bf16[192,2304]{1,0:T(8,128)(2,1)} %collective-permute-done.1.refs_1_, bf16[192,4608]{1,0:T(8,128)(2,1)} %copy-done.22, bf16[192,2304]{1,0:T(8,128)(2,1)S(1)} %copy-done.7, ...), custom_call_target="tpu_custom_call" | custom-call | flops 1000 | bytes 1000 | tf_op jit(solution)/shard_map/product/pallas_call | solution.py:166
  217.8 4.0 %finish.5.refs_7_ = bf16[768,2048]{1,0:T(8,128)(2,1)} custom-call(s32[1]{0:T(128)} %bitcast.9.row_ref, f32[192,2048]{1,0:T(8,128)S(1)} %copy-done.5, f32[192,256]{1,0:T(8,128)S(1)} %copy-done.18, bf16[256,10240]{1,0:T(8,128)(2,1)} %all-gather.3.cloned.1.call-done.refs_2_.refs_3_.refs_4_.refs_10_, ...), custom_call_target="tpu_custom_call", output_to_operand_aliasing={{}: (8, {})} | custom-call | flops 1000 | bytes 1000 | tf_op jit(solution)/shard_map/finish/pallas_call | solution.py:222
  221.8 3.9 %finish.6.refs_7_ = bf16[768,2048]{1,0:T(8,128)(2,1)} custom-call(s32[1]{0:T(128)} %bitcast.8.row_ref, f32[384,2048]{1,0:T(8,128)S(1)} %copy-done, f32[384,256]{1,0:T(8,128)S(1)} %get-tuple-element.52.refs_1_, bf16[256,10240]{1,0:T(8,128)(2,1)} %all-gather.3.cloned.1.call-done.refs_2_.refs_3_.refs_4_.refs_10_, ...), custom_call_target="tpu_custom_call", output_to_operand_aliasing={{}: (8, {})} | custom-call | flops 1000 | bytes 1000 | tf_op jit(solution)/shard_map/finish/pallas_call | solution.py:222
  225.7 3.8 %finish.7 = bf16[768,2048]{1,0:T(8,128)(2,1)} custom-call(s32[1]{0:T(128)} %bitcast.row_ref, f32[384,2048]{1,0:T(8,128)S(1)} %copy-done, f32[384,256]{1,0:T(8,128)S(1)} %get-tuple-element.52.refs_1_, bf16[256,10240]{1,0:T(8,128)(2,1)} %all-gather.3.cloned.1.call-done.refs_2_.refs_3_.refs_4_.refs_10_, ...), custom_call_target="tpu_custom_call", output_to_operand_aliasing={{}: (8, {})} | custom-call | flops 1000 | bytes 1000 | tf_op jit(solution)/shard_map/finish/pallas_call | solution.py:222
  (80 shorter events, 20.2 us)
Async XLA Ops:
  6.5 68.6 %all-gather.3.cloned.1.call-start = ((), (), s32[]{:S(2)}) async-start(), calls=%async_computation | async-start | bytes 6553600 | tf_op jit(solution)/shard_map/all_gather | solution.py:264
  6.5 3.0 %copy-start.23 = (bf16[1,8192,64]{1,2,0:T(8,128)(2,1)S(1)}, bf16[1,8192,64]{1,2,0:T(8,128)(2,1)}, u32[]{:S(2)}) copy-start(bf16[1,8192,64]{1,2,0:T(8,128)(2,1)} %param.9) | copy-start | bytes 3145732
  6.5 3.0 %copy-start.24 = (bf16[1,64,2048]{2,1,0:T(8,128)(2,1)S(1)}, bf16[1,64,2048]{2,1,0:T(8,128)(2,1)}, u32[]{:S(2)}) copy-start(bf16[1,64,2048]{2,1,0:T(8,128)(2,1)} %param.10) | copy-start | bytes 786436
  9.6 2.5 %copy-start.25 = (bf16[8192]{0:T(1024)(128)(2,1)S(1)}, bf16[8192]{0:T(1024)(128)(2,1)}, u32[]{:S(2)}) copy-start(bf16[8192]{0:T(1024)(128)(2,1)} %param.7) | copy-start | bytes 49156
  10.8 137.2 %all-gather.5.cloned.1.call-start = ((), (), s32[]{:S(2)}) async-start(), calls=%async_computation.1 | async-start | bytes 16515072 | tf_op jit(solution)/shard_map/all_gather | solution.py:294
  10.8 52.6 %collective-permute-start = (bf16[448,2048]{1,0:T(8,128)(2,1)}, bf16[448,2048]{1,0:T(8,128)(2,1)}, u32[]{:S(2)}, u32[]{:S(2)}) collective-permute-start(bf16[448,2048]{1,0:T(8,128)(2,1)} %constant_dynamic-slice_fusion), channel_id=1, source_target_pairs={{0,1},{3,2},{4,5},{7,6},{8,9},{11,10},{12,13},{15,14},{16,17},{19,... | collective-permute-start | bytes 5505032 | tf_op jit(solution)/shard_map/ppermute | solution.py:251
  18.0 21.7 %copy-start.1 = (bf16[192,4608]{1,0:T(8,128)(2,1)}, bf16[192,4608]{1,0:T(8,128)(2,1)S(1)}, u32[]{:S(2)}) copy-start(bf16[192,4608]{1,0:T(8,128)(2,1)S(1)} %get-tuple-element.35.refs_1_) | copy-start | bytes 5308420
  18.0 42.2 %collective-permute-start.5 = (bf16[192,4608]{1,0:T(8,128)(2,1)S(1)}, bf16[192,4608]{1,0:T(8,128)(2,1)S(1)}, u32[]{:S(2)}, u32[]{:S(2)}) collective-permute-start(bf16[192,4608]{1,0:T(8,128)(2,1)S(1)} %get-tuple-element.35.refs_1_), channel_id=1, source_target_pairs={{1,2},{2,1},{5,6},{6,5},{9,10},{10,9},{13,14},{14,13},{17,18},{18,... | collective-permute-start | bytes 5308424 | tf_op jit(solution)/shard_map/ppermute | solution.py:253
  21.5 40.7 %collective-permute-start.4 = (bf16[192,4608]{1,0:T(8,128)(2,1)S(1)}, bf16[192,4608]{1,0:T(8,128)(2,1)S(1)}, u32[]{:S(2)}, u32[]{:S(2)}) collective-permute-start(bf16[192,4608]{1,0:T(8,128)(2,1)S(1)} %get-tuple-element.35.refs_1_), channel_id=1, source_target_pairs={{1,0},{2,3},{5,4},{6,7},{9,8},{10,11},{13,12},{14,15},{17,16},{18,... | collective-permute-start | bytes 5308424 | tf_op jit(solution)/shard_map/ppermute | solution.py:252
  39.7 35.2 %copy-start.26 = (s32[768]{0:T(1024)S(1)}, s32[768]{0:T(1024)}, u32[]{:S(2)}) copy-start(s32[768]{0:T(1024)} %param.11) | copy-start | bytes 9220
  60.2 2.0 copy-start.2
  63.4 32.7 %collective-permute-start.6 = (bf16[192,3584]{1,0:T(8,128)(2,1)S(1)}, bf16[192,3584]{1,0:T(8,128)(2,1)}, u32[]{:S(2)}, u32[]{:S(2)}) collective-permute-start(bf16[192,3584]{1,0:T(8,128)(2,1)S(1)} %get-tuple-element.39.refs_0_), channel_id=1, source_target_pairs={{1,2},{2,1},{5,6},{6,5},{9,10},{10,9},{13,14},{14,13},{17,18},{18,... | collective-permute-start | bytes 4128776 | tf_op jit(solution)/shard_map/ppermute | solution.py:253
  66.9 22.1 %collective-permute-start.1 = (bf16[192,2304]{1,0:T(8,128)(2,1)}, bf16[192,2304]{1,0:T(8,128)(2,1)}, u32[]{:S(2)}, u32[]{:S(2)}) collective-permute-start(bf16[192,2304]{1,0:T(8,128)(2,1)} %copy-done.21), channel_id=1, source_target_pairs={{0,1},{3,2},{4,5},{7,6},{8,9},{11,10},{12,13},{15,14},{16,17},{19,... | collective-permute-start | bytes 2654216 | tf_op jit(solution)/shard_map/ppermute | solution.py:251
  68.2 43.0 %collective-permute-start.10 = (bf16[192,4608]{1,0:T(8,128)(2,1)}, bf16[192,4608]{1,0:T(8,128)(2,1)}, u32[]{:S(2)}, u32[]{:S(2)}) collective-permute-start(bf16[192,4608]{1,0:T(8,128)(2,1)} %copy-done.2), channel_id=1, source_target_pairs={{1,0},{2,3},{5,4},{6,7},{9,8},{10,11},{13,12},{14,15},{17,16},{18,... | collective-permute-start | bytes 5308424 | tf_op jit(solution)/shard_map/ppermute | solution.py:252
  81.1 7.9 %copy-start.20 = (bf16[192,2304]{1,0:T(8,128)(2,1)S(1)}, bf16[192,2304]{1,0:T(8,128)(2,1)}, u32[]{:S(2)}) copy-start(bf16[192,2304]{1,0:T(8,128)(2,1)} %copy-done.19) | copy-start | bytes 2654212
  81.1 41.2 %copy-start.3 = (bf16[192,4608]{1,0:T(8,128)(2,1)S(1)}, bf16[192,4608]{1,0:T(8,128)(2,1)}, u32[]{:S(2)}) copy-start(bf16[192,4608]{1,0:T(8,128)(2,1)} %copy-done.2) | copy-start | bytes 5308420
  89.0 20.9 %collective-permute-start.2 = (bf16[192,2304]{1,0:T(8,128)(2,1)S(1)}, bf16[192,2304]{1,0:T(8,128)(2,1)S(1)}, u32[]{:S(2)}, u32[]{:S(2)}) collective-permute-start(bf16[192,2304]{1,0:T(8,128)(2,1)S(1)} %copy-done.20), channel_id=1, source_target_pairs={{0,1},{3,2},{4,5},{7,6},{8,9},{11,10},{12,13},{15,14},{16,17},{19,... | collective-permute-start | bytes 2654216 | tf_op jit(solution)/shard_map/ppermute | solution.py:251
  96.1 21.3 %collective-permute-start.7 = (bf16[192,2304]{1,0:T(8,128)(2,1)}, bf16[192,2304]{1,0:T(8,128)(2,1)S(1)}, u32[]{:S(2)}, u32[]{:S(2)}) collective-permute-start(bf16[192,2304]{1,0:T(8,128)(2,1)} %collective-permute-done.1.refs_1_), channel_id=1, source_target_pairs={{1,2},{2,1},{5,6},{6,5},{9,10},{10,9},{13,14},{14,13},{17,18},{18,... | collective-permute-start | bytes 2654216 | tf_op jit(solution)/shard_map/ppermute | solution.py:253
  109.9 30.5 %copy-start.6 = (bf16[192,2304]{1,0:T(8,128)(2,1)}, bf16[192,2304]{1,0:T(8,128)(2,1)S(1)}, u32[]{:S(2)}) copy-start(bf16[192,2304]{1,0:T(8,128)(2,1)S(1)} %collective-permute-done.2.refs_3_) | copy-start | bytes 2654212
  109.9 34.7 %collective-permute-start.3 = (bf16[192,3584]{1,0:T(8,128)(2,1)S(1)}, bf16[192,3584]{1,0:T(8,128)(2,1)}, u32[]{:S(2)}, u32[]{:S(2)}) collective-permute-start(bf16[192,3584]{1,0:T(8,128)(2,1)S(1)} %get-tuple-element.39.refs_0_), channel_id=1, source_target_pairs={{0,1},{3,2},{4,5},{7,6},{8,9},{11,10},{12,13},{15,14},{16,17},{19,... | collective-permute-start | bytes 4128776 | tf_op jit(solution)/shard_map/ppermute | solution.py:251
  117.4 23.0 %copy-start.8 = (bf16[192,2304]{1,0:T(8,128)(2,1)}, bf16[192,2304]{1,0:T(8,128)(2,1)S(1)}, u32[]{:S(2)}) copy-start(bf16[192,2304]{1,0:T(8,128)(2,1)S(1)} %collective-permute-done.7.refs_5_) | copy-start | bytes 2654212
  117.4 24.9 %collective-permute-start.11 = (bf16[192,2304]{1,0:T(8,128)(2,1)S(1)}, bf16[192,2304]{1,0:T(8,128)(2,1)S(1)}, u32[]{:S(2)}, u32[]{:S(2)}) collective-permute-start(bf16[192,2304]{1,0:T(8,128)(2,1)S(1)} %collective-permute-done.7.refs_5_), channel_id=1, source_target_pairs={{1,0},{2,3},{5,4},{6,7},{9,8},{10,11},{13,12},{14,15},{17,16},{18,... | collective-permute-start | bytes 2654216 | tf_op jit(solution)/shard_map/ppermute | solution.py:252
  118.8 24.5 %collective-permute-start.8 = (bf16[192,2304]{1,0:T(8,128)(2,1)S(1)}, bf16[192,2304]{1,0:T(8,128)(2,1)S(1)}, u32[]{:S(2)}, u32[]{:S(2)}) collective-permute-start(bf16[192,2304]{1,0:T(8,128)(2,1)S(1)} %collective-permute-done.2.refs_3_), channel_id=1, source_target_pairs={{1,2},{2,1},{5,6},{6,5},{9,10},{10,9},{13,14},{14,13},{17,18},{18,... | collective-permute-start | bytes 2654216 | tf_op jit(solution)/shard_map/ppermute | solution.py:253
  140.4 1.2 copy-start.4
  143.3 19.2 %copy-start.12 = (bf16[192,2304]{1,0:T(8,128)(2,1)}, bf16[192,2304]{1,0:T(8,128)(2,1)S(1)}, u32[]{:S(2)}) copy-start(bf16[192,2304]{1,0:T(8,128)(2,1)S(1)} %collective-permute-done.8.refs_7_) | copy-start | bytes 2654212
  143.3 19.2 %collective-permute-start.12 = (bf16[192,2304]{1,0:T(8,128)(2,1)S(1)}, bf16[192,2304]{1,0:T(8,128)(2,1)S(1)}, u32[]{:S(2)}, u32[]{:S(2)}) collective-permute-start(bf16[192,2304]{1,0:T(8,128)(2,1)S(1)} %collective-permute-done.8.refs_7_), channel_id=1, source_target_pairs={{1,0},{2,3},{5,4},{6,7},{9,8},{10,11},{13,12},{14,15},{17,16},{18,... | collective-permute-start | bytes 2654216 | tf_op jit(solution)/shard_map/ppermute | solution.py:252
  144.6 30.9 %collective-permute-start.9 = (bf16[192,3584]{1,0:T(8,128)(2,1)}, bf16[192,3584]{1,0:T(8,128)(2,1)}, u32[]{:S(2)}, u32[]{:S(2)}) collective-permute-start(bf16[192,3584]{1,0:T(8,128)(2,1)} %collective-permute-done.3.refs_0_), channel_id=1, source_target_pairs={{1,2},{2,1},{5,6},{6,5},{9,10},{10,9},{13,14},{14,13},{17,18},{18,... | collective-permute-start | bytes 4128776 | tf_op jit(solution)/shard_map/ppermute | solution.py:253
  163.5 54.3 %collective-permute-start.14 = (bf16[384,2176]{1,0:T(8,128)(2,1)}, bf16[384,2176]{1,0:T(8,128)(2,1)S(1)}, u32[]{:S(2)}, u32[]{:S(2)}) collective-permute-start(bf16[384,2176]{1,0:T(8,128)(2,1)} %product_sent.2), channel_id=1, source_target_pairs={{1,0},{2,3},{5,4},{6,7},{9,8},{10,11},{13,12},{14,15},{17,16},{18,... | collective-permute-start | bytes 5013512 | tf_op jit(solution)/shard_map/ppermute | solution.py:252
  186.9 38.8 %collective-permute-start.13 = (bf16[192,2176]{1,0:T(8,128)(2,1)}, bf16[192,2176]{1,0:T(8,128)(2,1)S(1)}, u32[]{:S(2)}, u32[]{:S(2)}) collective-permute-start(bf16[192,2176]{1,0:T(8,128)(2,1)} %product_sent.3), channel_id=1, source_target_pairs={{1,0},{2,3},{5,4},{6,7},{9,8},{10,11},{13,12},{14,15},{17,16},{18,... | collective-permute-start | bytes 2506760 | tf_op jit(solution)/shard_map/ppermute | solution.py:252
  194.3 23.5 %copy-start.5 = (f32[192,2048]{1,0:T(8,128)S(1)}, f32[192,2048]{1,0:T(8,128)}, u32[]{:S(2)}) copy-start(f32[192,2048]{1,0:T(8,128)} %copy-done.4) | copy-start | bytes 4718596
  194.3 23.5 %copy-start.18 = (f32[192,256]{1,0:T(8,128)S(1)}, f32[192,256]{1,0:T(8,128)}, u32[]{:S(2)}) copy-start(f32[192,256]{1,0:T(8,128)} %copy-done.17) | copy-start | bytes 589828
  217.8 4.1 %copy-start = (f32[384,2048]{1,0:T(8,128)S(1)}, f32[384,2048]{1,0:T(8,128)}, u32[]{:S(2)}) copy-start(f32[384,2048]{1,0:T(8,128)} %get-tuple-element.51.refs_0_) | copy-start | bytes 9437188
  (12 other events, 12.5 us)
Sparse Core Ops, SparseCore 0:
  10.9 41.5 all-gather.2
  63.5 82.3 all-gather.4

commit v4 on v3

--- a/solution.py
+++ b/solution.py
@@ -77,8 +77,9 @@
     return pl.BlockSpec(shape, lambda *_: (0, 0), pipeline_mode=pl.Buffered(1))
 
 
-def product(pieces, rows, depth, weight, pool=None, choose=None):
-    features = weight.shape[1]
+def product(pieces, rows, first, weights, pool=None, choose=None, carry=None, flops=1000):
+    features = weights[0][0].shape[1]
+    depth = sum(count for _, _, count in weights)
     pool_rows = 0 if pool is None else pool.shape[0]
     tile = 256
     tiles = features // tile
@@ -90,17 +91,21 @@
 
     def kernel(*refs):
         refs = list(refs)
-        x_refs = [refs.pop(0) for _ in flat]
-        w_ref = refs.pop(0)
+        take = lambda count: [refs.pop(0) for _ in range(count)]
+        x_refs, w_refs = take(len(flat)), take(len(weights))
         if pool is not None:
-            down_ref = refs.pop(0)
+            (down_ref,) = take(1)
         if choose is not None:
-            owner_ref, ids_ref = refs.pop(0), refs.pop(0)
+            owner_ref, ids_ref = take(2)
+        if carry is not None:
+            acc_ref, sum_ref = take(2)
+        (out_ref,) = take(1)
+        if pool is not None and choose is None:
+            (low_ref,) = take(1)
+        (xs,) = take(1)
         if pool is not None:
-            sem, held = refs.pop(), refs.pop()
-            fetch = pltpu.make_async_copy(down_ref.at[:, pl.ds(0, depth)], held, sem)
-        xs = refs.pop()
-        out_ref = refs.pop(0)
+            held, sem = take(2)
+            fetch = pltpu.make_async_copy(down_ref.at[:, pl.ds(first, depth)], held, sem)
         n = pl.program_id(0)
 
         @pl.when(n == 0)
@@ -111,15 +116,24 @@
                     (at,) = [i for i, b in enumerate(flat) if a is b]
                     y = x_refs[at][:, lo:hi]
                     x = y if x is None else x + y
-                xs[row : row + x.shape[0], feature : feature + x.shape[1]] = x
+                at = feature - first
+                xs[row : row + x.shape[0], at : at + x.shape[1]] = x
             if pool is not None:
                 fetch.start()
 
-        p = jnp.dot(xs[...], w_ref[...], preferred_element_type=f32)
-        if choose is None:
+        p = None
+        at = 0
+        for w_ref in w_refs:
+            x = xs[:, at : at + w_ref.shape[0]]
+            at += w_ref.shape[0]
+            y = jnp.dot(x, w_ref[...], preferred_element_type=f32)
+            p = y if p is None else p + y
+        if choose is not None:
+            out_ref[:, pl.ds(pl.multiple_of(n * tile, tile), tile)] = p.astype(bf16)
+        elif carry is not None:
+            out_ref[...] = p + acc_ref[...]
+        else:
             out_ref[...] = p
-        else:
-            out_ref[:, pl.ds(pl.multiple_of(n * tile, tile), tile)] = p.astype(bf16)
 
         if pool is not None:
 
@@ -127,8 +141,10 @@
             def _():
                 fetch.wait()
                 low = dot_t(xs[...], held[...])
+                if carry is not None:
+                    low = low + sum_ref[...]
                 if choose is None:
-                    refs[0][...] = low
+                    low_ref[...] = low
                 else:
                     low = jnp.where(ids_ref[...] == owner_ref[...], low, 0.0)
                     chosen = low[:, :lanes]
@@ -137,29 +153,35 @@
                     out_ref[:, features:] = chosen.astype(bf16)
 
     in_specs = [constant(a.shape) for a in flat]
-    in_specs += [pl.BlockSpec((depth, tile), lambda n: (0, n))]
-    operands = flat + [weight]
+    operands = list(flat)
+    for array, row, count in weights:
+        if row % count == 0:
+            spec = pl.BlockSpec((count, tile), lambda n, at=row // count: (at, n))
+        else:
+            spec = pl.BlockSpec(
+                (pl.Element(count), pl.Element(tile)), lambda n, at=row: (at, n * tile)
+            )
+        in_specs.append(spec)
+        operands.append(array)
     if pool is not None:
         in_specs.append(pl.BlockSpec(memory_space=pl.ANY))
         operands.append(pool)
-    if pool is None:
-        out_shape = jax.ShapeDtypeStruct((rows, features), f32)
-        out_specs = pl.BlockSpec((rows, tile), lambda n: (0, n))
-    elif choose is None:
-        out_shape = [
-            jax.ShapeDtypeStruct((rows, features), f32),
-            jax.ShapeDtypeStruct((rows, pool_rows), f32),
-        ]
-        out_specs = [
-            pl.BlockSpec((rows, tile), lambda n: (0, n)),
-            pl.BlockSpec((rows, pool_rows), lambda n: (0, 0)),
-        ]
-    else:
+    if choose is not None:
         owner, ids = choose
         in_specs += [constant((1, pool_rows)), constant((rows, 1))]
         operands += [owner, ids]
+    if carry is not None:
+        in_specs += [pl.BlockSpec((rows, tile), lambda n: (0, n)), constant((rows, pool_rows))]
+        operands += list(carry)
+    if choose is not None:
         out_shape = jax.ShapeDtypeStruct((rows, features + lanes), bf16)
         out_specs = pl.BlockSpec((rows, features + lanes), lambda n: (0, 0))
+    else:
+        out_shape = jax.ShapeDtypeStruct((rows, features), f32)
+        out_specs = pl.BlockSpec((rows, tile), lambda n: (0, n))
+        if pool is not None:
+            out_shape = [out_shape, jax.ShapeDtypeStruct((rows, pool_rows), f32)]
+            out_specs = [out_specs, pl.BlockSpec((rows, pool_rows), lambda n: (0, 0))]
     scratch = [pltpu.VMEM((rows, depth), bf16)]
     if pool is not None:
         scratch += [pltpu.VMEM((pool_rows, depth), bf16), pltpu.SemaphoreType.DMA(())]
@@ -171,7 +193,7 @@
         out_shape=out_shape,
         scratch_shapes=scratch,
         compiler_params=pltpu.CompilerParams(vmem_limit_bytes=vmem),
-        cost_estimate=pl.CostEstimate(flops=1000, bytes_accessed=1000, transcendentals=0),
+        cost_estimate=pl.CostEstimate(flops=flops, bytes_accessed=1000, transcendentals=0),
         name="product" if choose is None else "product_sent",
     )(*operands)
 
@@ -252,6 +274,7 @@
     outward = lambda a: lax.ppermute(a, "tensor", [(1, 0), (2, 3)])
     cross = lambda a: lax.ppermute(a, "tensor", [(1, 2), (2, 1)])
 
+
     h = width * 7 // 16
     m = (width + h) // 2
     piece = h // (count * lax.axis_size("groups"))
@@ -259,7 +282,6 @@
     sent = inward(share)
     layer_input = after(layer_input, share)
     adapter_down_weight = after(adapter_down_weight, share)
-
     pool = jnp.concatenate([adapter_down_weight[0].T, adapter_up_weight[0]], axis=1)
     pool = lax.all_gather(pool, "replica", axis=0, tiled=True)
     owner = jnp.repeat(jnp.arange(count, dtype=jnp.int32), rank)[None, :]
@@ -268,8 +290,8 @@
     own_h, own_d, own_d0, own_d1 = norm_chunks(
         layer_input, input_norm_weight[None, :], [(0, h), (h, width), (h, m), (m, width)]
     )
-    w = query_base_matrix
-    own = product([(0, 0, [own_h]), (0, h, [own_d])], rows, width, w)
+    w = [(query_base_matrix, 0, width)]
+    own = product([(0, 0, [own_h]), (0, h, [own_d])], rows, 0, w)
     out_own = outward(own_d)
     mid_d = cross(own_d)
     end_d0 = inward(after(own_d0, sent))
@@ -286,35 +308,38 @@
     out_far0 = outward(after(far_d0, out_mid))
     far_d1 = cross(after(end_d1, far_d0))
     mid = product(
-        [(0, 0, [mid_h]), (0, h, [after(mid_d, far_d0), out_mid])], rows, width, w, pool
+        [(0, 0, [mid_h]), (0, h, [after(mid_d, far_d0), out_mid])], rows, 0, w, pool,
+        flops=1000,
     )
     out_far1 = outward(after(far_d1, out_far0, mid[0]))
     far_h = cross(after(end_h, far_d1))
     sent = after(sent, mid_d, out_own, own)
-    help_weight = lax.all_gather(sent, ("groups", "replica"), axis=0, tiled=True)
+    sent = lax.all_gather(sent, ("groups", "replica"), axis=0, tiled=True)
+    help_weight = [(sent, 0, h)]
 
     pick = lambda row: lax.dynamic_slice_in_dim(ids, row * rows, rows, 0)
     ids_near = jnp.concatenate([pick(t), pick(mid_row)], axis=0)
     part_near = product(
-        [(0, 0, [own_h]), (rows, 0, [mid_h])], 2 * rows, h, help_weight, pool,
+        [(0, 0, [own_h]), (rows, 0, [mid_h])], 2 * rows, 0, help_weight, pool,
         (owner, ids_near),
     )
-    far_h = after(far_h, part_near)
-    part_near = outward(after(part_near, out_far1))
-    part_far = product([(0, 0, [far_h])], rows, h, help_weight, pool, (owner, pick(far_row)))
-    far_h = after(far_h, part_far)
-    part_far = outward(part_far)
-    cut = m - h
     distant = product(
         [
-            (0, 0, [end_h]),
-            (0, h, [end_d0, (out_own, 0, cut)]),
-            (0, m, [end_d1, (out_own, cut, width - h)]),
-            (rows, 0, [far_h]),
+            (0, h, [after(end_d0, part_near), (out_own, 0, m - h)]),
+            (0, m, [end_d1, (out_own, m - h, width - h)]),
             (rows, h, [far_d0, out_far0]),
             (rows, m, [far_d1, out_far1]),
         ],
-        2 * rows, width, w, pool,
+        2 * rows, h, [(query_base_matrix, h, width - h)], pool,
+    )
+    part_near = outward(after(part_near, out_far1))
+    far_h = after(far_h, distant[0])
+    part_far = product([(0, 0, [far_h])], rows, 0, help_weight, pool, (owner, pick(far_row)))
+    far_h = after(far_h, part_far)
+    part_far = outward(part_far)
+    distant = product(
+        [(0, 0, [end_h]), (rows, 0, [far_h])],
+        2 * rows, 0, [(query_base_matrix, 0, h)], pool, None, distant,
     )
     out = finish(*mid, 0, part_near, 1, *last, mid_row, rows, out)
     out = finish(*distant, 0, part_near, 0, *last, t ^ 1, rows, out)

time: 238 us -> 236 us (level)
  the two profiles are of different devices: /device:TPU:12 before, /device:TPU:0 now
where the time goes in v4:
time: 236 us; the launch traced here: 234 us
  Pallas kernels  108 us (46%)
  waiting for transfers between devices  53.1 us (22%)
  starting transfers between devices  33.7 us (14%)
  local copies, waits for them, and re-layouts  17.9 us (8%)
  between operations  13.8 us (6%)
  matrix products  5.97 us (3%)
    pallas_call x6, Pallas kernels, product(): pl.pallas_call(kernel, grid=(tiles,), in_specs=in_specs, out_specs=out_sp...  88.5 us
    ppermute x6, waiting for transfers between devices, body(): outward = lambda a: lax.ppermute(a, 'tensor', [(1, 0), (2, 3)])  27.6 us
    ppermute x4, waiting for transfers between devices, body(): inward = lambda a: lax.ppermute(a, 'tensor', [(0, 1), (3, 2)])  21.1 us
    ppermute x4, starting transfers between devices, body(): inward = lambda a: lax.ppermute(a, 'tensor', [(0, 1), (3, 2)])  20.2 us
    pallas_call x4, Pallas kernels, finish(): pl.pallas_call(kernel, grid_spec=pltpu.PrefetchScalarGridSpec(num_scalar_...  15.7 us
    unnamed x54, local copies, waits for them, and re-layouts  13.6 us
    ppermute x6, starting transfers between devices, body(): outward = lambda a: lax.ppermute(a, 'tensor', [(1, 0), (2, 3)])  7.71 us
    dot_general x2, matrix products, dot_t(): lax.dot_general(a, b, (((1,), (1,)), ((), ())), preferred_element_type=f32)  5.97 us
  transfers between devices with their start and end apart: 17, of which 7 were waited for; matrix products, arithmetic and copies ran while one was open for 3% of the time, Pallas kernels for 45%

profile of v4, /device:TPU:0, one launch (start us, length us, event | category | flops | bytes accessed | tf_op | source)
XLA Modules:
  0.0 233.9 jit_solution(1646354112841607381)
XLA Ops:
  6.5 3.0 %constant_dynamic-slice_fusion = bf16[448,2048]{1,0:T(8,128)(2,1)} fusion(bf16[8192,2048]{1,0:T(8,128)(2,1)} %refs_2_.3, s32[]{:T(128)S(6)} %select_n.20), kind=kLoop, calls=%fused_computation.7 | loop fusion | bytes 3670020 | tf_op jit(solution)/shard_map/dynamic_slice | solution.py:281
  10.8 6.2 %collective-permute-start = (bf16[448,2048]{1,0:T(8,128)(2,1)}, bf16[448,2048]{1,0:T(8,128)(2,1)}, u32[]{:S(2)}, u32[]{:S(2)}) collective-permute-start(bf16[448,2048]{1,0:T(8,128)(2,1)} %constant_dynamic-slice_fusion), channel_id=1, source_target_pairs={{0,1},{3,2},{4,5},{7,6},{8,9},{11,10},{12,13},{15,14},{16,17},{19,... | collective-permute-start | bytes 5505032 | tf_op jit(solution)/shard_map/ppermute | solution.py:273
  17.0 4.0 %norm_chunks.1 = (bf16[192,3584]{1,0:T(8,128)(2,1)S(1)}, bf16[192,4608]{1,0:T(8,128)(2,1)S(1)}, bf16[192,2304]{1,0:T(8,128)(2,1)S(1)}, bf16[192,2304]{1,0:T(8,128)(2,1)S(1)}) custom-call(bf16[192,8192]{1,0:T(8,128)(2,1)} %x_ref, bf16[1,8192]{1,0:T(2,128)(2,1)S(1)} %broadcast_in_dim.19.g_ref), custom_call_target="tpu_custom_call" | custom-call | flops 1000 | bytes 1000 | tf_op jit(solution)/shard_map/norm_chunks/pallas_call | solution.py:53
  23.7 1.3 collective-permute-start.9
  25.0 14.9 %product.4.refs_0_ = f32[192,2048]{1,0:T(8,128)S(1)} custom-call(bf16[192,3584]{1,0:T(8,128)(2,1)S(1)} %get-tuple-element.42.refs_0_, bf16[192,4608]{1,0:T(8,128)(2,1)S(1)} %get-tuple-element.38.refs_1_, bf16[8192,2048]{1,0:T(8,128)(2,1)} %refs_2_.3), custom_call_target="tpu_custom_call" | custom-call | flops 1000 | bytes 1000 | tf_op jit(solution)/shard_map/product/pallas_call | solution.py:188
  40.0 25.7 %collective-permute-done.9.refs_1_ = bf16[192,4608]{1,0:T(8,128)(2,1)S(1)} collective-permute-done((bf16[192,4608]{1,0:T(8,128)(2,1)S(1)}, bf16[192,4608]{1,0:T(8,128)(2,1)S(1)}, u32[]{:S(2)}, u32[]{:S(2)}) %collective-permute-start.9) | collective-permute-done | bytes 1769504 | tf_op jit(solution)/shard_map/ppermute | solution.py:274
  65.6 1.2 copy-done.22
  66.9 1.8 collective-permute-start.5
  68.7 4.0 %collective-permute-start.1 = (bf16[192,2304]{1,0:T(8,128)(2,1)}, bf16[192,2304]{1,0:T(8,128)(2,1)}, u32[]{:S(2)}, u32[]{:S(2)}) collective-permute-start(bf16[192,2304]{1,0:T(8,128)(2,1)} %copy-done.21), channel_id=1, source_target_pairs={{0,1},{3,2},{4,5},{7,6},{8,9},{11,10},{12,13},{15,14},{16,17},{19,... | collective-permute-start | bytes 2654216 | tf_op jit(solution)/shard_map/ppermute | solution.py:273
  72.7 1.3 collective-permute-start.10
  74.3 3.7 %fusion = f32[192,256]{1,0:T(8,128)S(1)} fusion(bf16[192,4608]{1,0:T(8,128)(2,1)} %copy-done.1, bf16[256,10240]{1,0:T(8,128)(2,1)} %all-gather.3.cloned.1.call-done.refs_2_.refs_3_.refs_4_.refs_8_), kind=kOutput, calls=%fused_computation | convolution fusion | flops 452984832 | bytes 4325376 | tf_op jit(solution)/shard_map/dot_general | solution.py:69
  78.0 2.2 fusion.4.refs_1_
  80.3 4.0 %finish.4.refs_7_ = bf16[768,2048]{1,0:T(8,128)(2,1)} custom-call(s32[1]{0:T(128)} %bitcast.1.row_ref, f32[192,2048]{1,0:T(8,128)S(1)} %product.4.refs_0_, f32[192,256]{1,0:T(8,128)S(1)} %fusion.4.refs_1_, bf16[256,10240]{1,0:T(8,128)(2,1)} %all-gather.3.cloned.1.call-done.refs_2_.refs_3_.refs_4_.refs_8_, ...), custom_call_target="tpu_custom_call" | custom-call | flops 1000 | bytes 1000 | tf_op jit(solution)/shard_map/finish/pallas_call | solution.py:244
  84.3 5.2 %collective-permute-done.1.refs_0_ = bf16[192,2304]{1,0:T(8,128)(2,1)} collective-permute-done((bf16[192,2304]{1,0:T(8,128)(2,1)}, bf16[192,2304]{1,0:T(8,128)(2,1)}, u32[]{:S(2)}, u32[]{:S(2)}) %collective-permute-start.1) | collective-permute-done | bytes 884768 | tf_op jit(solution)/shard_map/ppermute | solution.py:273
  89.5 4.4 %collective-permute-start.2 = (bf16[192,2304]{1,0:T(8,128)(2,1)S(1)}, bf16[192,2304]{1,0:T(8,128)(2,1)S(1)}, u32[]{:S(2)}, u32[]{:S(2)}) collective-permute-start(bf16[192,2304]{1,0:T(8,128)(2,1)S(1)} %copy-done.20), channel_id=1, source_target_pairs={{0,1},{3,2},{4,5},{7,6},{8,9},{11,10},{12,13},{15,14},{16,17},{19,... | collective-permute-start | bytes 2654216 | tf_op jit(solution)/shard_map/ppermute | solution.py:273
  94.7 15.7 %collective-permute-done.2.refs_2_ = bf16[192,2304]{1,0:T(8,128)(2,1)S(1)} collective-permute-done((bf16[192,2304]{1,0:T(8,128)(2,1)S(1)}, bf16[192,2304]{1,0:T(8,128)(2,1)S(1)}, u32[]{:S(2)}, u32[]{:S(2)}) %collective-permute-start.2) | collective-permute-done | bytes 884768 | tf_op jit(solution)/shard_map/ppermute | solution.py:273
  110.4 5.6 %collective-permute-start.3 = (bf16[192,3584]{1,0:T(8,128)(2,1)S(1)}, bf16[192,3584]{1,0:T(8,128)(2,1)}, u32[]{:S(2)}, u32[]{:S(2)}) collective-permute-start(bf16[192,3584]{1,0:T(8,128)(2,1)S(1)} %get-tuple-element.42.refs_0_), channel_id=1, source_target_pairs={{0,1},{3,2},{4,5},{7,6},{8,9},{11,10},{12,13},{15,14},{16,17},{19,... | collective-permute-start | bytes 4128776 | tf_op jit(solution)/shard_map/ppermute | solution.py:273
  116.0 1.3 collective-permute-start.11
  118.0 18.0 %product.5 = (f32[192,2048]{1,0:T(8,128)S(1)}, f32[192,256]{1,0:T(8,128)S(1)}) custom-call(bf16[192,3584]{1,0:T(8,128)(2,1)} %collective-permute-done.5.refs_1_.refs_0_, bf16[192,4608]{1,0:T(8,128)(2,1)S(1)} %copy-done.3, bf16[192,4608]{1,0:T(8,128)(2,1)} %collective-permute-done.10.refs_2_, bf16[8192,2048]{1,0:T(8,128)(2,1)} %refs_2_.3, ...), custom_call_target="tpu_custom_call" | custom-call | flops 1000 | bytes 1000 | tf_op jit(solution)/shard_map/product/pallas_call | solution.py:188
  139.5 1.3 collective-permute-start.12
  141.0 1.8 collective-permute-start.8
  143.8 4.4 %all-gather.5.cloned.1.call-done.refs_2_.refs_1_ = bf16[3584,2048]{1,0:T(8,128)(2,1)} async-done(((bf16[448,2048]{1,0:T(8,128)(2,1)}), bf16[3584,2048]{1,0:T(8,128)(2,1)}) %all-gather.5.cloned.1.call-update) | async-done | bytes 14680080 | tf_op jit(solution)/shard_map/all_gather | solution.py:317
  149.0 13.5 %product_sent.2 = bf16[384,2176]{1,0:T(8,128)(2,1)} custom-call(bf16[192,3584]{1,0:T(8,128)(2,1)S(1)} %get-tuple-element.42.refs_0_, bf16[192,3584]{1,0:T(8,128)(2,1)} %collective-permute-done.5.refs_1_.refs_0_, bf16[3584,2048]{1,0:T(8,128)(2,1)} %all-gather.5.cloned.1.call-done.refs_2_.refs_1_, ...), custom_call_target="tpu_custom_call" | custom-call | flops 1000 | bytes 1000 | tf_op jit(solution)/shard_map/product_sent/pallas_call | solution.py:188
  162.6 1.2 collective-permute-done.12.refs_6_
  164.7 1.3 collective-permute-start.14
  172.0 16.0 %product.6 = (f32[384,2048]{1,0:T(8,128)}, f32[384,256]{1,0:T(8,128)S(1)}) custom-call(bf16[192,2304]{1,0:T(8,128)(2,1)} %collective-permute-done.1.refs_0_, bf16[192,4608]{1,0:T(8,128)(2,1)} %copy-done.22, bf16[192,2304]{1,0:T(8,128)(2,1)S(1)} %copy-done.7, bf16[192,2304]{1,0:T(8,128)(2,1)S(1)} %copy-done.9, bf16[192,2304]{1,0:T(8,128)(2,1)S(1)} %copy-done.11, ...), custom_call_target="tpu_custom_call" | custom-call | flops 1000 | bytes 1000 | tf_op jit(solution)/shard_map/product/pallas_call | solution.py:188
  188.0 11.4 %product_sent.3 = bf16[192,2176]{1,0:T(8,128)(2,1)} custom-call(bf16[192,3584]{1,0:T(8,128)(2,1)} %collective-permute-done.8.refs_0_.refs_1_, bf16[3584,2048]{1,0:T(8,128)(2,1)} %all-gather.5.cloned.1.call-done.refs_2_.refs_1_, bf16[256,10240]{1,0:T(8,128)(2,1)} %all-gather.3.cloned.1.call-done.refs_2_.refs_3_.refs_4_.refs_8_, ...), custom_call_target="tpu_custom_call" | custom-call | flops 1000 | bytes 1000 | tf_op jit(solution)/shard_map/product_sent/pallas_call | solution.py:188
  199.4 1.3 collective-permute-start.13
  200.8 14.6 %product.7 = (f32[384,2048]{1,0:T(8,128)}, f32[384,256]{1,0:T(8,128)S(1)}) custom-call(bf16[192,3584]{1,0:T(8,128)(2,1)} %collective-permute-done.3.refs_0_, bf16[192,3584]{1,0:T(8,128)(2,1)} %collective-permute-done.8.refs_0_.refs_1_, bf16[8192,2048]{1,0:T(8,128)(2,1)} %refs_2_.3, ...), custom_call_target="tpu_custom_call" | custom-call | flops 1000 | bytes 1000 | tf_op jit(solution)/shard_map/product/pallas_call | solution.py:188
  215.4 4.0 %finish.5.refs_7_ = bf16[768,2048]{1,0:T(8,128)(2,1)} custom-call(s32[1]{0:T(128)} %bitcast.9.row_ref, f32[192,2048]{1,0:T(8,128)S(1)} %copy-done.5, f32[192,256]{1,0:T(8,128)S(1)} %copy-done.18, bf16[256,10240]{1,0:T(8,128)(2,1)} %all-gather.3.cloned.1.call-done.refs_2_.refs_3_.refs_4_.refs_8_, ...), custom_call_target="tpu_custom_call", output_to_operand_aliasing={{}: (8, {})} | custom-call | flops 1000 | bytes 1000 | tf_op jit(solution)/shard_map/finish/pallas_call | solution.py:244
  219.4 3.8 %finish.6.refs_7_ = bf16[768,2048]{1,0:T(8,128)(2,1)} custom-call(s32[1]{0:T(128)} %bitcast.8.row_ref, f32[384,2048]{1,0:T(8,128)S(1)} %copy-done, f32[384,256]{1,0:T(8,128)S(1)} %get-tuple-element.58.refs_1_, bf16[256,10240]{1,0:T(8,128)(2,1)} %all-gather.3.cloned.1.call-done.refs_2_.refs_3_.refs_4_.refs_8_, ...), custom_call_target="tpu_custom_call", output_to_operand_aliasing={{}: (8, {})} | custom-call | flops 1000 | bytes 1000 | tf_op jit(solution)/shard_map/finish/pallas_call | solution.py:244
  223.3 3.8 %finish.7 = bf16[768,2048]{1,0:T(8,128)(2,1)} custom-call(s32[1]{0:T(128)} %bitcast.row_ref, f32[384,2048]{1,0:T(8,128)S(1)} %copy-done, f32[384,256]{1,0:T(8,128)S(1)} %get-tuple-element.58.refs_1_, bf16[256,10240]{1,0:T(8,128)(2,1)} %all-gather.3.cloned.1.call-done.refs_2_.refs_3_.refs_4_.refs_8_, ...), custom_call_target="tpu_custom_call", output_to_operand_aliasing={{}: (8, {})} | custom-call | flops 1000 | bytes 1000 | tf_op jit(solution)/shard_map/finish/pallas_call | solution.py:244
  (81 shorter events, 18.1 us)
Async XLA Ops:
  6.5 67.8 %all-gather.3.cloned.1.call-start = ((), (), s32[]{:S(2)}) async-start(), calls=%async_computation | async-start | bytes 6553600 | tf_op jit(solution)/shard_map/all_gather | solution.py:286
  6.5 3.0 %copy-start.23 = (bf16[1,8192,64]{1,2,0:T(8,128)(2,1)S(1)}, bf16[1,8192,64]{1,2,0:T(8,128)(2,1)}, u32[]{:S(2)}) copy-start(bf16[1,8192,64]{1,2,0:T(8,128)(2,1)} %param.9) | copy-start | bytes 3145732
  6.5 3.0 %copy-start.24 = (bf16[1,64,2048]{2,1,0:T(8,128)(2,1)S(1)}, bf16[1,64,2048]{2,1,0:T(8,128)(2,1)}, u32[]{:S(2)}) copy-start(bf16[1,64,2048]{2,1,0:T(8,128)(2,1)} %param.10) | copy-start | bytes 786436
  9.6 7.4 %copy-start.25 = (bf16[8192]{0:T(1024)(128)(2,1)S(1)}, bf16[8192]{0:T(1024)(128)(2,1)}, u32[]{:S(2)}) copy-start(bf16[8192]{0:T(1024)(128)(2,1)} %param.7) | copy-start | bytes 49156
  10.8 137.3 %all-gather.5.cloned.1.call-start = ((), (), s32[]{:S(2)}) async-start(), calls=%async_computation.1 | async-start | bytes 16515072 | tf_op jit(solution)/shard_map/all_gather | solution.py:317
  10.8 56.1 %collective-permute-start = (bf16[448,2048]{1,0:T(8,128)(2,1)}, bf16[448,2048]{1,0:T(8,128)(2,1)}, u32[]{:S(2)}, u32[]{:S(2)}) collective-permute-start(bf16[448,2048]{1,0:T(8,128)(2,1)} %constant_dynamic-slice_fusion), channel_id=1, source_target_pairs={{0,1},{3,2},{4,5},{7,6},{8,9},{11,10},{12,13},{15,14},{16,17},{19,... | collective-permute-start | bytes 5505032 | tf_op jit(solution)/shard_map/ppermute | solution.py:273
  22.9 17.0 %copy-start.1 = (bf16[192,4608]{1,0:T(8,128)(2,1)}, bf16[192,4608]{1,0:T(8,128)(2,1)S(1)}, u32[]{:S(2)}) copy-start(bf16[192,4608]{1,0:T(8,128)(2,1)S(1)} %get-tuple-element.38.refs_1_) | copy-start | bytes 5308420
  22.9 17.0 %collective-permute-start.4 = (bf16[192,4608]{1,0:T(8,128)(2,1)S(1)}, bf16[192,4608]{1,0:T(8,128)(2,1)S(1)}, u32[]{:S(2)}, u32[]{:S(2)}) collective-permute-start(bf16[192,4608]{1,0:T(8,128)(2,1)S(1)} %get-tuple-element.38.refs_1_), channel_id=1, source_target_pairs={{1,2},{2,1},{5,6},{6,5},{9,10},{10,9},{13,14},{14,13},{17,18},{18,... | collective-permute-start | bytes 5308424 | tf_op jit(solution)/shard_map/ppermute | solution.py:275
  23.7 42.0 %collective-permute-start.9 = (bf16[192,4608]{1,0:T(8,128)(2,1)S(1)}, bf16[192,4608]{1,0:T(8,128)(2,1)S(1)}, u32[]{:S(2)}, u32[]{:S(2)}) collective-permute-start(bf16[192,4608]{1,0:T(8,128)(2,1)S(1)} %get-tuple-element.38.refs_1_), channel_id=1, source_target_pairs={{1,0},{2,3},{5,4},{6,7},{9,8},{10,11},{13,12},{14,15},{17,16},{18,... | collective-permute-start | bytes 5308424 | tf_op jit(solution)/shard_map/ppermute | solution.py:274
  39.9 34.2 %copy-start.26 = (s32[768]{0:T(1024)S(1)}, s32[768]{0:T(1024)}, u32[]{:S(2)}) copy-start(s32[768]{0:T(1024)} %param.11) | copy-start | bytes 9220
  39.9 25.7 %copy-start.2 = (bf16[192,4608]{1,0:T(8,128)(2,1)}, bf16[192,4608]{1,0:T(8,128)(2,1)S(1)}, u32[]{:S(2)}) copy-start(bf16[192,4608]{1,0:T(8,128)(2,1)S(1)} %collective-permute-done.4.refs_1_) | copy-start | bytes 5308420
  65.6 1.2 copy-start.22
  66.9 27.1 %collective-permute-start.5 = (bf16[192,3584]{1,0:T(8,128)(2,1)S(1)}, bf16[192,3584]{1,0:T(8,128)(2,1)}, u32[]{:S(2)}, u32[]{:S(2)}) collective-permute-start(bf16[192,3584]{1,0:T(8,128)(2,1)S(1)} %get-tuple-element.42.refs_0_), channel_id=1, source_target_pairs={{1,2},{2,1},{5,6},{6,5},{9,10},{10,9},{13,14},{14,13},{17,18},{18,... | collective-permute-start | bytes 4128776 | tf_op jit(solution)/shard_map/ppermute | solution.py:275
  68.7 20.8 %collective-permute-start.1 = (bf16[192,2304]{1,0:T(8,128)(2,1)}, bf16[192,2304]{1,0:T(8,128)(2,1)}, u32[]{:S(2)}, u32[]{:S(2)}) collective-permute-start(bf16[192,2304]{1,0:T(8,128)(2,1)} %copy-done.21), channel_id=1, source_target_pairs={{0,1},{3,2},{4,5},{7,6},{8,9},{11,10},{12,13},{15,14},{16,17},{19,... | collective-permute-start | bytes 2654216 | tf_op jit(solution)/shard_map/ppermute | solution.py:273
  72.7 43.3 %collective-permute-start.10 = (bf16[192,4608]{1,0:T(8,128)(2,1)}, bf16[192,4608]{1,0:T(8,128)(2,1)}, u32[]{:S(2)}, u32[]{:S(2)}) collective-permute-start(bf16[192,4608]{1,0:T(8,128)(2,1)} %copy-done.2), channel_id=1, source_target_pairs={{1,0},{2,3},{5,4},{6,7},{9,8},{10,11},{13,12},{14,15},{17,16},{18,... | collective-permute-start | bytes 5308424 | tf_op jit(solution)/shard_map/ppermute | solution.py:274
  80.3 9.2 %copy-start.20 = (bf16[192,2304]{1,0:T(8,128)(2,1)S(1)}, bf16[192,2304]{1,0:T(8,128)(2,1)}, u32[]{:S(2)}) copy-start(bf16[192,2304]{1,0:T(8,128)(2,1)} %copy-done.19) | copy-start | bytes 2654212
  80.3 37.7 %copy-start.3 = (bf16[192,4608]{1,0:T(8,128)(2,1)S(1)}, bf16[192,4608]{1,0:T(8,128)(2,1)}, u32[]{:S(2)}) copy-start(bf16[192,4608]{1,0:T(8,128)(2,1)} %copy-done.2) | copy-start | bytes 5308420
  89.5 20.9 %collective-permute-start.2 = (bf16[192,2304]{1,0:T(8,128)(2,1)S(1)}, bf16[192,2304]{1,0:T(8,128)(2,1)S(1)}, u32[]{:S(2)}, u32[]{:S(2)}) collective-permute-start(bf16[192,2304]{1,0:T(8,128)(2,1)S(1)} %copy-done.20), channel_id=1, source_target_pairs={{0,1},{3,2},{4,5},{7,6},{8,9},{11,10},{12,13},{15,14},{16,17},{19,... | collective-permute-start | bytes 2654216 | tf_op jit(solution)/shard_map/ppermute | solution.py:273
  94.0 22.0 %collective-permute-start.6 = (bf16[192,2304]{1,0:T(8,128)(2,1)}, bf16[192,2304]{1,0:T(8,128)(2,1)S(1)}, u32[]{:S(2)}, u32[]{:S(2)}) collective-permute-start(bf16[192,2304]{1,0:T(8,128)(2,1)} %collective-permute-done.1.refs_0_), channel_id=1, source_target_pairs={{1,2},{2,1},{5,6},{6,5},{9,10},{10,9},{13,14},{14,13},{17,18},{18,... | collective-permute-start | bytes 2654216 | tf_op jit(solution)/shard_map/ppermute | solution.py:275
  110.4 25.6 %copy-start.6 = (bf16[192,2304]{1,0:T(8,128)(2,1)}, bf16[192,2304]{1,0:T(8,128)(2,1)S(1)}, u32[]{:S(2)}) copy-start(bf16[192,2304]{1,0:T(8,128)(2,1)S(1)} %collective-permute-done.2.refs_2_) | copy-start | bytes 2654212
  110.4 30.6 %collective-permute-start.3 = (bf16[192,3584]{1,0:T(8,128)(2,1)S(1)}, bf16[192,3584]{1,0:T(8,128)(2,1)}, u32[]{:S(2)}, u32[]{:S(2)}) collective-permute-start(bf16[192,3584]{1,0:T(8,128)(2,1)S(1)} %get-tuple-element.42.refs_0_), channel_id=1, source_target_pairs={{0,1},{3,2},{4,5},{7,6},{8,9},{11,10},{12,13},{15,14},{16,17},{19,... | collective-permute-start | bytes 4128776 | tf_op jit(solution)/shard_map/ppermute | solution.py:273
  116.0 20.1 %copy-start.8 = (bf16[192,2304]{1,0:T(8,128)(2,1)}, bf16[192,2304]{1,0:T(8,128)(2,1)S(1)}, u32[]{:S(2)}) copy-start(bf16[192,2304]{1,0:T(8,128)(2,1)S(1)} %collective-permute-done.6.refs_3_) | copy-start | bytes 2654212
  116.0 22.5 %collective-permute-start.11 = (bf16[192,2304]{1,0:T(8,128)(2,1)S(1)}, bf16[192,2304]{1,0:T(8,128)(2,1)S(1)}, u32[]{:S(2)}, u32[]{:S(2)}) collective-permute-start(bf16[192,2304]{1,0:T(8,128)(2,1)S(1)} %collective-permute-done.6.refs_3_), channel_id=1, source_target_pairs={{1,0},{2,3},{5,4},{6,7},{9,8},{10,11},{13,12},{14,15},{17,16},{18,... | collective-permute-start | bytes 2654216 | tf_op jit(solution)/shard_map/ppermute | solution.py:274
  117.3 22.2 %collective-permute-start.7 = (bf16[192,2304]{1,0:T(8,128)(2,1)S(1)}, bf16[192,2304]{1,0:T(8,128)(2,1)S(1)}, u32[]{:S(2)}, u32[]{:S(2)}) collective-permute-start(bf16[192,2304]{1,0:T(8,128)(2,1)S(1)} %collective-permute-done.2.refs_2_), channel_id=1, source_target_pairs={{1,2},{2,1},{5,6},{6,5},{9,10},{10,9},{13,14},{14,13},{17,18},{18,... | collective-permute-start | bytes 2654216 | tf_op jit(solution)/shard_map/ppermute | solution.py:275
  139.5 23.1 %copy-start.12 = (bf16[192,2304]{1,0:T(8,128)(2,1)}, bf16[192,2304]{1,0:T(8,128)(2,1)S(1)}, u32[]{:S(2)}) copy-start(bf16[192,2304]{1,0:T(8,128)(2,1)S(1)} %collective-permute-done.7.refs_5_) | copy-start | bytes 2654212
  139.5 24.3 %collective-permute-start.12 = (bf16[192,2304]{1,0:T(8,128)(2,1)S(1)}, bf16[192,2304]{1,0:T(8,128)(2,1)S(1)}, u32[]{:S(2)}, u32[]{:S(2)}) collective-permute-start(bf16[192,2304]{1,0:T(8,128)(2,1)S(1)} %collective-permute-done.7.refs_5_), channel_id=1, source_target_pairs={{1,0},{2,3},{5,4},{6,7},{9,8},{10,11},{13,12},{14,15},{17,16},{18,... | collective-permute-start | bytes 2654216 | tf_op jit(solution)/shard_map/ppermute | solution.py:274
  141.0 47.0 %collective-permute-start.8 = (bf16[192,3584]{1,0:T(8,128)(2,1)}, bf16[192,3584]{1,0:T(8,128)(2,1)}, u32[]{:S(2)}, u32[]{:S(2)}) collective-permute-start(bf16[192,3584]{1,0:T(8,128)(2,1)} %collective-permute-done.3.refs_0_), channel_id=1, source_target_pairs={{1,2},{2,1},{5,6},{6,5},{9,10},{10,9},{13,14},{14,13},{17,18},{18,... | collective-permute-start | bytes 4128776 | tf_op jit(solution)/shard_map/ppermute | solution.py:275
  164.7 50.6 %collective-permute-start.14 = (bf16[384,2176]{1,0:T(8,128)(2,1)}, bf16[384,2176]{1,0:T(8,128)(2,1)S(1)}, u32[]{:S(2)}, u32[]{:S(2)}) collective-permute-start(bf16[384,2176]{1,0:T(8,128)(2,1)} %product_sent.2), channel_id=1, source_target_pairs={{1,0},{2,3},{5,4},{6,7},{9,8},{10,11},{13,12},{14,15},{17,16},{18,... | collective-permute-start | bytes 5013512 | tf_op jit(solution)/shard_map/ppermute | solution.py:274
  199.4 23.8 %collective-permute-start.13 = (bf16[192,2176]{1,0:T(8,128)(2,1)}, bf16[192,2176]{1,0:T(8,128)(2,1)S(1)}, u32[]{:S(2)}, u32[]{:S(2)}) collective-permute-start(bf16[192,2176]{1,0:T(8,128)(2,1)} %product_sent.3), channel_id=1, source_target_pairs={{1,0},{2,3},{5,4},{6,7},{9,8},{10,11},{13,12},{14,15},{17,16},{18,... | collective-permute-start | bytes 2506760 | tf_op jit(solution)/shard_map/ppermute | solution.py:274
  200.7 14.6 %copy-start.5 = (f32[192,2048]{1,0:T(8,128)S(1)}, f32[192,2048]{1,0:T(8,128)}, u32[]{:S(2)}) copy-start(f32[192,2048]{1,0:T(8,128)} %copy-done.4) | copy-start | bytes 4718596
  200.7 14.6 %copy-start.18 = (f32[192,256]{1,0:T(8,128)S(1)}, f32[192,256]{1,0:T(8,128)}, u32[]{:S(2)}) copy-start(f32[192,256]{1,0:T(8,128)} %copy-done.17) | copy-start | bytes 589828
  215.4 4.0 %copy-start = (f32[384,2048]{1,0:T(8,128)S(1)}, f32[384,2048]{1,0:T(8,128)}, u32[]{:S(2)}) copy-start(f32[384,2048]{1,0:T(8,128)} %get-tuple-element.57.refs_0_) | copy-start | bytes 9437188
  (12 other events, 12.3 us)
Sparse Core Ops, SparseCore 0:
  10.9 43.1 all-gather.2
  67.0 81.0 all-gather.4

commit v5 on v4

--- a/solution.py
+++ b/solution.py
@@ -7,7 +7,7 @@
 
 adapter_scale = 2.0
 lanes = 128
-vmem = 48 * 1024 * 1024
+vmem = 60 * 1024 * 1024
 f32 = jnp.float32
 bf16 = jnp.bfloat16
 
@@ -59,7 +59,7 @@
         ],
         out_specs=[pl.BlockSpec((block, hi - lo), lambda i: (i, 0)) for lo, hi in spans],
         out_shape=[jax.ShapeDtypeStruct((rows, hi - lo), bf16) for lo, hi in spans],
-        compiler_params=pltpu.CompilerParams(vmem_limit_bytes=vmem),
+        compiler_params=pltpu.CompilerParams(vmem_limit_bytes=vmem // 2),
         cost_estimate=pl.CostEstimate(flops=1000, bytes_accessed=1000, transcendentals=0),
         name="norm_chunks",
     )(x, gain)
@@ -251,7 +251,7 @@
         ),
         out_shape=jax.ShapeDtypeStruct((ids.shape[0], features), bf16),
         input_output_aliases=aliases,
-        compiler_params=pltpu.CompilerParams(vmem_limit_bytes=vmem),
+        compiler_params=pltpu.CompilerParams(vmem_limit_bytes=vmem // 4),
         cost_estimate=pl.CostEstimate(flops=1000, bytes_accessed=1000, transcendentals=0),
         name="finish",
     )(row.reshape(1), *operands)
@@ -287,33 +287,42 @@
     owner = jnp.repeat(jnp.arange(count, dtype=jnp.int32), rank)[None, :]
     ids = token_adapter_index[:, None]
 
-    own_h, own_d, own_d0, own_d1 = norm_chunks(
-        layer_input, input_norm_weight[None, :], [(0, h), (h, width), (h, m), (m, width)]
+    c = h + (width - h) * 7 // 9
+    own_h, own_a, own_b, own_d0, own_d1 = norm_chunks(
+        layer_input,
+        input_norm_weight[None, :],
+        [(0, h), (h, c), (c, width), (h, m), (m, width)],
     )
     w = [(query_base_matrix, 0, width)]
-    own = product([(0, 0, [own_h]), (0, h, [own_d])], rows, 0, w)
-    out_own = outward(own_d)
-    mid_d = cross(own_d)
+    own = product([(0, 0, [own_h]), (0, h, [own_a]), (0, c, [own_b])], rows, 0, w)
+    out_own_a = outward(own_a)
+    mid_a = cross(own_a)
+    out_own_b = outward(after(own_b, out_own_a))
+    mid_b = cross(after(own_b, mid_a))
+    out_mid_a = outward(after(mid_a, out_own_a))
     end_d0 = inward(after(own_d0, sent))
-    out_mid = outward(after(mid_d, out_own))
-    mid_h = cross(after(own_h, mid_d, own))
+    mid_h = cross(after(own_h, mid_a))
+    out_mid_b = outward(after(mid_b, out_own_b))
     mid_row = jnp.where(t < 2, 2, 1).astype(jnp.int32)
     far_row = jnp.where(t < 2, 3, 0).astype(jnp.int32)
     last = (pool, width, owner, ids)
-    own_low = dot_t(own_h, pool[:, :h]) + dot_t(own_d, pool[:, h:width])
+    own_low = (
+        dot_t(own_h, pool[:, :h]) + dot_t(own_a, pool[:, h:c]) + dot_t(after(own_b, out_own_b, mid_b), pool[:, c:width])
+    )
     out = finish(own, own_low, 0, None, 0, *last, t, rows, None)
     end_d1 = inward(after(own_d1, end_d0, out))
     far_d0 = cross(after(end_d0, mid_h))
-    end_h = inward(after(own_h, end_d1))
-    out_far0 = outward(after(far_d0, out_mid))
+    mid = product([(0, 0, [mid_h])], rows, 0, [(query_base_matrix, 0, h)], pool)
+    end_h = inward(after(own_h, end_d1, out_mid_a, mid[0]))
+    out_far0 = outward(after(far_d0, out_mid_b))
     far_d1 = cross(after(end_d1, far_d0))
     mid = product(
-        [(0, 0, [mid_h]), (0, h, [after(mid_d, far_d0), out_mid])], rows, 0, w, pool,
-        flops=1000,
+        [(0, h, [after(mid_a, far_d0), out_mid_a]), (0, c, [mid_b, out_mid_b])],
+        rows, h, [(query_base_matrix, h, width - h)], pool, None, mid,
     )
     out_far1 = outward(after(far_d1, out_far0, mid[0]))
     far_h = cross(after(end_h, far_d1))
-    sent = after(sent, mid_d, out_own, own)
+    sent = after(sent, mid_a, out_own_a, own)
     sent = lax.all_gather(sent, ("groups", "replica"), axis=0, tiled=True)
     help_weight = [(sent, 0, h)]
 
@@ -325,8 +334,9 @@
     )
     distant = product(
         [
-            (0, h, [after(end_d0, part_near), (out_own, 0, m - h)]),
-            (0, m, [end_d1, (out_own, m - h, width - h)]),
+            (0, h, [after(end_d0, part_near), (out_own_a, 0, m - h)]),
+            (0, m, [(end_d1, 0, c - m), (out_own_a, m - h, c - h)]),
+            (0, c, [(end_d1, c - m, width - m), out_own_b]),
             (rows, h, [far_d0, out_far0]),
             (rows, m, [far_d1, out_far1]),
         ],

time: 236 us -> 230 us (0.975)
  waiting for transfers between devices: 53.1 us -> 31.5 us
  starting transfers between devices: 33.7 us -> 49 us
  Pallas kernels: 108 us -> 115 us
  local copies, waits for them, and re-layouts: 17.9 us -> 11.9 us
    pallas_call x6 -> x7, Pallas kernels: 88.5 us -> 102 us  [product(): pl.pallas_call(kernel, grid=(tiles,), in_specs=in_specs, out_specs=out_sp...]
    ppermute x4, starting transfers between devices: 20.2 us -> 31.7 us  [body(): inward = lambda a: lax.ppermute(a, 'tensor', [(0, 1), (3, 2)])]
    ppermute x4, waiting for transfers between devices: 21.1 us -> 10.8 us  [body(): inward = lambda a: lax.ppermute(a, 'tensor', [(0, 1), (3, 2)])]
    ppermute x6 -> x8, waiting for transfers between devices: 27.6 us -> 20.6 us  [body(): outward = lambda a: lax.ppermute(a, 'tensor', [(1, 0), (2, 3)])]
    unnamed x54 -> x48, local copies, waits for them, and re-layouts: 13.6 us -> 6.94 us
    pallas_call x4, Pallas kernels: 15.7 us -> 9.81 us  [finish(): pl.pallas_call(kernel, grid_spec=pltpu.PrefetchScalarGridSpec(num_scalar_...]
    all_gather x1, waiting for transfers between devices: 4.35 us -> 0.01 us  [body(): sent = lax.all_gather(sent, ('groups', 'replica'), axis=0, tiled=True)]
    ppermute x6 -> x8, starting transfers between devices: 7.71 us -> 10.3 us  [body(): outward = lambda a: lax.ppermute(a, 'tensor', [(1, 0), (2, 3)])]
  transfers between devices with their start and end apart: 17 -> 20, of which waited for: 7 -> 5; matrix products, arithmetic and copies ran while one was open for 3% -> 3% of each run, Pallas kernels for 45% -> 49%
where the time goes in v5:
time: 230 us; the launch traced here: 228 us
  Pallas kernels  115 us (50%)
  starting transfers between devices  49 us (21%)
  waiting for transfers between devices  31.5 us (14%)
  between operations  13.8 us (6%)
  local copies, waits for them, and re-layouts  11.9 us (5%)
  matrix products  5.5 us (2%)
    pallas_call x7, Pallas kernels, product(): pl.pallas_call(kernel, grid=(tiles,), in_specs=in_specs, out_specs=out_sp...  102 us
    ppermute x4, starting transfers between devices, body(): inward = lambda a: lax.ppermute(a, 'tensor', [(0, 1), (3, 2)])  31.7 us
    ppermute x8, waiting for transfers between devices, body(): outward = lambda a: lax.ppermute(a, 'tensor', [(1, 0), (2, 3)])  20.6 us
    ppermute x4, waiting for transfers between devices, body(): inward = lambda a: lax.ppermute(a, 'tensor', [(0, 1), (3, 2)])  10.8 us
    ppermute x8, starting transfers between devices, body(): outward = lambda a: lax.ppermute(a, 'tensor', [(1, 0), (2, 3)])  10.3 us
    pallas_call x4, Pallas kernels, finish(): pl.pallas_call(kernel, grid_spec=pltpu.PrefetchScalarGridSpec(num_scalar_...  9.81 us
    ppermute x6, starting transfers between devices, body(): cross = lambda a: lax.ppermute(a, 'tensor', [(1, 2), (2, 1)])  6.98 us
    unnamed x48, local copies, waits for them, and re-layouts  6.94 us
  transfers between devices with their start and end apart: 20, of which 5 were waited for; matrix products, arithmetic and copies ran while one was open for 3% of the time, Pallas kernels for 49%

profile of v5, /device:TPU:0, one launch (start us, length us, event | category | flops | bytes accessed | tf_op | source)
XLA Modules:
  0.0 227.7 jit_solution(13850812963214599765)
XLA Ops:
  6.5 3.0 %constant_dynamic-slice_fusion = bf16[448,2048]{1,0:T(8,128)(2,1)} fusion(bf16[8192,2048]{1,0:T(8,128)(2,1)} %refs_2_.1, s32[]{:T(128)S(6)} %select_n.20), kind=kLoop, calls=%fused_computation.9 | loop fusion | bytes 3670020 | tf_op jit(solution)/shard_map/dynamic_slice | solution.py:281
  10.9 6.3 %collective-permute-start = (bf16[448,2048]{1,0:T(8,128)(2,1)}, bf16[448,2048]{1,0:T(8,128)(2,1)}, u32[]{:S(2)}, u32[]{:S(2)}) collective-permute-start(bf16[448,2048]{1,0:T(8,128)(2,1)} %constant_dynamic-slice_fusion), channel_id=1, source_target_pairs={{0,1},{3,2},{4,5},{7,6},{8,9},{11,10},{12,13},{15,14},{16,17},{19,... | collective-permute-start | bytes 5505032 | tf_op jit(solution)/shard_map/ppermute | solution.py:273
  17.2 3.2 %norm_chunks.1 = (bf16[192,3584]{1,0:T(8,128)(2,1)S(1)}, bf16[192,3584]{1,0:T(8,128)(2,1)}, bf16[192,1024]{1,0:T(8,128)(2,1)S(1)}, bf16[192,2304]{1,0:T(8,128)(2,1)}, bf16[192,2304]{1,0:T(8,128)(2,1)}) custom-call(bf16[192,8192]{1,0:T(8,128)(2,1)S(1)} %copy-done.6, bf16[1,8192]{1,0:T(2,128)(2,1)S(1)} %broadcast_in_dim.19.g_ref), custom_call_target="tpu_custom_call" | custom-call | flops 1000 | bytes 1000 | tf_op jit(solution)/shard_map/norm_chunks/pallas_call | solution.py:53
  22.2 1.8 collective-permute-start.4
  25.3 16.9 %product.5.refs_0_ = f32[192,2048]{1,0:T(8,128)} custom-call(bf16[192,3584]{1,0:T(8,128)(2,1)} %copy-done.4, bf16[192,3584]{1,0:T(8,128)(2,1)} %get-tuple-element.45.refs_1_, bf16[192,1024]{1,0:T(8,128)(2,1)} %copy-done.7, bf16[8192,2048]{1,0:T(8,128)(2,1)} %refs_2_.1), custom_call_target="tpu_custom_call" | custom-call | flops 1000 | bytes 1000 | tf_op jit(solution)/shard_map/product/pallas_call | solution.py:188
  42.2 15.5 %collective-permute-done.2.refs_1_ = bf16[192,3584]{1,0:T(8,128)(2,1)S(1)} collective-permute-done((bf16[192,3584]{1,0:T(8,128)(2,1)}, bf16[192,3584]{1,0:T(8,128)(2,1)S(1)}, u32[]{:S(2)}, u32[]{:S(2)}) %collective-permute-start.2) | collective-permute-done | bytes 1376288 | tf_op jit(solution)/shard_map/ppermute | solution.py:274
  57.8 1.4 collective-permute-start.5
  61.3 9.0 %collective-permute-start.1 = (bf16[192,2304]{1,0:T(8,128)(2,1)}, bf16[192,2304]{1,0:T(8,128)(2,1)}, u32[]{:S(2)}, u32[]{:S(2)}) collective-permute-start(bf16[192,2304]{1,0:T(8,128)(2,1)} %get-tuple-element.44), channel_id=1, source_target_pairs={{0,1},{3,2},{4,5},{7,6},{8,9},{11,10},{12,13},{15,14},{16,17},{19,... | collective-permute-start | bytes 2654216 | tf_op jit(solution)/shard_map/ppermute | solution.py:273
  70.5 1.3 collective-permute-start.7
  71.9 2.8 %fusion = f32[192,256]{1,0:T(8,128)S(1)} fusion(bf16[192,3584]{1,0:T(8,128)(2,1)} %get-tuple-element.45.refs_1_, bf16[256,10240]{1,0:T(8,128)(2,1)} %all-gather.3.cloned.1.call-done.refs_2_.refs_3_.refs_5_.refs_9_), kind=kOutput, calls=%fused_computation | convolution fusion | flops 352321536 | bytes 3407872 | tf_op jit(solution)/shard_map/dot_general | solution.py:69
  74.7 2.4 %fusion.4 = f32[192,256]{1,0:T(8,128)S(1)} fusion(f32[192,256]{1,0:T(8,128)S(1)} %fusion, bf16[192,3584]{1,0:T(8,128)(2,1)S(1)} %copy-done.5, bf16[256,10240]{1,0:T(8,128)(2,1)} %all-gather.3.cloned.1.call-done.refs_2_.refs_3_.refs_5_.refs_9_), kind=kOutput, calls=%fused_computation.6 | convolution fusion | flops 352370688 | bytes 3604480 | tf_op jit(solution)/shard_map/dot_general | solution.py:69
  77.4 2.3 %finish.4.refs_7_ = bf16[768,2048]{1,0:T(8,128)(2,1)} custom-call(s32[1]{0:T(128)} %bitcast.1.row_ref, f32[192,2048]{1,0:T(8,128)S(1)} %copy-done.3, f32[192,256]{1,0:T(8,128)S(1)} %convolution_add_fusion.refs_1_, bf16[256,10240]{1,0:T(8,128)(2,1)S(1)} %copy-done, s32[1,256]{1,0:T(1,128)S(1)} %broadcast_in_dim_reshape.13.refs_3_.refs_4_, ...), custom_call_target="tpu_custom_call" | custom-call | flops 1000 | bytes 1000 | tf_op jit(solution)/shard_map/finish/pallas_call | solution.py:244
  79.7 7.0 %collective-permute-done.1.refs_0_ = bf16[192,2304]{1,0:T(8,128)(2,1)} collective-permute-done((bf16[192,2304]{1,0:T(8,128)(2,1)}, bf16[192,2304]{1,0:T(8,128)(2,1)}, u32[]{:S(2)}, u32[]{:S(2)}) %collective-permute-start.1) | collective-permute-done | bytes 884768 | tf_op jit(solution)/shard_map/ppermute | solution.py:273
  86.7 5.3 %collective-permute-start.6 = (bf16[192,2304]{1,0:T(8,128)(2,1)}, bf16[192,2304]{1,0:T(8,128)(2,1)}, u32[]{:S(2)}, u32[]{:S(2)}) collective-permute-start(bf16[192,2304]{1,0:T(8,128)(2,1)} %get-tuple-element.51), channel_id=1, source_target_pairs={{0,1},{3,2},{4,5},{7,6},{8,9},{11,10},{12,13},{15,14},{16,17},{19,... | collective-permute-start | bytes 2654216 | tf_op jit(solution)/shard_map/ppermute | solution.py:273
  92.1 1.6 collective-permute-start.10
  95.0 13.0 %product.6 = (f32[192,2048]{1,0:T(8,128)}, f32[192,256]{1,0:T(8,128)}) custom-call(bf16[192,3584]{1,0:T(8,128)(2,1)} %copy-done.14, bf16[8192,2048]{1,0:T(8,128)(2,1)} %refs_2_.1, bf16[256,10240]{1,0:T(8,128)(2,1)} %all-gather.3.cloned.1.call-done.refs_2_.refs_3_.refs_5_.refs_9_), custom_call_target="tpu_custom_call" | custom-call | flops 1000 | bytes 1000 | tf_op jit(solution)/shard_map/product/pallas_call | solution.py:188
  108.0 11.1 %collective-permute-start.9 = (bf16[192,3584]{1,0:T(8,128)(2,1)S(1)}, bf16[192,3584]{1,0:T(8,128)(2,1)}, u32[]{:S(2)}, u32[]{:S(2)}) collective-permute-start(bf16[192,3584]{1,0:T(8,128)(2,1)S(1)} %copy-done.5), channel_id=1, source_target_pairs={{0,1},{3,2},{4,5},{7,6},{8,9},{11,10},{12,13},{15,14},{16,17},{19,... | collective-permute-start | bytes 4128776 | tf_op jit(solution)/shard_map/ppermute | solution.py:273
  119.1 1.3 collective-permute-start.14
  121.1 14.2 %product.7 = (f32[192,2048]{1,0:T(8,128)}, f32[192,256]{1,0:T(8,128)}) custom-call(bf16[192,3584]{1,0:T(8,128)(2,1)} %collective-permute-done.4.refs_0_, bf16[192,3584]{1,0:T(8,128)(2,1)} %collective-permute-done.7.refs_1_, bf16[192,1024]{1,0:T(8,128)(2,1)} %collective-permute-done.5.refs_2_, bf16[192,1024]{1,0:T(8,128)(2,1)} %copy-done.20, ...), custom_call_target="tpu_custom_call" | custom-call | flops 1000 | bytes 1000 | tf_op jit(solution)/shard_map/product/pallas_call | solution.py:188
  135.3 4.8 %collective-permute-done.14.refs_5_ = bf16[192,2304]{1,0:T(8,128)(2,1)S(1)} collective-permute-done((bf16[192,2304]{1,0:T(8,128)(2,1)}, bf16[192,2304]{1,0:T(8,128)(2,1)S(1)}, u32[]{:S(2)}, u32[]{:S(2)}) %collective-permute-start.14) | collective-permute-done | bytes 884768 | tf_op jit(solution)/shard_map/ppermute | solution.py:274
  140.1 1.3 collective-permute-start.15
  141.4 3.8 %collective-permute-done.9.refs_0_ = bf16[192,3584]{1,0:T(8,128)(2,1)} collective-permute-done((bf16[192,3584]{1,0:T(8,128)(2,1)S(1)}, bf16[192,3584]{1,0:T(8,128)(2,1)}, u32[]{:S(2)}, u32[]{:S(2)}) %collective-permute-start.9) | collective-permute-done | bytes 1376288 | tf_op jit(solution)/shard_map/ppermute | solution.py:273
  146.9 14.0 %product_sent.2 = bf16[384,2176]{1,0:T(8,128)(2,1)} custom-call(bf16[192,3584]{1,0:T(8,128)(2,1)} %copy-done.4, bf16[192,3584]{1,0:T(8,128)(2,1)} %copy-done.14, bf16[3584,2048]{1,0:T(8,128)(2,1)} %all-gather.5.cloned.1.call-done.refs_2_.refs_1_, bf16[256,10240]{1,0:T(8,128)(2,1)} %all-gather.3.cloned.1.call-done.refs_2_.refs_3_.refs_5_.refs_9_, ...), custom_call_target="tpu_custom_call" | custom-call | flops 1000 | bytes 1000 | tf_op jit(solution)/shard_map/product_sent/pallas_call | solution.py:188
  163.3 17.5 %product.8 = (f32[384,2048]{1,0:T(8,128)}, f32[384,256]{1,0:T(8,128)}) custom-call(bf16[192,2304]{1,0:T(8,128)(2,1)} %collective-permute-done.1.refs_0_, bf16[192,3584]{1,0:T(8,128)(2,1)} %copy-done.16, bf16[192,2304]{1,0:T(8,128)(2,1)} %collective-permute-done.6.refs_2_, bf16[192,1024]{1,0:T(8,128)(2,1)} %collective-permute-done.3.refs_3_, ...), custom_call_target="tpu_custom_call" | custom-call | flops 1000 | bytes 1000 | tf_op jit(solution)/shard_map/product/pallas_call | solution.py:188
  182.0 11.4 %product_sent.3 = bf16[192,2176]{1,0:T(8,128)(2,1)} custom-call(bf16[192,3584]{1,0:T(8,128)(2,1)} %copy-done.15, bf16[3584,2048]{1,0:T(8,128)(2,1)} %all-gather.5.cloned.1.call-done.refs_2_.refs_1_, bf16[256,10240]{1,0:T(8,128)(2,1)} %all-gather.3.cloned.1.call-done.refs_2_.refs_3_.refs_5_.refs_9_, s32[1,256]{1,0:T(1,128)} %copy-done.12, s32[192,1]{1,0:T(8,128)} %copy.19.refs_4_), custom_call_target="tpu_custom_call" | custom-call | flops 1000 | bytes 1000 | tf_op jit(solution)/shard_map/product_sent/pallas_call | solution.py:188
  193.4 1.3 collective-permute-start.16
  194.7 14.8 %product.9 = (f32[384,2048]{1,0:T(8,128)}, f32[384,256]{1,0:T(8,128)}) custom-call(bf16[192,3584]{1,0:T(8,128)(2,1)} %collective-permute-done.9.refs_0_, bf16[192,3584]{1,0:T(8,128)(2,1)} %copy-done.15, bf16[8192,2048]{1,0:T(8,128)(2,1)} %refs_2_.1, bf16[256,10240]{1,0:T(8,128)(2,1)} %all-gather.3.cloned.1.call-done.refs_2_.refs_3_.refs_5_.refs_9_, ...), custom_call_target="tpu_custom_call" | custom-call | flops 1000 | bytes 1000 | tf_op jit(solution)/shard_map/product/pallas_call | solution.py:188
  209.5 2.5 %copy-done.1 = bf16[256,10240]{1,0:T(8,128)(2,1)S(1)} copy-done((bf16[256,10240]{1,0:T(8,128)(2,1)S(1)}, bf16[256,10240]{1,0:T(8,128)(2,1)}, u32[]{:S(2)}) %copy-start.1) | copy-done | bytes 5242904
  212.0 1.4 copy-done.9
  213.4 2.5 %finish.5.refs_7_ = bf16[768,2048]{1,0:T(8,128)(2,1)} custom-call(s32[1]{0:T(128)} %bitcast.9.row_ref, f32[192,2048]{1,0:T(8,128)S(1)} %copy-done.9, f32[192,256]{1,0:T(8,128)S(1)} %copy-done.11, bf16[256,10240]{1,0:T(8,128)(2,1)S(1)} %copy-done.1, s32[1,256]{1,0:T(1,128)S(1)} %copy-done.13, ...), custom_call_target="tpu_custom_call", output_to_operand_aliasing={{}: (8, {})} | custom-call | flops 1000 | bytes 1000 | tf_op jit(solution)/shard_map/finish/pallas_call | solution.py:244
  215.9 2.5 %finish.6.refs_7_ = bf16[768,2048]{1,0:T(8,128)(2,1)} custom-call(s32[1]{0:T(128)} %bitcast.8.row_ref, f32[384,2048]{1,0:T(8,128)S(1)} %copy-done.2, f32[384,256]{1,0:T(8,128)S(1)} %copy-done.10, bf16[256,10240]{1,0:T(8,128)(2,1)S(1)} %copy-done.1, s32[1,256]{1,0:T(1,128)S(1)} %copy-done.13, ...), custom_call_target="tpu_custom_call", output_to_operand_aliasing={{}: (8, {})} | custom-call | flops 1000 | bytes 1000 | tf_op jit(solution)/shard_map/finish/pallas_call | solution.py:244
  218.4 2.5 %finish.7 = bf16[768,2048]{1,0:T(8,128)(2,1)} custom-call(s32[1]{0:T(128)} %bitcast.row_ref, f32[384,2048]{1,0:T(8,128)S(1)} %copy-done.2, f32[384,256]{1,0:T(8,128)S(1)} %copy-done.10, bf16[256,10240]{1,0:T(8,128)(2,1)S(1)} %copy-done.1, s32[1,256]{1,0:T(1,128)S(1)} %copy-done.13, ...), custom_call_target="tpu_custom_call", output_to_operand_aliasing={{}: (8, {})} | custom-call | flops 1000 | bytes 1000 | tf_op jit(solution)/shard_map/finish/pallas_call | solution.py:244
  (83 shorter events, 14.3 us)
Async XLA Ops:
  6.5 65.3 %all-gather.3.cloned.1.call-start = ((), (), s32[]{:S(2)}) async-start(), calls=%async_computation | async-start | bytes 6553600 | tf_op jit(solution)/shard_map/all_gather | solution.py:286
  6.5 3.0 %copy-start.21 = (bf16[1,64,2048]{2,1,0:T(8,128)(2,1)S(1)}, bf16[1,64,2048]{2,1,0:T(8,128)(2,1)}, u32[]{:S(2)}) copy-start(bf16[1,64,2048]{2,1,0:T(8,128)(2,1)} %param.10) | copy-start | bytes 786436
  9.6 7.6 %copy-start.22 = (bf16[8192]{0:T(1024)(128)(2,1)S(1)}, bf16[8192]{0:T(1024)(128)(2,1)}, u32[]{:S(2)}) copy-start(bf16[8192]{0:T(1024)(128)(2,1)} %param.7) | copy-start | bytes 49156
  9.6 7.6 %copy-start.6 = (bf16[192,8192]{1,0:T(8,128)(2,1)S(1)}, bf16[192,8192]{1,0:T(8,128)(2,1)}, u32[]{:S(2)}) copy-start(bf16[192,8192]{1,0:T(8,128)(2,1)} %x_ref) | copy-start | bytes 9437188
  10.8 136.1 %all-gather.5.cloned.1.call-start = ((), (), s32[]{:S(2)}) async-start(), calls=%async_computation.1 | async-start | bytes 16515072 | tf_op jit(solution)/shard_map/all_gather | solution.py:326
  10.9 46.9 %collective-permute-start = (bf16[448,2048]{1,0:T(8,128)(2,1)}, bf16[448,2048]{1,0:T(8,128)(2,1)}, u32[]{:S(2)}, u32[]{:S(2)}) collective-permute-start(bf16[448,2048]{1,0:T(8,128)(2,1)} %constant_dynamic-slice_fusion), channel_id=1, source_target_pairs={{0,1},{3,2},{4,5},{7,6},{8,9},{11,10},{12,13},{15,14},{16,17},{19,... | collective-permute-start | bytes 5505032 | tf_op jit(solution)/shard_map/ppermute | solution.py:273
  22.2 20.0 %collective-permute-start.4 = (bf16[192,3584]{1,0:T(8,128)(2,1)}, bf16[192,3584]{1,0:T(8,128)(2,1)}, u32[]{:S(2)}, u32[]{:S(2)}) collective-permute-start(bf16[192,3584]{1,0:T(8,128)(2,1)} %get-tuple-element.45.refs_1_), channel_id=1, source_target_pairs={{1,2},{2,1},{5,6},{6,5},{9,10},{10,9},{13,14},{14,13},{17,18},{18,... | collective-permute-start | bytes 4128776 | tf_op jit(solution)/shard_map/ppermute | solution.py:275
  24.0 33.7 %collective-permute-start.2 = (bf16[192,3584]{1,0:T(8,128)(2,1)}, bf16[192,3584]{1,0:T(8,128)(2,1)S(1)}, u32[]{:S(2)}, u32[]{:S(2)}) collective-permute-start(bf16[192,3584]{1,0:T(8,128)(2,1)} %get-tuple-element.45.refs_1_), channel_id=1, source_target_pairs={{1,0},{2,3},{5,4},{6,7},{9,8},{10,11},{13,12},{14,15},{17,16},{18,... | collective-permute-start | bytes 4128776 | tf_op jit(solution)/shard_map/ppermute | solution.py:274
  42.2 15.6 %copy-start.8 = (bf16[192,1024]{1,0:T(8,128)(2,1)S(1)}, bf16[192,1024]{1,0:T(8,128)(2,1)}, u32[]{:S(2)}) copy-start(bf16[192,1024]{1,0:T(8,128)(2,1)} %copy-done.7) | copy-start | bytes 1179652
  42.2 18.3 %copy-start.5 = (bf16[192,3584]{1,0:T(8,128)(2,1)S(1)}, bf16[192,3584]{1,0:T(8,128)(2,1)}, u32[]{:S(2)}) copy-start(bf16[192,3584]{1,0:T(8,128)(2,1)} %copy-done.4) | copy-start | bytes 4128772
  42.2 28.1 %copy-start.23 = (s32[768]{0:T(1024)S(1)}, s32[768]{0:T(1024)}, u32[]{:S(2)}) copy-start(s32[768]{0:T(1024)} %param.11) | copy-start | bytes 9220
  57.8 14.0 %collective-permute-start.5 = (bf16[192,1024]{1,0:T(8,128)(2,1)S(1)}, bf16[192,1024]{1,0:T(8,128)(2,1)}, u32[]{:S(2)}, u32[]{:S(2)}) collective-permute-start(bf16[192,1024]{1,0:T(8,128)(2,1)S(1)} %copy-done.8), channel_id=1, source_target_pairs={{1,2},{2,1},{5,6},{6,5},{9,10},{10,9},{13,14},{14,13},{17,18},{18,... | collective-permute-start | bytes 1179656 | tf_op jit(solution)/shard_map/ppermute | solution.py:275
  59.2 12.6 %collective-permute-start.3 = (bf16[192,1024]{1,0:T(8,128)(2,1)S(1)}, bf16[192,1024]{1,0:T(8,128)(2,1)}, u32[]{:S(2)}, u32[]{:S(2)}) collective-permute-start(bf16[192,1024]{1,0:T(8,128)(2,1)S(1)} %copy-done.8), channel_id=1, source_target_pairs={{1,0},{2,3},{5,4},{6,7},{9,8},{10,11},{13,12},{14,15},{17,16},{18,... | collective-permute-start | bytes 1179656 | tf_op jit(solution)/shard_map/ppermute | solution.py:274
  60.5 31.6 %collective-permute-start.8 = (bf16[192,3584]{1,0:T(8,128)(2,1)S(1)}, bf16[192,3584]{1,0:T(8,128)(2,1)S(1)}, u32[]{:S(2)}, u32[]{:S(2)}) collective-permute-start(bf16[192,3584]{1,0:T(8,128)(2,1)S(1)} %copy-done.5), channel_id=1, source_target_pairs={{1,2},{2,1},{5,6},{6,5},{9,10},{10,9},{13,14},{14,13},{17,18},{18,... | collective-permute-start | bytes 4128776 | tf_op jit(solution)/shard_map/ppermute | solution.py:275
  61.3 25.5 %collective-permute-start.1 = (bf16[192,2304]{1,0:T(8,128)(2,1)}, bf16[192,2304]{1,0:T(8,128)(2,1)}, u32[]{:S(2)}, u32[]{:S(2)}) collective-permute-start(bf16[192,2304]{1,0:T(8,128)(2,1)} %get-tuple-element.44), channel_id=1, source_target_pairs={{0,1},{3,2},{4,5},{7,6},{8,9},{11,10},{12,13},{15,14},{16,17},{19,... | collective-permute-start | bytes 2654216 | tf_op jit(solution)/shard_map/ppermute | solution.py:273
  70.3 7.1 %copy-start.12 = (s32[1,256]{1,0:T(1,128)}, s32[1,256]{1,0:T(1,128)S(1)}, u32[]{:S(2)}) copy-start(s32[1,256]{1,0:T(1,128)S(1)} %broadcast_in_dim_reshape.13.refs_3_.refs_4_) | copy-start | bytes 3076
  70.5 37.5 %collective-permute-start.7 = (bf16[192,3584]{1,0:T(8,128)(2,1)}, bf16[192,3584]{1,0:T(8,128)(2,1)}, u32[]{:S(2)}, u32[]{:S(2)}) collective-permute-start(bf16[192,3584]{1,0:T(8,128)(2,1)} %collective-permute-done.4.refs_0_), channel_id=1, source_target_pairs={{1,0},{2,3},{5,4},{6,7},{9,8},{10,11},{13,12},{14,15},{17,16},{18,... | collective-permute-start | bytes 4128776 | tf_op jit(solution)/shard_map/ppermute | solution.py:274
  71.8 5.2 %copy-start = (bf16[256,10240]{1,0:T(8,128)(2,1)S(1)}, bf16[256,10240]{1,0:T(8,128)(2,1)}, u32[]{:S(2)}) copy-start(bf16[256,10240]{1,0:T(8,128)(2,1)} %all-gather.3.cloned.1.call-done.refs_2_.refs_3_.refs_5_.refs_9_) | copy-start | bytes 15728644
  86.7 21.2 %collective-permute-start.6 = (bf16[192,2304]{1,0:T(8,128)(2,1)}, bf16[192,2304]{1,0:T(8,128)(2,1)}, u32[]{:S(2)}, u32[]{:S(2)}) collective-permute-start(bf16[192,2304]{1,0:T(8,128)(2,1)} %get-tuple-element.51), channel_id=1, source_target_pairs={{0,1},{3,2},{4,5},{7,6},{8,9},{11,10},{12,13},{15,14},{16,17},{19,... | collective-permute-start | bytes 2654216 | tf_op jit(solution)/shard_map/ppermute | solution.py:273
  92.1 27.0 %collective-permute-start.10 = (bf16[192,2304]{1,0:T(8,128)(2,1)}, bf16[192,2304]{1,0:T(8,128)(2,1)}, u32[]{:S(2)}, u32[]{:S(2)}) collective-permute-start(bf16[192,2304]{1,0:T(8,128)(2,1)} %collective-permute-done.1.refs_0_), channel_id=1, source_target_pairs={{1,2},{2,1},{5,6},{6,5},{9,10},{10,9},{13,14},{14,13},{17,18},{18,... | collective-permute-start | bytes 2654216 | tf_op jit(solution)/shard_map/ppermute | solution.py:275
  93.7 25.4 %collective-permute-start.13 = (bf16[192,1024]{1,0:T(8,128)(2,1)}, bf16[192,1024]{1,0:T(8,128)(2,1)S(1)}, u32[]{:S(2)}, u32[]{:S(2)}) collective-permute-start(bf16[192,1024]{1,0:T(8,128)(2,1)} %collective-permute-done.5.refs_2_), channel_id=1, source_target_pairs={{1,0},{2,3},{5,4},{6,7},{9,8},{10,11},{13,12},{14,15},{17,16},{18,... | collective-permute-start | bytes 1179656 | tf_op jit(solution)/shard_map/ppermute | solution.py:274
  108.0 37.2 %collective-permute-start.9 = (bf16[192,3584]{1,0:T(8,128)(2,1)S(1)}, bf16[192,3584]{1,0:T(8,128)(2,1)}, u32[]{:S(2)}, u32[]{:S(2)}) collective-permute-start(bf16[192,3584]{1,0:T(8,128)(2,1)S(1)} %copy-done.5), channel_id=1, source_target_pairs={{0,1},{3,2},{4,5},{7,6},{8,9},{11,10},{12,13},{15,14},{16,17},{19,... | collective-permute-start | bytes 4128776 | tf_op jit(solution)/shard_map/ppermute | solution.py:273
  119.1 21.0 %collective-permute-start.14 = (bf16[192,2304]{1,0:T(8,128)(2,1)}, bf16[192,2304]{1,0:T(8,128)(2,1)S(1)}, u32[]{:S(2)}, u32[]{:S(2)}) collective-permute-start(bf16[192,2304]{1,0:T(8,128)(2,1)} %collective-permute-done.10.refs_4_), channel_id=1, source_target_pairs={{1,0},{2,3},{5,4},{6,7},{9,8},{10,11},{13,12},{14,15},{17,16},{18,... | collective-permute-start | bytes 2654216 | tf_op jit(solution)/shard_map/ppermute | solution.py:274
  120.4 19.7 %collective-permute-start.11 = (bf16[192,2304]{1,0:T(8,128)(2,1)}, bf16[192,2304]{1,0:T(8,128)(2,1)S(1)}, u32[]{:S(2)}, u32[]{:S(2)}) collective-permute-start(bf16[192,2304]{1,0:T(8,128)(2,1)} %collective-permute-done.6.refs_2_), channel_id=1, source_target_pairs={{1,2},{2,1},{5,6},{6,5},{9,10},{10,9},{13,14},{14,13},{17,18},{18,... | collective-permute-start | bytes 2654216 | tf_op jit(solution)/shard_map/ppermute | solution.py:275
  140.1 20.9 %copy-start.18 = (bf16[192,2304]{1,0:T(8,128)(2,1)}, bf16[192,2304]{1,0:T(8,128)(2,1)S(1)}, u32[]{:S(2)}) copy-start(bf16[192,2304]{1,0:T(8,128)(2,1)S(1)} %collective-permute-done.14.refs_5_) | copy-start | bytes 2654212
  140.1 20.9 %copy-start.19 = (bf16[192,2304]{1,0:T(8,128)(2,1)}, bf16[192,2304]{1,0:T(8,128)(2,1)S(1)}, u32[]{:S(2)}) copy-start(bf16[192,2304]{1,0:T(8,128)(2,1)S(1)} %collective-permute-done.11.refs_6_) | copy-start | bytes 2654212
  140.1 21.1 %collective-permute-start.15 = (bf16[192,2304]{1,0:T(8,128)(2,1)S(1)}, bf16[192,2304]{1,0:T(8,128)(2,1)}, u32[]{:S(2)}, u32[]{:S(2)}) collective-permute-start(bf16[192,2304]{1,0:T(8,128)(2,1)S(1)} %collective-permute-done.11.refs_6_), channel_id=1, source_target_pairs={{1,0},{2,3},{5,4},{6,7},{9,8},{10,11},{13,12},{14,15},{17,16},{18,... | collective-permute-start | bytes 2654216 | tf_op jit(solution)/shard_map/ppermute | solution.py:274
  145.2 35.6 %collective-permute-start.12 = (bf16[192,3584]{1,0:T(8,128)(2,1)}, bf16[192,3584]{1,0:T(8,128)(2,1)S(1)}, u32[]{:S(2)}, u32[]{:S(2)}) collective-permute-start(bf16[192,3584]{1,0:T(8,128)(2,1)} %collective-permute-done.9.refs_0_), channel_id=1, source_target_pairs={{1,2},{2,1},{5,6},{6,5},{9,10},{10,9},{13,14},{14,13},{17,18},{18,... | collective-permute-start | bytes 4128776 | tf_op jit(solution)/shard_map/ppermute | solution.py:275
  161.2 48.2 %collective-permute-start.17 = (bf16[384,2176]{1,0:T(8,128)(2,1)}, bf16[384,2176]{1,0:T(8,128)(2,1)S(1)}, u32[]{:S(2)}, u32[]{:S(2)}) collective-permute-start(bf16[384,2176]{1,0:T(8,128)(2,1)} %product_sent.2), channel_id=1, source_target_pairs={{1,0},{2,3},{5,4},{6,7},{9,8},{10,11},{13,12},{14,15},{17,16},{18,... | collective-permute-start | bytes 5013512 | tf_op jit(solution)/shard_map/ppermute | solution.py:274
  193.4 25.0 %collective-permute-start.16 = (bf16[192,2176]{1,0:T(8,128)(2,1)}, bf16[192,2176]{1,0:T(8,128)(2,1)S(1)}, u32[]{:S(2)}, u32[]{:S(2)}) collective-permute-start(bf16[192,2176]{1,0:T(8,128)(2,1)} %product_sent.3), channel_id=1, source_target_pairs={{1,0},{2,3},{5,4},{6,7},{9,8},{10,11},{13,12},{14,15},{17,16},{18,... | collective-permute-start | bytes 2506760 | tf_op jit(solution)/shard_map/ppermute | solution.py:274
  194.7 14.8 %copy-start.11 = (f32[192,256]{1,0:T(8,128)S(1)}, f32[192,256]{1,0:T(8,128)}, u32[]{:S(2)}) copy-start(f32[192,256]{1,0:T(8,128)} %get-tuple-element.74.refs_1_) | copy-start | bytes 589828
  194.7 14.8 %copy-start.13 = (s32[1,256]{1,0:T(1,128)S(1)}, s32[1,256]{1,0:T(1,128)}, u32[]{:S(2)}) copy-start(s32[1,256]{1,0:T(1,128)} %copy-done.12) | copy-start | bytes 3076
  (12 other events, 24.0 us)
Sparse Core Ops, SparseCore 0:
  10.9 43.1 all-gather.2
  57.9 81.1 all-gather.4

commit v6 on v5

--- a/solution.py
+++ b/solution.py
@@ -7,7 +7,7 @@
 
 adapter_scale = 2.0
 lanes = 128
-vmem = 60 * 1024 * 1024
+vmem = 56 * 1024 * 1024
 f32 = jnp.float32
 bf16 = jnp.bfloat16
 

time: 230 us -> 229 us (level)
    unnamed x48 -> x58, local copies, waits for them, and re-layouts: 6.94 us -> 6.12 us
  transfers between devices with their start and end apart: 20 -> 20, of which waited for: 5 -> 6; matrix products, arithmetic and copies ran while one was open for 3% -> 3% of each run, Pallas kernels for 49% -> 50%
where the time goes in v6:
time: 229 us; the launch traced here: 227 us
  Pallas kernels  115 us (50%)
  starting transfers between devices  47.7 us (21%)
  waiting for transfers between devices  32.6 us (14%)
  between operations  13.9 us (6%)
  local copies, waits for them, and re-layouts  11.1 us (5%)
  matrix products  5.49 us (2%)
    pallas_call x7, Pallas kernels, product(): pl.pallas_call(kernel, grid=(tiles,), in_specs=in_specs, out_specs=out_sp...  102 us
    ppermute x4, starting transfers between devices, body(): inward = lambda a: lax.ppermute(a, 'tensor', [(0, 1), (3, 2)])  30.3 us
    ppermute x8, waiting for transfers between devices, body(): outward = lambda a: lax.ppermute(a, 'tensor', [(1, 0), (2, 3)])  20.8 us
    ppermute x4, waiting for transfers between devices, body(): inward = lambda a: lax.ppermute(a, 'tensor', [(0, 1), (3, 2)])  11.8 us
    ppermute x8, starting transfers between devices, body(): outward = lambda a: lax.ppermute(a, 'tensor', [(1, 0), (2, 3)])  10.3 us
    pallas_call x4, Pallas kernels, finish(): pl.pallas_call(kernel, grid_spec=pltpu.PrefetchScalarGridSpec(num_scalar_...  9.81 us
    ppermute x6, starting transfers between devices, body(): cross = lambda a: lax.ppermute(a, 'tensor', [(1, 2), (2, 1)])  7.11 us
    unnamed x58, local copies, waits for them, and re-layouts  6.12 us
  transfers between devices with their start and end apart: 20, of which 6 were waited for; matrix products, arithmetic and copies ran while one was open for 3% of the time, Pallas kernels for 50%

profile of v6, /device:TPU:0, one launch (start us, length us, event | category | flops | bytes accessed | tf_op | source)
XLA Modules:
  0.0 227.3 jit_solution(15849341164842954390)
XLA Ops:
  6.5 3.0 %constant_dynamic-slice_fusion = bf16[448,2048]{1,0:T(8,128)(2,1)} fusion(bf16[8192,2048]{1,0:T(8,128)(2,1)} %refs_2_.1, s32[]{:T(128)S(6)} %select_n.20), kind=kLoop, calls=%fused_computation.9 | loop fusion | bytes 3670020 | tf_op jit(solution)/shard_map/dynamic_slice | solution.py:281
  10.9 6.3 %collective-permute-start = (bf16[448,2048]{1,0:T(8,128)(2,1)}, bf16[448,2048]{1,0:T(8,128)(2,1)}, u32[]{:S(2)}, u32[]{:S(2)}) collective-permute-start(bf16[448,2048]{1,0:T(8,128)(2,1)} %constant_dynamic-slice_fusion), channel_id=1, source_target_pairs={{0,1},{3,2},{4,5},{7,6},{8,9},{11,10},{12,13},{15,14},{16,17},{19,... | collective-permute-start | bytes 5505032 | tf_op jit(solution)/shard_map/ppermute | solution.py:273
  17.2 3.2 %norm_chunks.1 = (bf16[192,3584]{1,0:T(8,128)(2,1)}, bf16[192,3584]{1,0:T(8,128)(2,1)S(1)}, bf16[192,1024]{1,0:T(8,128)(2,1)S(1)}, bf16[192,2304]{1,0:T(8,128)(2,1)S(1)}, bf16[192,2304]{1,0:T(8,128)(2,1)}) custom-call(bf16[192,8192]{1,0:T(8,128)(2,1)S(1)} %copy-done.3, bf16[1,8192]{1,0:T(2,128)(2,1)S(1)} %broadcast_in_dim.19.g_ref), custom_call_target="tpu_custom_call" | custom-call | flops 1000 | bytes 1000 | tf_op jit(solution)/shard_map/norm_chunks/pallas_call | solution.py:53
  22.8 1.3 collective-permute-start.2
  24.1 16.8 %product.5.refs_0_ = f32[192,2048]{1,0:T(8,128)} custom-call(bf16[192,3584]{1,0:T(8,128)(2,1)} %get-tuple-element.55.refs_0_, bf16[192,3584]{1,0:T(8,128)(2,1)} %copy-done.8, bf16[192,1024]{1,0:T(8,128)(2,1)} %copy-done.4, bf16[8192,2048]{1,0:T(8,128)(2,1)} %refs_2_.1), custom_call_target="tpu_custom_call" | custom-call | flops 1000 | bytes 1000 | tf_op jit(solution)/shard_map/product/pallas_call | solution.py:188
  41.0 15.4 %collective-permute-done.2.refs_1_ = bf16[192,3584]{1,0:T(8,128)(2,1)S(1)} collective-permute-done((bf16[192,3584]{1,0:T(8,128)(2,1)S(1)}, bf16[192,3584]{1,0:T(8,128)(2,1)S(1)}, u32[]{:S(2)}, u32[]{:S(2)}) %collective-permute-start.2) | collective-permute-done | bytes 1376288 | tf_op jit(solution)/shard_map/ppermute | solution.py:274
  57.5 1.4 collective-permute-start.5
  60.2 1.8 collective-permute-start.8
  61.9 7.2 %collective-permute-start.1 = (bf16[192,2304]{1,0:T(8,128)(2,1)}, bf16[192,2304]{1,0:T(8,128)(2,1)}, u32[]{:S(2)}, u32[]{:S(2)}) collective-permute-start(bf16[192,2304]{1,0:T(8,128)(2,1)} %copy-done.13), channel_id=1, source_target_pairs={{0,1},{3,2},{4,5},{7,6},{8,9},{11,10},{12,13},{15,14},{16,17},{19,... | collective-permute-start | bytes 2654216 | tf_op jit(solution)/shard_map/ppermute | solution.py:273
  69.4 1.3 collective-permute-start.7
  70.8 2.4 %fusion = f32[192,256]{1,0:T(8,128)S(1)} fusion(bf16[192,3584]{1,0:T(8,128)(2,1)S(1)} %copy-done.9, bf16[256,10240]{1,0:T(8,128)(2,1)} %all-gather.3.cloned.1.call-done.refs_2_.refs_3_.refs_5_.refs_9_), kind=kOutput, calls=%fused_computation | convolution fusion | flops 352321536 | bytes 3407872 | tf_op jit(solution)/shard_map/dot_general | solution.py:69
  73.2 2.8 %fusion.4 = f32[192,256]{1,0:T(8,128)S(1)} fusion(f32[192,256]{1,0:T(8,128)S(1)} %fusion, bf16[192,3584]{1,0:T(8,128)(2,1)} %get-tuple-element.55.refs_0_, bf16[256,10240]{1,0:T(8,128)(2,1)} %all-gather.3.cloned.1.call-done.refs_2_.refs_3_.refs_5_.refs_9_), kind=kOutput, calls=%fused_computation.6 | convolution fusion | flops 352370688 | bytes 3604480 | tf_op jit(solution)/shard_map/dot_general | solution.py:69
  76.4 2.3 %finish.4.refs_7_ = bf16[768,2048]{1,0:T(8,128)(2,1)} custom-call(s32[1]{0:T(128)} %bitcast.1.row_ref, f32[192,2048]{1,0:T(8,128)S(1)} %copy-done.2, f32[192,256]{1,0:T(8,128)S(1)} %convolution_add_fusion.refs_1_, bf16[256,10240]{1,0:T(8,128)(2,1)S(1)} %copy-done, s32[1,256]{1,0:T(1,128)S(1)} %broadcast_in_dim_reshape.13.refs_3_.refs_4_, ...), custom_call_target="tpu_custom_call" | custom-call | flops 1000 | bytes 1000 | tf_op jit(solution)/shard_map/finish/pallas_call | solution.py:244
  78.7 7.0 %collective-permute-done.1.refs_0_ = bf16[192,2304]{1,0:T(8,128)(2,1)} collective-permute-done((bf16[192,2304]{1,0:T(8,128)(2,1)}, bf16[192,2304]{1,0:T(8,128)(2,1)}, u32[]{:S(2)}, u32[]{:S(2)}) %collective-permute-start.1) | collective-permute-done | bytes 884768 | tf_op jit(solution)/shard_map/ppermute | solution.py:273
  85.7 4.4 %collective-permute-start.6 = (bf16[192,2304]{1,0:T(8,128)(2,1)}, bf16[192,2304]{1,0:T(8,128)(2,1)S(1)}, u32[]{:S(2)}, u32[]{:S(2)}) collective-permute-start(bf16[192,2304]{1,0:T(8,128)(2,1)} %get-tuple-element.51), channel_id=1, source_target_pairs={{0,1},{3,2},{4,5},{7,6},{8,9},{11,10},{12,13},{15,14},{16,17},{19,... | collective-permute-start | bytes 2654216 | tf_op jit(solution)/shard_map/ppermute | solution.py:273
  90.9 1.3 collective-permute-start.13
  92.2 13.1 %product.6 = (f32[192,2048]{1,0:T(8,128)}, f32[192,256]{1,0:T(8,128)}) custom-call(bf16[192,3584]{1,0:T(8,128)(2,1)} %collective-permute-done.8.refs_0_.refs_1_, bf16[8192,2048]{1,0:T(8,128)(2,1)} %refs_2_.1, bf16[256,10240]{1,0:T(8,128)(2,1)} %all-gather.3.cloned.1.call-done.refs_2_.refs_3_.refs_5_.refs_9_), custom_call_target="tpu_custom_call" | custom-call | flops 1000 | bytes 1000 | tf_op jit(solution)/shard_map/product/pallas_call | solution.py:188
  105.2 1.4 collective-permute-done.6.refs_2_
  106.6 12.3 %collective-permute-start.9 = (bf16[192,3584]{1,0:T(8,128)(2,1)}, bf16[192,3584]{1,0:T(8,128)(2,1)}, u32[]{:S(2)}, u32[]{:S(2)}) collective-permute-start(bf16[192,3584]{1,0:T(8,128)(2,1)} %get-tuple-element.55.refs_0_), channel_id=1, source_target_pairs={{0,1},{3,2},{4,5},{7,6},{8,9},{11,10},{12,13},{15,14},{16,17},{19,... | collective-permute-start | bytes 4128776 | tf_op jit(solution)/shard_map/ppermute | solution.py:273
  120.9 14.0 %product.7 = (f32[192,2048]{1,0:T(8,128)}, f32[192,256]{1,0:T(8,128)}) custom-call(bf16[192,3584]{1,0:T(8,128)(2,1)} %copy-done.15, bf16[192,3584]{1,0:T(8,128)(2,1)} %collective-permute-done.7.refs_1_, bf16[192,1024]{1,0:T(8,128)(2,1)} %collective-permute-done.5.refs_2_, bf16[192,1024]{1,0:T(8,128)(2,1)} %copy-done.23, bf16[8192,2048]{1,0:T(8,128)(2,1)} %refs_2_.1, ...), custom_call_target="tpu_custom_call" | custom-call | flops 1000 | bytes 1000 | tf_op jit(solution)/shard_map/product/pallas_call | solution.py:188
  135.0 4.8 %collective-permute-done.14.refs_5_ = bf16[192,2304]{1,0:T(8,128)(2,1)S(1)} collective-permute-done((bf16[192,2304]{1,0:T(8,128)(2,1)S(1)}, bf16[192,2304]{1,0:T(8,128)(2,1)S(1)}, u32[]{:S(2)}, u32[]{:S(2)}) %collective-permute-start.14) | collective-permute-done | bytes 884768 | tf_op jit(solution)/shard_map/ppermute | solution.py:274
  142.1 3.4 %collective-permute-done.9.refs_0_ = bf16[192,3584]{1,0:T(8,128)(2,1)} collective-permute-done((bf16[192,3584]{1,0:T(8,128)(2,1)}, bf16[192,3584]{1,0:T(8,128)(2,1)}, u32[]{:S(2)}, u32[]{:S(2)}) %collective-permute-start.9) | collective-permute-done | bytes 1376288 | tf_op jit(solution)/shard_map/ppermute | solution.py:273
  145.5 1.8 collective-permute-start.12
  148.2 14.0 %product_sent.2 = bf16[384,2176]{1,0:T(8,128)(2,1)} custom-call(bf16[192,3584]{1,0:T(8,128)(2,1)} %get-tuple-element.55.refs_0_, bf16[192,3584]{1,0:T(8,128)(2,1)} %collective-permute-done.8.refs_0_.refs_1_, bf16[3584,2048]{1,0:T(8,128)(2,1)} %all-gather.5.cloned.1.call-done.refs_2_.refs_1_, ...), custom_call_target="tpu_custom_call" | custom-call | flops 1000 | bytes 1000 | tf_op jit(solution)/shard_map/product_sent/pallas_call | solution.py:188
  162.3 1.3 collective-permute-start.17
  164.4 17.5 %product.8 = (f32[384,2048]{1,0:T(8,128)}, f32[384,256]{1,0:T(8,128)}) custom-call(bf16[192,2304]{1,0:T(8,128)(2,1)} %collective-permute-done.1.refs_0_, bf16[192,3584]{1,0:T(8,128)(2,1)} %copy-done.14, bf16[192,2304]{1,0:T(8,128)(2,1)} %copy-done.17, bf16[192,1024]{1,0:T(8,128)(2,1)} %copy-done.22, bf16[192,2304]{1,0:T(8,128)(2,1)} %copy-done.18, ...), custom_call_target="tpu_custom_call" | custom-call | flops 1000 | bytes 1000 | tf_op jit(solution)/shard_map/product/pallas_call | solution.py:188
  181.9 11.4 %product_sent.3 = bf16[192,2176]{1,0:T(8,128)(2,1)} custom-call(bf16[192,3584]{1,0:T(8,128)(2,1)} %collective-permute-done.12.refs_0_.refs_1_, bf16[3584,2048]{1,0:T(8,128)(2,1)} %all-gather.5.cloned.1.call-done.refs_2_.refs_1_, bf16[256,10240]{1,0:T(8,128)(2,1)} %all-gather.3.cloned.1.call-done.refs_2_.refs_3_.refs_5_.refs_9_, s32[1,256]{1,0:T(1,128)} %copy-done.11, ...), custom_call_target="tpu_custom_call" | custom-call | flops 1000 | bytes 1000 | tf_op jit(solution)/shard_map/product_sent/pallas_call | solution.py:188
  194.7 15.4 %product.9 = (f32[384,2048]{1,0:T(8,128)}, f32[384,256]{1,0:T(8,128)}) custom-call(bf16[192,3584]{1,0:T(8,128)(2,1)} %collective-permute-done.9.refs_0_, bf16[192,3584]{1,0:T(8,128)(2,1)} %collective-permute-done.12.refs_0_.refs_1_, bf16[8192,2048]{1,0:T(8,128)(2,1)} %refs_2_.1, ...), custom_call_target="tpu_custom_call" | custom-call | flops 1000 | bytes 1000 | tf_op jit(solution)/shard_map/product/pallas_call | solution.py:188
  210.1 1.4 copy-done.6
  212.5 2.5 %finish.5.refs_7_ = bf16[768,2048]{1,0:T(8,128)(2,1)} custom-call(s32[1]{0:T(128)} %bitcast.9.row_ref, f32[192,2048]{1,0:T(8,128)S(1)} %copy-done.6, f32[192,256]{1,0:T(8,128)S(1)} %copy-done.10, bf16[256,10240]{1,0:T(8,128)(2,1)S(1)} %bitcast.15, s32[1,256]{1,0:T(1,128)S(1)} %copy-done.12, ...), custom_call_target="tpu_custom_call", output_to_operand_aliasing={{}: (8, {})} | custom-call | flops 1000 | bytes 1000 | tf_op jit(solution)/shard_map/finish/pallas_call | solution.py:244
  215.0 2.5 %finish.6.refs_7_ = bf16[768,2048]{1,0:T(8,128)(2,1)} custom-call(s32[1]{0:T(128)} %bitcast.8.row_ref, f32[384,2048]{1,0:T(8,128)S(1)} %copy-done.1, f32[384,256]{1,0:T(8,128)S(1)} %copy-done.7, bf16[256,10240]{1,0:T(8,128)(2,1)S(1)} %bitcast.15, s32[1,256]{1,0:T(1,128)S(1)} %copy-done.12, ...), custom_call_target="tpu_custom_call", output_to_operand_aliasing={{}: (8, {})} | custom-call | flops 1000 | bytes 1000 | tf_op jit(solution)/shard_map/finish/pallas_call | solution.py:244
  218.0 2.5 %finish.7 = bf16[768,2048]{1,0:T(8,128)(2,1)} custom-call(s32[1]{0:T(128)} %bitcast.row_ref, f32[384,2048]{1,0:T(8,128)S(1)} %copy-done.1, f32[384,256]{1,0:T(8,128)S(1)} %copy-done.7, bf16[256,10240]{1,0:T(8,128)(2,1)S(1)} %bitcast.15, s32[1,256]{1,0:T(1,128)S(1)} %copy-done.12, ...), custom_call_target="tpu_custom_call", output_to_operand_aliasing={{}: (8, {})} | custom-call | flops 1000 | bytes 1000 | tf_op jit(solution)/shard_map/finish/pallas_call | solution.py:244
  (94 shorter events, 16.2 us)
Async XLA Ops:
  6.5 64.2 %all-gather.3.cloned.1.call-start = ((), (), s32[]{:S(2)}) async-start(), calls=%async_computation | async-start | bytes 6553600 | tf_op jit(solution)/shard_map/all_gather | solution.py:286
  9.6 7.6 %copy-start.25 = (bf16[8192]{0:T(1024)(128)(2,1)S(1)}, bf16[8192]{0:T(1024)(128)(2,1)}, u32[]{:S(2)}) copy-start(bf16[8192]{0:T(1024)(128)(2,1)} %param.7) | copy-start | bytes 49156
  9.6 7.6 %copy-start.3 = (bf16[192,8192]{1,0:T(8,128)(2,1)S(1)}, bf16[192,8192]{1,0:T(8,128)(2,1)}, u32[]{:S(2)}) copy-start(bf16[192,8192]{1,0:T(8,128)(2,1)} %x_ref) | copy-start | bytes 9437188
  10.8 137.4 %all-gather.5.cloned.1.call-start = ((), (), s32[]{:S(2)}) async-start(), calls=%async_computation.1 | async-start | bytes 16515072 | tf_op jit(solution)/shard_map/all_gather | solution.py:326
  10.9 46.6 %collective-permute-start = (bf16[448,2048]{1,0:T(8,128)(2,1)}, bf16[448,2048]{1,0:T(8,128)(2,1)}, u32[]{:S(2)}, u32[]{:S(2)}) collective-permute-start(bf16[448,2048]{1,0:T(8,128)(2,1)} %constant_dynamic-slice_fusion), channel_id=1, source_target_pairs={{0,1},{3,2},{4,5},{7,6},{8,9},{11,10},{12,13},{15,14},{16,17},{19,... | collective-permute-start | bytes 5505032 | tf_op jit(solution)/shard_map/ppermute | solution.py:273
  22.1 18.9 %collective-permute-start.4 = (bf16[192,3584]{1,0:T(8,128)(2,1)S(1)}, bf16[192,3584]{1,0:T(8,128)(2,1)S(1)}, u32[]{:S(2)}, u32[]{:S(2)}) collective-permute-start(bf16[192,3584]{1,0:T(8,128)(2,1)S(1)} %get-tuple-element.45.refs_1_), channel_id=1, source_target_pairs={{1,2},{2,1},{5,6},{6,5},{9,10},{10,9},{13,14},{14,13},{17,18},{18,... | collective-permute-start | bytes 4128776 | tf_op jit(solution)/shard_map/ppermute | solution.py:275
  22.8 33.5 %collective-permute-start.2 = (bf16[192,3584]{1,0:T(8,128)(2,1)S(1)}, bf16[192,3584]{1,0:T(8,128)(2,1)S(1)}, u32[]{:S(2)}, u32[]{:S(2)}) collective-permute-start(bf16[192,3584]{1,0:T(8,128)(2,1)S(1)} %get-tuple-element.45.refs_1_), channel_id=1, source_target_pairs={{1,0},{2,3},{5,4},{6,7},{9,8},{10,11},{13,12},{14,15},{17,16},{18,... | collective-permute-start | bytes 4128776 | tf_op jit(solution)/shard_map/ppermute | solution.py:274
  40.9 16.5 %copy-start.5 = (bf16[192,1024]{1,0:T(8,128)(2,1)S(1)}, bf16[192,1024]{1,0:T(8,128)(2,1)}, u32[]{:S(2)}) copy-start(bf16[192,1024]{1,0:T(8,128)(2,1)} %copy-done.4) | copy-start | bytes 1179652
  40.9 28.3 %copy-start.26 = (s32[768]{0:T(1024)S(1)}, s32[768]{0:T(1024)}, u32[]{:S(2)}) copy-start(s32[768]{0:T(1024)} %param.11) | copy-start | bytes 9220
  40.9 29.9 %copy-start.9 = (bf16[192,3584]{1,0:T(8,128)(2,1)S(1)}, bf16[192,3584]{1,0:T(8,128)(2,1)}, u32[]{:S(2)}) copy-start(bf16[192,3584]{1,0:T(8,128)(2,1)} %copy-done.8) | copy-start | bytes 4128772
  40.9 15.4 %copy-start.15 = (bf16[192,3584]{1,0:T(8,128)(2,1)}, bf16[192,3584]{1,0:T(8,128)(2,1)S(1)}, u32[]{:S(2)}) copy-start(bf16[192,3584]{1,0:T(8,128)(2,1)S(1)} %collective-permute-done.4.refs_0_) | copy-start | bytes 4128772
  57.5 13.3 %collective-permute-start.5 = (bf16[192,1024]{1,0:T(8,128)(2,1)S(1)}, bf16[192,1024]{1,0:T(8,128)(2,1)}, u32[]{:S(2)}, u32[]{:S(2)}) collective-permute-start(bf16[192,1024]{1,0:T(8,128)(2,1)S(1)} %copy-done.5), channel_id=1, source_target_pairs={{1,2},{2,1},{5,6},{6,5},{9,10},{10,9},{13,14},{14,13},{17,18},{18,... | collective-permute-start | bytes 1179656 | tf_op jit(solution)/shard_map/ppermute | solution.py:275
  58.9 11.9 %collective-permute-start.3 = (bf16[192,1024]{1,0:T(8,128)(2,1)S(1)}, bf16[192,1024]{1,0:T(8,128)(2,1)S(1)}, u32[]{:S(2)}, u32[]{:S(2)}) collective-permute-start(bf16[192,1024]{1,0:T(8,128)(2,1)S(1)} %copy-done.5), channel_id=1, source_target_pairs={{1,0},{2,3},{5,4},{6,7},{9,8},{10,11},{13,12},{14,15},{17,16},{18,... | collective-permute-start | bytes 1179656 | tf_op jit(solution)/shard_map/ppermute | solution.py:274
  60.2 30.0 %collective-permute-start.8 = (bf16[192,3584]{1,0:T(8,128)(2,1)}, bf16[192,3584]{1,0:T(8,128)(2,1)}, u32[]{:S(2)}, u32[]{:S(2)}) collective-permute-start(bf16[192,3584]{1,0:T(8,128)(2,1)} %get-tuple-element.55.refs_0_), channel_id=1, source_target_pairs={{1,2},{2,1},{5,6},{6,5},{9,10},{10,9},{13,14},{14,13},{17,18},{18,... | collective-permute-start | bytes 4128776 | tf_op jit(solution)/shard_map/ppermute | solution.py:275
  61.9 23.8 %collective-permute-start.1 = (bf16[192,2304]{1,0:T(8,128)(2,1)}, bf16[192,2304]{1,0:T(8,128)(2,1)}, u32[]{:S(2)}, u32[]{:S(2)}) collective-permute-start(bf16[192,2304]{1,0:T(8,128)(2,1)} %copy-done.13), channel_id=1, source_target_pairs={{0,1},{3,2},{4,5},{7,6},{8,9},{11,10},{12,13},{15,14},{16,17},{19,... | collective-permute-start | bytes 2654216 | tf_op jit(solution)/shard_map/ppermute | solution.py:273
  69.4 35.8 %collective-permute-start.7 = (bf16[192,3584]{1,0:T(8,128)(2,1)}, bf16[192,3584]{1,0:T(8,128)(2,1)}, u32[]{:S(2)}, u32[]{:S(2)}) collective-permute-start(bf16[192,3584]{1,0:T(8,128)(2,1)} %copy-done.15), channel_id=1, source_target_pairs={{1,0},{2,3},{5,4},{6,7},{9,8},{10,11},{13,12},{14,15},{17,16},{18,... | collective-permute-start | bytes 4128776 | tf_op jit(solution)/shard_map/ppermute | solution.py:274
  85.7 20.9 %collective-permute-start.6 = (bf16[192,2304]{1,0:T(8,128)(2,1)}, bf16[192,2304]{1,0:T(8,128)(2,1)S(1)}, u32[]{:S(2)}, u32[]{:S(2)}) collective-permute-start(bf16[192,2304]{1,0:T(8,128)(2,1)} %get-tuple-element.51), channel_id=1, source_target_pairs={{0,1},{3,2},{4,5},{7,6},{8,9},{11,10},{12,13},{15,14},{16,17},{19,... | collective-permute-start | bytes 2654216 | tf_op jit(solution)/shard_map/ppermute | solution.py:273
  90.1 28.7 %collective-permute-start.10 = (bf16[192,2304]{1,0:T(8,128)(2,1)}, bf16[192,2304]{1,0:T(8,128)(2,1)S(1)}, u32[]{:S(2)}, u32[]{:S(2)}) collective-permute-start(bf16[192,2304]{1,0:T(8,128)(2,1)} %collective-permute-done.1.refs_0_), channel_id=1, source_target_pairs={{1,2},{2,1},{5,6},{6,5},{9,10},{10,9},{13,14},{14,13},{17,18},{18,... | collective-permute-start | bytes 2654216 | tf_op jit(solution)/shard_map/ppermute | solution.py:275
  90.9 28.0 %collective-permute-start.13 = (bf16[192,1024]{1,0:T(8,128)(2,1)}, bf16[192,1024]{1,0:T(8,128)(2,1)S(1)}, u32[]{:S(2)}, u32[]{:S(2)}) collective-permute-start(bf16[192,1024]{1,0:T(8,128)(2,1)} %collective-permute-done.5.refs_2_), channel_id=1, source_target_pairs={{1,0},{2,3},{5,4},{6,7},{9,8},{10,11},{13,12},{14,15},{17,16},{18,... | collective-permute-start | bytes 1179656 | tf_op jit(solution)/shard_map/ppermute | solution.py:274
  106.6 28.4 %copy-start.17 = (bf16[192,2304]{1,0:T(8,128)(2,1)}, bf16[192,2304]{1,0:T(8,128)(2,1)S(1)}, u32[]{:S(2)}) copy-start(bf16[192,2304]{1,0:T(8,128)(2,1)S(1)} %collective-permute-done.6.refs_2_) | copy-start | bytes 2654212
  106.6 38.9 %collective-permute-start.9 = (bf16[192,3584]{1,0:T(8,128)(2,1)}, bf16[192,3584]{1,0:T(8,128)(2,1)}, u32[]{:S(2)}, u32[]{:S(2)}) collective-permute-start(bf16[192,3584]{1,0:T(8,128)(2,1)} %get-tuple-element.55.refs_0_), channel_id=1, source_target_pairs={{0,1},{3,2},{4,5},{7,6},{8,9},{11,10},{12,13},{15,14},{16,17},{19,... | collective-permute-start | bytes 4128776 | tf_op jit(solution)/shard_map/ppermute | solution.py:273
  118.9 16.1 %copy-start.18 = (bf16[192,2304]{1,0:T(8,128)(2,1)}, bf16[192,2304]{1,0:T(8,128)(2,1)S(1)}, u32[]{:S(2)}) copy-start(bf16[192,2304]{1,0:T(8,128)(2,1)S(1)} %collective-permute-done.10.refs_4_) | copy-start | bytes 2654212
  118.9 20.9 %collective-permute-start.14 = (bf16[192,2304]{1,0:T(8,128)(2,1)S(1)}, bf16[192,2304]{1,0:T(8,128)(2,1)S(1)}, u32[]{:S(2)}, u32[]{:S(2)}) collective-permute-start(bf16[192,2304]{1,0:T(8,128)(2,1)S(1)} %collective-permute-done.10.refs_4_), channel_id=1, source_target_pairs={{1,0},{2,3},{5,4},{6,7},{9,8},{10,11},{13,12},{14,15},{17,16},{18,... | collective-permute-start | bytes 2654216 | tf_op jit(solution)/shard_map/ppermute | solution.py:274
  120.2 19.6 %collective-permute-start.11 = (bf16[192,2304]{1,0:T(8,128)(2,1)S(1)}, bf16[192,2304]{1,0:T(8,128)(2,1)S(1)}, u32[]{:S(2)}, u32[]{:S(2)}) collective-permute-start(bf16[192,2304]{1,0:T(8,128)(2,1)S(1)} %collective-permute-done.6.refs_2_), channel_id=1, source_target_pairs={{1,2},{2,1},{5,6},{6,5},{9,10},{10,9},{13,14},{14,13},{17,18},{18,... | collective-permute-start | bytes 2654216 | tf_op jit(solution)/shard_map/ppermute | solution.py:275
  140.8 21.5 %copy-start.20 = (bf16[192,2304]{1,0:T(8,128)(2,1)}, bf16[192,2304]{1,0:T(8,128)(2,1)S(1)}, u32[]{:S(2)}) copy-start(bf16[192,2304]{1,0:T(8,128)(2,1)S(1)} %collective-permute-done.11.refs_6_) | copy-start | bytes 2654212
  140.8 21.5 %collective-permute-start.15 = (bf16[192,2304]{1,0:T(8,128)(2,1)S(1)}, bf16[192,2304]{1,0:T(8,128)(2,1)S(1)}, u32[]{:S(2)}, u32[]{:S(2)}) collective-permute-start(bf16[192,2304]{1,0:T(8,128)(2,1)S(1)} %collective-permute-done.11.refs_6_), channel_id=1, source_target_pairs={{1,0},{2,3},{5,4},{6,7},{9,8},{10,11},{13,12},{14,15},{17,16},{18,... | collective-permute-start | bytes 2654216 | tf_op jit(solution)/shard_map/ppermute | solution.py:274
  145.5 36.4 %collective-permute-start.12 = (bf16[192,3584]{1,0:T(8,128)(2,1)}, bf16[192,3584]{1,0:T(8,128)(2,1)}, u32[]{:S(2)}, u32[]{:S(2)}) collective-permute-start(bf16[192,3584]{1,0:T(8,128)(2,1)} %collective-permute-done.9.refs_0_), channel_id=1, source_target_pairs={{1,2},{2,1},{5,6},{6,5},{9,10},{10,9},{13,14},{14,13},{17,18},{18,... | collective-permute-start | bytes 4128776 | tf_op jit(solution)/shard_map/ppermute | solution.py:275
  162.3 47.8 %collective-permute-start.17 = (bf16[384,2176]{1,0:T(8,128)(2,1)}, bf16[384,2176]{1,0:T(8,128)(2,1)S(1)}, u32[]{:S(2)}, u32[]{:S(2)}) collective-permute-start(bf16[384,2176]{1,0:T(8,128)(2,1)} %product_sent.2), channel_id=1, source_target_pairs={{1,0},{2,3},{5,4},{6,7},{9,8},{10,11},{13,12},{14,15},{17,16},{18,... | collective-permute-start | bytes 5013512 | tf_op jit(solution)/shard_map/ppermute | solution.py:274
  193.3 24.7 %collective-permute-start.16 = (bf16[192,2176]{1,0:T(8,128)(2,1)}, bf16[192,2176]{1,0:T(8,128)(2,1)S(1)}, u32[]{:S(2)}, u32[]{:S(2)}) collective-permute-start(bf16[192,2176]{1,0:T(8,128)(2,1)} %product_sent.3), channel_id=1, source_target_pairs={{1,0},{2,3},{5,4},{6,7},{9,8},{10,11},{13,12},{14,15},{17,16},{18,... | collective-permute-start | bytes 2506760 | tf_op jit(solution)/shard_map/ppermute | solution.py:274
  194.6 15.5 %slice-start = ((s8[5242880]{0:T(1024)(128)(4,1)}), s8[4194304]{0:T(1024)(128)(4,1)S(1)}, s32[]{:S(2)}) async-start(s8[5242880]{0:T(1024)(128)(4,1)} %bitcast.14), calls=%async_computation.2 | async-start | bytes 8388608
  194.7 15.5 %slice-start.1 = ((s8[5242880]{0:T(1024)(128)(4,1)}), s8[1048576]{0:T(1024)(128)(4,1)S(1)}, s32[]{:S(2)}) async-start(s8[5242880]{0:T(1024)(128)(4,1)} %bitcast.14), calls=%async_computation.3 | async-start | bytes 2097152
  194.7 15.5 %copy-start.12 = (s32[1,256]{1,0:T(1,128)S(1)}, s32[1,256]{1,0:T(1,128)}, u32[]{:S(2)}) copy-start(s32[1,256]{1,0:T(1,128)} %copy-done.11) | copy-start | bytes 3076
  (17 other events, 42.1 us)
Sparse Core Ops, SparseCore 0:
  10.9 43.1 all-gather.2
  57.6 81.1 all-gather.4

commit v7 on v6

--- a/solution.py
+++ b/solution.py
@@ -7,7 +7,7 @@
 
 adapter_scale = 2.0
 lanes = 128
-vmem = 56 * 1024 * 1024
+vmem = 52 * 1024 * 1024
 f32 = jnp.float32
 bf16 = jnp.bfloat16
 

time: 229 us -> 228 us (level)
  waiting for transfers between devices: 32.6 us -> 35.6 us
    ppermute x8, waiting for transfers between devices: 20.8 us -> 24.1 us  [body(): outward = lambda a: lax.ppermute(a, 'tensor', [(1, 0), (2, 3)])]
    unnamed x58 -> x42, local copies, waits for them, and re-layouts: 6.12 us -> 6.18 us
  transfers between devices with their start and end apart: 20 -> 20, of which waited for: 6 -> 7; matrix products, arithmetic and copies ran while one was open for 3% -> 3% of each run, Pallas kernels for 50% -> 49%
where the time goes in v7:
time: 228 us; the launch traced here: 227 us
  Pallas kernels  114 us (50%)
  starting transfers between devices  46.4 us (20%)
  waiting for transfers between devices  35.6 us (16%)
  between operations  13.9 us (6%)
  local copies, waits for them, and re-layouts  9.82 us (4%)
  matrix products  6.48 us (3%)
    pallas_call x7, Pallas kernels, product(): pl.pallas_call(kernel, grid=(tiles,), in_specs=in_specs, out_specs=out_sp...  101 us
    ppermute x4, starting transfers between devices, body(): inward = lambda a: lax.ppermute(a, 'tensor', [(0, 1), (3, 2)])  29.9 us
    ppermute x8, waiting for transfers between devices, body(): outward = lambda a: lax.ppermute(a, 'tensor', [(1, 0), (2, 3)])  24.1 us
    ppermute x4, waiting for transfers between devices, body(): inward = lambda a: lax.ppermute(a, 'tensor', [(0, 1), (3, 2)])  11.5 us
    ppermute x8, starting transfers between devices, body(): outward = lambda a: lax.ppermute(a, 'tensor', [(1, 0), (2, 3)])  10.3 us
    pallas_call x4, Pallas kernels, finish(): pl.pallas_call(kernel, grid_spec=pltpu.PrefetchScalarGridSpec(num_scalar_...  9.85 us
    dot_general x3, matrix products, dot_t(): lax.dot_general(a, b, (((1,), (1,)), ((), ())), preferred_element_type=f32)  6.48 us
    unnamed x42, local copies, waits for them, and re-layouts  6.18 us
  transfers between devices with their start and end apart: 20, of which 7 were waited for; matrix products, arithmetic and copies ran while one was open for 3% of the time, Pallas kernels for 49%

profile of v7, /device:TPU:0, one launch (start us, length us, event | category | flops | bytes accessed | tf_op | source)
XLA Modules:
  0.0 227.2 jit_solution(15858097718984102999)
XLA Ops:
  6.5 3.0 %constant_dynamic-slice_fusion = bf16[448,2048]{1,0:T(8,128)(2,1)} fusion(bf16[8192,2048]{1,0:T(8,128)(2,1)} %refs_2_.1, s32[]{:T(128)S(6)} %select_n.20), kind=kLoop, calls=%fused_computation.9 | loop fusion | bytes 3670020 | tf_op jit(solution)/shard_map/dynamic_slice | solution.py:281
  10.9 5.0 %collective-permute-start = (bf16[448,2048]{1,0:T(8,128)(2,1)}, bf16[448,2048]{1,0:T(8,128)(2,1)S(1)}, u32[]{:S(2)}, u32[]{:S(2)}) collective-permute-start(bf16[448,2048]{1,0:T(8,128)(2,1)} %constant_dynamic-slice_fusion), channel_id=1, source_target_pairs={{0,1},{3,2},{4,5},{7,6},{8,9},{11,10},{12,13},{15,14},{16,17},{19,... | collective-permute-start | bytes 5505032 | tf_op jit(solution)/shard_map/ppermute | solution.py:273
  16.0 1.9 copy-done.4
  17.8 3.1 %norm_chunks.1 = (bf16[192,3584]{1,0:T(8,128)(2,1)S(1)}, bf16[192,3584]{1,0:T(8,128)(2,1)}, bf16[192,1024]{1,0:T(8,128)(2,1)}, bf16[192,2304]{1,0:T(8,128)(2,1)S(1)}, bf16[192,2304]{1,0:T(8,128)(2,1)S(1)}) custom-call(bf16[192,8192]{1,0:T(8,128)(2,1)S(1)} %copy-done.4, bf16[1,8192]{1,0:T(2,128)(2,1)S(1)} %broadcast_in_dim.19.g_ref), custom_call_target="tpu_custom_call" | custom-call | flops 1000 | bytes 1000 | tf_op jit(solution)/shard_map/norm_chunks/pallas_call | solution.py:53
  23.6 1.3 collective-permute-start.2
  24.9 16.4 %product.5.refs_0_ = f32[192,2048]{1,0:T(8,128)} custom-call(bf16[192,3584]{1,0:T(8,128)(2,1)S(1)} %get-tuple-element.55.refs_0_, bf16[192,3584]{1,0:T(8,128)(2,1)} %get-tuple-element.45.refs_1_, bf16[192,1024]{1,0:T(8,128)(2,1)} %get-tuple-element.50.refs_2_, bf16[8192,2048]{1,0:T(8,128)(2,1)} %refs_2_.1), custom_call_target="tpu_custom_call" | custom-call | flops 1000 | bytes 1000 | tf_op jit(solution)/shard_map/product/pallas_call | solution.py:188
  42.5 15.0 %collective-permute-done.2.refs_1_ = bf16[192,3584]{1,0:T(8,128)(2,1)} collective-permute-done((bf16[192,3584]{1,0:T(8,128)(2,1)}, bf16[192,3584]{1,0:T(8,128)(2,1)}, u32[]{:S(2)}, u32[]{:S(2)}) %collective-permute-start.2) | collective-permute-done | bytes 1376288 | tf_op jit(solution)/shard_map/ppermute | solution.py:274
  58.7 1.4 collective-permute-start.5
  62.2 8.9 %collective-permute-start.1 = (bf16[192,2304]{1,0:T(8,128)(2,1)}, bf16[192,2304]{1,0:T(8,128)(2,1)}, u32[]{:S(2)}, u32[]{:S(2)}) collective-permute-start(bf16[192,2304]{1,0:T(8,128)(2,1)} %copy-done.8), channel_id=1, source_target_pairs={{0,1},{3,2},{4,5},{7,6},{8,9},{11,10},{12,13},{15,14},{16,17},{19,... | collective-permute-start | bytes 2654216 | tf_op jit(solution)/shard_map/ppermute | solution.py:273
  71.4 1.3 collective-permute-start.7
  72.8 2.8 %fusion = f32[192,256]{1,0:T(8,128)S(1)} fusion(bf16[192,3584]{1,0:T(8,128)(2,1)} %get-tuple-element.45.refs_1_, bf16[256,10240]{1,0:T(8,128)(2,1)} %all-gather.3.cloned.1.call-done.refs_2_.refs_3_.refs_5_.refs_9_), kind=kOutput, calls=%fused_computation | convolution fusion | flops 352321536 | bytes 3407872 | tf_op jit(solution)/shard_map/dot_general | solution.py:69
  75.6 2.4 %fusion.4 = f32[192,256]{1,0:T(8,128)S(1)} fusion(f32[192,256]{1,0:T(8,128)S(1)} %fusion, bf16[192,3584]{1,0:T(8,128)(2,1)S(1)} %get-tuple-element.55.refs_0_, bf16[256,10240]{1,0:T(8,128)(2,1)} %all-gather.3.cloned.1.call-done.refs_2_.refs_3_.refs_5_.refs_9_), kind=kOutput, calls=%fused_computation.6 | convolution fusion | flops 352370688 | bytes 3604480 | tf_op jit(solution)/shard_map/dot_general | solution.py:69
  77.9 1.3 convolution_add_fusion.refs_1_
  79.3 2.3 %finish.4.refs_7_ = bf16[768,2048]{1,0:T(8,128)(2,1)} custom-call(s32[1]{0:T(128)} %bitcast.1.row_ref, f32[192,2048]{1,0:T(8,128)S(1)} %copy-done.2, f32[192,256]{1,0:T(8,128)S(1)} %convolution_add_fusion.refs_1_, bf16[256,10240]{1,0:T(8,128)(2,1)S(1)} %copy-done, s32[1,256]{1,0:T(1,128)S(1)} %broadcast_in_dim_reshape.13.refs_3_.refs_4_, ...), custom_call_target="tpu_custom_call" | custom-call | flops 1000 | bytes 1000 | tf_op jit(solution)/shard_map/finish/pallas_call | solution.py:244
  81.6 6.1 %collective-permute-done.1.refs_0_ = bf16[192,2304]{1,0:T(8,128)(2,1)} collective-permute-done((bf16[192,2304]{1,0:T(8,128)(2,1)}, bf16[192,2304]{1,0:T(8,128)(2,1)}, u32[]{:S(2)}, u32[]{:S(2)}) %collective-permute-start.1) | collective-permute-done | bytes 884768 | tf_op jit(solution)/shard_map/ppermute | solution.py:273
  87.7 4.4 %collective-permute-start.6 = (bf16[192,2304]{1,0:T(8,128)(2,1)S(1)}, bf16[192,2304]{1,0:T(8,128)(2,1)S(1)}, u32[]{:S(2)}, u32[]{:S(2)}) collective-permute-start(bf16[192,2304]{1,0:T(8,128)(2,1)S(1)} %copy-done.7), channel_id=1, source_target_pairs={{0,1},{3,2},{4,5},{7,6},{8,9},{11,10},{12,13},{15,14},{16,17},{19,... | collective-permute-start | bytes 2654216 | tf_op jit(solution)/shard_map/ppermute | solution.py:273
  92.9 1.3 collective-permute-start.13
  94.2 12.6 %product.6 = (f32[192,2048]{1,0:T(8,128)}, f32[192,256]{1,0:T(8,128)S(1)}) custom-call(bf16[192,3584]{1,0:T(8,128)(2,1)S(1)} %collective-permute-done.8.refs_0_.refs_1_, bf16[8192,2048]{1,0:T(8,128)(2,1)} %refs_2_.1, bf16[256,10240]{1,0:T(8,128)(2,1)} %all-gather.3.cloned.1.call-done.refs_2_.refs_3_.refs_5_.refs_9_), custom_call_target="tpu_custom_call" | custom-call | flops 1000 | bytes 1000 | tf_op jit(solution)/shard_map/product/pallas_call | solution.py:188
  106.8 1.5 collective-permute-done.6.refs_2_
  108.3 11.5 %collective-permute-start.9 = (bf16[192,3584]{1,0:T(8,128)(2,1)S(1)}, bf16[192,3584]{1,0:T(8,128)(2,1)}, u32[]{:S(2)}, u32[]{:S(2)}) collective-permute-start(bf16[192,3584]{1,0:T(8,128)(2,1)S(1)} %get-tuple-element.55.refs_0_), channel_id=1, source_target_pairs={{0,1},{3,2},{4,5},{7,6},{8,9},{11,10},{12,13},{15,14},{16,17},{19,... | collective-permute-start | bytes 4128776 | tf_op jit(solution)/shard_map/ppermute | solution.py:273
  121.8 13.9 %product.7 = (f32[192,2048]{1,0:T(8,128)}, f32[192,256]{1,0:T(8,128)S(1)}) custom-call(bf16[192,3584]{1,0:T(8,128)(2,1)} %copy-done.10, bf16[192,3584]{1,0:T(8,128)(2,1)} %collective-permute-done.7.refs_1_, bf16[192,1024]{1,0:T(8,128)(2,1)} %collective-permute-done.5.refs_2_, bf16[192,1024]{1,0:T(8,128)(2,1)S(1)} %collective-permute-done.13.refs_3_, ...), custom_call_target="tpu_custom_call" | custom-call | flops 1000 | bytes 1000 | tf_op jit(solution)/shard_map/product/pallas_call | solution.py:188
  135.7 5.0 %collective-permute-done.14.refs_5_ = bf16[192,2304]{1,0:T(8,128)(2,1)S(1)} collective-permute-done((bf16[192,2304]{1,0:T(8,128)(2,1)S(1)}, bf16[192,2304]{1,0:T(8,128)(2,1)S(1)}, u32[]{:S(2)}, u32[]{:S(2)}) %collective-permute-start.14) | collective-permute-done | bytes 884768 | tf_op jit(solution)/shard_map/ppermute | solution.py:274
  141.9 3.9 %collective-permute-done.9.refs_0_ = bf16[192,3584]{1,0:T(8,128)(2,1)} collective-permute-done((bf16[192,3584]{1,0:T(8,128)(2,1)S(1)}, bf16[192,3584]{1,0:T(8,128)(2,1)}, u32[]{:S(2)}, u32[]{:S(2)}) %collective-permute-start.9) | collective-permute-done | bytes 1376288 | tf_op jit(solution)/shard_map/ppermute | solution.py:273
  145.9 1.8 collective-permute-start.12
  148.0 13.5 %product_sent.2 = bf16[384,2176]{1,0:T(8,128)(2,1)} custom-call(bf16[192,3584]{1,0:T(8,128)(2,1)S(1)} %get-tuple-element.55.refs_0_, bf16[192,3584]{1,0:T(8,128)(2,1)} %copy-done.3, bf16[3584,2048]{1,0:T(8,128)(2,1)} %all-gather.5.cloned.1.call-done.refs_2_.refs_1_, bf16[256,10240]{1,0:T(8,128)(2,1)} %all-gather.3.cloned.1.call-done.refs_2_.refs_3_.refs_5_.refs_9_, ...), custom_call_target="tpu_custom_call" | custom-call | flops 1000 | bytes 1000 | tf_op jit(solution)/shard_map/product_sent/pallas_call | solution.py:188
  163.3 17.4 %product.8 = (f32[384,2048]{1,0:T(8,128)}, f32[384,256]{1,0:T(8,128)S(1)}) custom-call(bf16[192,2304]{1,0:T(8,128)(2,1)} %collective-permute-done.1.refs_0_, bf16[192,3584]{1,0:T(8,128)(2,1)} %collective-permute-done.2.refs_1_, bf16[192,2304]{1,0:T(8,128)(2,1)} %copy-done.12, bf16[192,1024]{1,0:T(8,128)(2,1)} %collective-permute-done.3.refs_3_, ...), custom_call_target="tpu_custom_call" | custom-call | flops 1000 | bytes 1000 | tf_op jit(solution)/shard_map/product/pallas_call | solution.py:188
  180.6 11.4 %product_sent.3 = bf16[192,2176]{1,0:T(8,128)(2,1)} custom-call(bf16[192,3584]{1,0:T(8,128)(2,1)} %collective-permute-done.12.refs_0_.refs_1_, bf16[3584,2048]{1,0:T(8,128)(2,1)} %all-gather.5.cloned.1.call-done.refs_2_.refs_1_, bf16[256,10240]{1,0:T(8,128)(2,1)} %all-gather.3.cloned.1.call-done.refs_2_.refs_3_.refs_5_.refs_9_, ...), custom_call_target="tpu_custom_call" | custom-call | flops 1000 | bytes 1000 | tf_op jit(solution)/shard_map/product_sent/pallas_call | solution.py:188
  193.4 15.6 %product.9 = (f32[384,2048]{1,0:T(8,128)}, f32[384,256]{1,0:T(8,128)S(1)}) custom-call(bf16[192,3584]{1,0:T(8,128)(2,1)} %collective-permute-done.9.refs_0_, bf16[192,3584]{1,0:T(8,128)(2,1)} %collective-permute-done.12.refs_0_.refs_1_, bf16[8192,2048]{1,0:T(8,128)(2,1)} %refs_2_.1, ...), custom_call_target="tpu_custom_call" | custom-call | flops 1000 | bytes 1000 | tf_op jit(solution)/shard_map/product/pallas_call | solution.py:188
  209.0 2.5 %finish.5.refs_7_ = bf16[768,2048]{1,0:T(8,128)(2,1)} custom-call(s32[1]{0:T(128)} %bitcast.9.row_ref, f32[192,2048]{1,0:T(8,128)S(1)} %copy-done.5, f32[192,256]{1,0:T(8,128)S(1)} %get-tuple-element.74.refs_1_, bf16[256,10240]{1,0:T(8,128)(2,1)S(1)} %bitcast.15, ...), custom_call_target="tpu_custom_call", output_to_operand_aliasing={{}: (8, {})} | custom-call | flops 1000 | bytes 1000 | tf_op jit(solution)/shard_map/finish/pallas_call | solution.py:244
  211.6 2.5 %finish.6.refs_7_ = bf16[768,2048]{1,0:T(8,128)(2,1)} custom-call(s32[1]{0:T(128)} %bitcast.8.row_ref, f32[384,2048]{1,0:T(8,128)S(1)} %copy-done.1, f32[384,256]{1,0:T(8,128)S(1)} %get-tuple-element.72.refs_1_, bf16[256,10240]{1,0:T(8,128)(2,1)S(1)} %bitcast.15, ...), custom_call_target="tpu_custom_call", output_to_operand_aliasing={{}: (8, {})} | custom-call | flops 1000 | bytes 1000 | tf_op jit(solution)/shard_map/finish/pallas_call | solution.py:244
  214.1 3.8 %collective-permute-done.16.refs_5_.refs_6_ = bf16[192,2176]{1,0:T(8,128)(2,1)S(1)} collective-permute-done((bf16[192,2176]{1,0:T(8,128)(2,1)}, bf16[192,2176]{1,0:T(8,128)(2,1)S(1)}, u32[]{:S(2)}, u32[]{:S(2)}) %collective-permute-start.16) | collective-permute-done | bytes 835616 | tf_op jit(solution)/shard_map/ppermute | solution.py:274
  217.8 2.5 %finish.7 = bf16[768,2048]{1,0:T(8,128)(2,1)} custom-call(s32[1]{0:T(128)} %bitcast.row_ref, f32[384,2048]{1,0:T(8,128)S(1)} %copy-done.1, f32[384,256]{1,0:T(8,128)S(1)} %get-tuple-element.72.refs_1_, bf16[256,10240]{1,0:T(8,128)(2,1)S(1)} %bitcast.15, s32[1,256]{1,0:T(1,128)S(1)} %broadcast_in_dim_reshape.13.refs_3_.refs_4_, ...), custom_call_target="tpu_custom_call", output_to_operand_aliasing={{}: (8, {})} | custom-call | flops 1000 | bytes 1000 | tf_op jit(solution)/shard_map/finish/pallas_call | solution.py:244
  (78 shorter events, 16.0 us)
Async XLA Ops:
  6.5 66.2 %all-gather.3.cloned.1.call-start = ((), (), s32[]{:S(2)}) async-start(), calls=%async_computation | async-start | bytes 6553600 | tf_op jit(solution)/shard_map/all_gather | solution.py:286
  9.6 6.3 %copy-start.17 = (bf16[8192]{0:T(1024)(128)(2,1)S(1)}, bf16[8192]{0:T(1024)(128)(2,1)}, u32[]{:S(2)}) copy-start(bf16[8192]{0:T(1024)(128)(2,1)} %param.7) | copy-start | bytes 49156
  10.8 137.1 %all-gather.5.cloned.1.call-start = ((), (), s32[]{:S(2)}) async-start(), calls=%async_computation.1 | async-start | bytes 16515072 | tf_op jit(solution)/shard_map/all_gather | solution.py:326
  10.9 46.6 %collective-permute-start = (bf16[448,2048]{1,0:T(8,128)(2,1)}, bf16[448,2048]{1,0:T(8,128)(2,1)S(1)}, u32[]{:S(2)}, u32[]{:S(2)}) collective-permute-start(bf16[448,2048]{1,0:T(8,128)(2,1)} %constant_dynamic-slice_fusion), channel_id=1, source_target_pairs={{0,1},{3,2},{4,5},{7,6},{8,9},{11,10},{12,13},{15,14},{16,17},{19,... | collective-permute-start | bytes 5505032 | tf_op jit(solution)/shard_map/ppermute | solution.py:273
  22.9 18.5 %collective-permute-start.4 = (bf16[192,3584]{1,0:T(8,128)(2,1)}, bf16[192,3584]{1,0:T(8,128)(2,1)S(1)}, u32[]{:S(2)}, u32[]{:S(2)}) collective-permute-start(bf16[192,3584]{1,0:T(8,128)(2,1)} %get-tuple-element.45.refs_1_), channel_id=1, source_target_pairs={{1,2},{2,1},{5,6},{6,5},{9,10},{10,9},{13,14},{14,13},{17,18},{18,... | collective-permute-start | bytes 4128776 | tf_op jit(solution)/shard_map/ppermute | solution.py:275
  23.6 33.9 %collective-permute-start.2 = (bf16[192,3584]{1,0:T(8,128)(2,1)}, bf16[192,3584]{1,0:T(8,128)(2,1)}, u32[]{:S(2)}, u32[]{:S(2)}) collective-permute-start(bf16[192,3584]{1,0:T(8,128)(2,1)} %get-tuple-element.45.refs_1_), channel_id=1, source_target_pairs={{1,0},{2,3},{5,4},{6,7},{9,8},{10,11},{13,12},{14,15},{17,16},{18,... | collective-permute-start | bytes 4128776 | tf_op jit(solution)/shard_map/ppermute | solution.py:274
  41.4 29.9 %copy-start.18 = (s32[768]{0:T(1024)S(1)}, s32[768]{0:T(1024)}, u32[]{:S(2)}) copy-start(s32[768]{0:T(1024)} %param.11) | copy-start | bytes 9220
  58.7 14.0 %collective-permute-start.5 = (bf16[192,1024]{1,0:T(8,128)(2,1)}, bf16[192,1024]{1,0:T(8,128)(2,1)}, u32[]{:S(2)}, u32[]{:S(2)}) collective-permute-start(bf16[192,1024]{1,0:T(8,128)(2,1)} %get-tuple-element.50.refs_2_), channel_id=1, source_target_pairs={{1,2},{2,1},{5,6},{6,5},{9,10},{10,9},{13,14},{14,13},{17,18},{18,... | collective-permute-start | bytes 1179656 | tf_op jit(solution)/shard_map/ppermute | solution.py:275
  60.2 12.6 %collective-permute-start.3 = (bf16[192,1024]{1,0:T(8,128)(2,1)}, bf16[192,1024]{1,0:T(8,128)(2,1)}, u32[]{:S(2)}, u32[]{:S(2)}) collective-permute-start(bf16[192,1024]{1,0:T(8,128)(2,1)} %get-tuple-element.50.refs_2_), channel_id=1, source_target_pairs={{1,0},{2,3},{5,4},{6,7},{9,8},{10,11},{13,12},{14,15},{17,16},{18,... | collective-permute-start | bytes 1179656 | tf_op jit(solution)/shard_map/ppermute | solution.py:274
  61.5 30.7 %collective-permute-start.8 = (bf16[192,3584]{1,0:T(8,128)(2,1)S(1)}, bf16[192,3584]{1,0:T(8,128)(2,1)S(1)}, u32[]{:S(2)}, u32[]{:S(2)}) collective-permute-start(bf16[192,3584]{1,0:T(8,128)(2,1)S(1)} %get-tuple-element.55.refs_0_), channel_id=1, source_target_pairs={{1,2},{2,1},{5,6},{6,5},{9,10},{10,9},{13,14},{14,13},{17,18},{18,... | collective-permute-start | bytes 4128776 | tf_op jit(solution)/shard_map/ppermute | solution.py:275
  62.2 25.5 %collective-permute-start.1 = (bf16[192,2304]{1,0:T(8,128)(2,1)}, bf16[192,2304]{1,0:T(8,128)(2,1)}, u32[]{:S(2)}, u32[]{:S(2)}) collective-permute-start(bf16[192,2304]{1,0:T(8,128)(2,1)} %copy-done.8), channel_id=1, source_target_pairs={{0,1},{3,2},{4,5},{7,6},{8,9},{11,10},{12,13},{15,14},{16,17},{19,... | collective-permute-start | bytes 2654216 | tf_op jit(solution)/shard_map/ppermute | solution.py:273
  71.4 35.4 %collective-permute-start.7 = (bf16[192,3584]{1,0:T(8,128)(2,1)}, bf16[192,3584]{1,0:T(8,128)(2,1)}, u32[]{:S(2)}, u32[]{:S(2)}) collective-permute-start(bf16[192,3584]{1,0:T(8,128)(2,1)} %copy-done.10), channel_id=1, source_target_pairs={{1,0},{2,3},{5,4},{6,7},{9,8},{10,11},{13,12},{14,15},{17,16},{18,... | collective-permute-start | bytes 4128776 | tf_op jit(solution)/shard_map/ppermute | solution.py:274
  72.8 5.2 %copy-start = (bf16[256,10240]{1,0:T(8,128)(2,1)S(1)}, bf16[256,10240]{1,0:T(8,128)(2,1)}, u32[]{:S(2)}) copy-start(bf16[256,10240]{1,0:T(8,128)(2,1)} %all-gather.3.cloned.1.call-done.refs_2_.refs_3_.refs_5_.refs_9_) | copy-start | bytes 15728644
  79.3 8.4 %copy-start.7 = (bf16[192,2304]{1,0:T(8,128)(2,1)S(1)}, bf16[192,2304]{1,0:T(8,128)(2,1)}, u32[]{:S(2)}) copy-start(bf16[192,2304]{1,0:T(8,128)(2,1)} %copy-done.6) | copy-start | bytes 2654212
  87.7 20.6 %collective-permute-start.6 = (bf16[192,2304]{1,0:T(8,128)(2,1)S(1)}, bf16[192,2304]{1,0:T(8,128)(2,1)S(1)}, u32[]{:S(2)}, u32[]{:S(2)}) collective-permute-start(bf16[192,2304]{1,0:T(8,128)(2,1)S(1)} %copy-done.7), channel_id=1, source_target_pairs={{0,1},{3,2},{4,5},{7,6},{8,9},{11,10},{12,13},{15,14},{16,17},{19,... | collective-permute-start | bytes 2654216 | tf_op jit(solution)/shard_map/ppermute | solution.py:273
  92.1 14.7 %copy-start.3 = (bf16[192,3584]{1,0:T(8,128)(2,1)}, bf16[192,3584]{1,0:T(8,128)(2,1)S(1)}, u32[]{:S(2)}) copy-start(bf16[192,3584]{1,0:T(8,128)(2,1)S(1)} %collective-permute-done.8.refs_0_.refs_1_) | copy-start | bytes 4128772
  92.1 27.6 %collective-permute-start.10 = (bf16[192,2304]{1,0:T(8,128)(2,1)}, bf16[192,2304]{1,0:T(8,128)(2,1)S(1)}, u32[]{:S(2)}, u32[]{:S(2)}) collective-permute-start(bf16[192,2304]{1,0:T(8,128)(2,1)} %collective-permute-done.1.refs_0_), channel_id=1, source_target_pairs={{1,2},{2,1},{5,6},{6,5},{9,10},{10,9},{13,14},{14,13},{17,18},{18,... | collective-permute-start | bytes 2654216 | tf_op jit(solution)/shard_map/ppermute | solution.py:275
  92.9 26.9 %collective-permute-start.13 = (bf16[192,1024]{1,0:T(8,128)(2,1)}, bf16[192,1024]{1,0:T(8,128)(2,1)S(1)}, u32[]{:S(2)}, u32[]{:S(2)}) collective-permute-start(bf16[192,1024]{1,0:T(8,128)(2,1)} %collective-permute-done.5.refs_2_), channel_id=1, source_target_pairs={{1,0},{2,3},{5,4},{6,7},{9,8},{10,11},{13,12},{14,15},{17,16},{18,... | collective-permute-start | bytes 1179656 | tf_op jit(solution)/shard_map/ppermute | solution.py:274
  108.3 27.4 %copy-start.12 = (bf16[192,2304]{1,0:T(8,128)(2,1)}, bf16[192,2304]{1,0:T(8,128)(2,1)S(1)}, u32[]{:S(2)}) copy-start(bf16[192,2304]{1,0:T(8,128)(2,1)S(1)} %collective-permute-done.6.refs_2_) | copy-start | bytes 2654212
  108.3 37.6 %collective-permute-start.9 = (bf16[192,3584]{1,0:T(8,128)(2,1)S(1)}, bf16[192,3584]{1,0:T(8,128)(2,1)}, u32[]{:S(2)}, u32[]{:S(2)}) collective-permute-start(bf16[192,3584]{1,0:T(8,128)(2,1)S(1)} %get-tuple-element.55.refs_0_), channel_id=1, source_target_pairs={{0,1},{3,2},{4,5},{7,6},{8,9},{11,10},{12,13},{15,14},{16,17},{19,... | collective-permute-start | bytes 4128776 | tf_op jit(solution)/shard_map/ppermute | solution.py:273
  119.8 15.9 %copy-start.13 = (bf16[192,2304]{1,0:T(8,128)(2,1)}, bf16[192,2304]{1,0:T(8,128)(2,1)S(1)}, u32[]{:S(2)}) copy-start(bf16[192,2304]{1,0:T(8,128)(2,1)S(1)} %collective-permute-done.10.refs_4_) | copy-start | bytes 2654212
  119.8 20.9 %collective-permute-start.14 = (bf16[192,2304]{1,0:T(8,128)(2,1)S(1)}, bf16[192,2304]{1,0:T(8,128)(2,1)S(1)}, u32[]{:S(2)}, u32[]{:S(2)}) collective-permute-start(bf16[192,2304]{1,0:T(8,128)(2,1)S(1)} %collective-permute-done.10.refs_4_), channel_id=1, source_target_pairs={{1,0},{2,3},{5,4},{6,7},{9,8},{10,11},{13,12},{14,15},{17,16},{18,... | collective-permute-start | bytes 2654216 | tf_op jit(solution)/shard_map/ppermute | solution.py:274
  121.1 19.6 %collective-permute-start.11 = (bf16[192,2304]{1,0:T(8,128)(2,1)S(1)}, bf16[192,2304]{1,0:T(8,128)(2,1)S(1)}, u32[]{:S(2)}, u32[]{:S(2)}) collective-permute-start(bf16[192,2304]{1,0:T(8,128)(2,1)S(1)} %collective-permute-done.6.refs_2_), channel_id=1, source_target_pairs={{1,2},{2,1},{5,6},{6,5},{9,10},{10,9},{13,14},{14,13},{17,18},{18,... | collective-permute-start | bytes 2654216 | tf_op jit(solution)/shard_map/ppermute | solution.py:275
  140.6 5.2 %copy-start.14 = (bf16[192,2304]{1,0:T(8,128)(2,1)}, bf16[192,2304]{1,0:T(8,128)(2,1)S(1)}, u32[]{:S(2)}) copy-start(bf16[192,2304]{1,0:T(8,128)(2,1)S(1)} %collective-permute-done.14.refs_5_) | copy-start | bytes 2654212
  140.6 20.9 %copy-start.15 = (bf16[192,2304]{1,0:T(8,128)(2,1)}, bf16[192,2304]{1,0:T(8,128)(2,1)S(1)}, u32[]{:S(2)}) copy-start(bf16[192,2304]{1,0:T(8,128)(2,1)S(1)} %collective-permute-done.11.refs_6_) | copy-start | bytes 2654212
  140.6 21.2 %collective-permute-start.15 = (bf16[192,2304]{1,0:T(8,128)(2,1)S(1)}, bf16[192,2304]{1,0:T(8,128)(2,1)}, u32[]{:S(2)}, u32[]{:S(2)}) collective-permute-start(bf16[192,2304]{1,0:T(8,128)(2,1)S(1)} %collective-permute-done.11.refs_6_), channel_id=1, source_target_pairs={{1,0},{2,3},{5,4},{6,7},{9,8},{10,11},{13,12},{14,15},{17,16},{18,... | collective-permute-start | bytes 2654216 | tf_op jit(solution)/shard_map/ppermute | solution.py:274
  145.9 34.8 %collective-permute-start.12 = (bf16[192,3584]{1,0:T(8,128)(2,1)}, bf16[192,3584]{1,0:T(8,128)(2,1)}, u32[]{:S(2)}, u32[]{:S(2)}) collective-permute-start(bf16[192,3584]{1,0:T(8,128)(2,1)} %collective-permute-done.9.refs_0_), channel_id=1, source_target_pairs={{1,2},{2,1},{5,6},{6,5},{9,10},{10,9},{13,14},{14,13},{17,18},{18,... | collective-permute-start | bytes 4128776 | tf_op jit(solution)/shard_map/ppermute | solution.py:275
  161.9 47.1 %collective-permute-start.17 = (bf16[384,2176]{1,0:T(8,128)(2,1)}, bf16[384,2176]{1,0:T(8,128)(2,1)S(1)}, u32[]{:S(2)}, u32[]{:S(2)}) collective-permute-start(bf16[384,2176]{1,0:T(8,128)(2,1)} %product_sent.2), channel_id=1, source_target_pairs={{1,0},{2,3},{5,4},{6,7},{9,8},{10,11},{13,12},{14,15},{17,16},{18,... | collective-permute-start | bytes 5013512 | tf_op jit(solution)/shard_map/ppermute | solution.py:274
  192.0 25.8 %collective-permute-start.16 = (bf16[192,2176]{1,0:T(8,128)(2,1)}, bf16[192,2176]{1,0:T(8,128)(2,1)S(1)}, u32[]{:S(2)}, u32[]{:S(2)}) collective-permute-start(bf16[192,2176]{1,0:T(8,128)(2,1)} %product_sent.3), channel_id=1, source_target_pairs={{1,0},{2,3},{5,4},{6,7},{9,8},{10,11},{13,12},{14,15},{17,16},{18,... | collective-permute-start | bytes 2506760 | tf_op jit(solution)/shard_map/ppermute | solution.py:274
  193.3 15.7 %slice-start = ((s8[5242880]{0:T(1024)(128)(4,1)}), s8[4194304]{0:T(1024)(128)(4,1)S(1)}, s32[]{:S(2)}) async-start(s8[5242880]{0:T(1024)(128)(4,1)} %bitcast.14), calls=%async_computation.2 | async-start | bytes 8388608
  193.3 15.7 %slice-start.1 = ((s8[5242880]{0:T(1024)(128)(4,1)}), s8[1048576]{0:T(1024)(128)(4,1)S(1)}, s32[]{:S(2)}) async-start(s8[5242880]{0:T(1024)(128)(4,1)} %bitcast.14), calls=%async_computation.3 | async-start | bytes 2097152
  193.4 15.7 %copy-start.5 = (f32[192,2048]{1,0:T(8,128)S(1)}, f32[192,2048]{1,0:T(8,128)}, u32[]{:S(2)}) copy-start(f32[192,2048]{1,0:T(8,128)} %get-tuple-element.65.refs_0_) | copy-start | bytes 4718596
  (9 other events, 18.5 us)
Sparse Core Ops, SparseCore 0:
  10.9 43.1 all-gather.2
  58.9 81.1 all-gather.4
